TPU v7x, 512 devices: a whole 4x8x8 slice. The times are simulated.
512 devices in a mesh: wide: 64 (over x, z_hi, y), narrow: 8 (over z_lo, core).
Axes of the slice: x: 4, y: 8, z: 8 (z_hi: 2, z_lo: 4; z = z_hi * 4 + z_lo), core: 2. Of those that a mesh axis runs over, the one named last changes fastest.
Arguments:
- pooled: bfloat16 [9216, 8, 64, 128], P(None, 'narrow', 'wide'), may hold values from -6 to 6
- w_top: bfloat16 [8, 4096, 512], P('narrow', 'wide'), may hold values from -0.03125 to 0.03125
- bias: float32 [512], replicated, may hold values from -4 to 4
- grad_hidden: bfloat16 [9216, 512], P('wide', 'narrow'), may hold values from -6 to 6
Outputs:
- hidden: bfloat16 [9216, 512], P('wide', 'narrow')
- grad_pooled: bfloat16 [9216, 8, 64, 128], P('wide', 'narrow')
All inputs are finite; a program needn't handle non-finite values.
Results may differ from a plain program's by a relative error of at most 0.009.
Values may be sent and summed in bfloat16 or wider, within the bound.
No kernel may reach another device: no remote copies, remote signals or barrier semaphores. Data moves between devices by JAX's collectives and lax.ppermute only.
A program may use at most 64 MiB of HBM per device.

v0:
```python
import jax
import jax.numpy as jnp
from jax import lax
from jax.sharding import PartitionSpec as P


def from_partner(x, axis, bit):
    return lax.ppermute(x, axis, [(i, i ^ 1 << bit) for i in range(lax.axis_size(axis))])


def gate_slope(pre_act):
    sigmoid_v = jax.nn.sigmoid(pre_act)
    return sigmoid_v * (1.0 + pre_act * (1.0 - sigmoid_v))


def body(pooled, w_top, bias, grad_hidden):
    by_sample = lax.all_to_all(pooled, "wide", split_axis=0, concat_axis=2, tiled=True)
    mine_block = by_sample[:, 0]
    sample_count = mine_block.shape[0]
    field_count = mine_block.shape[1]
    gram_scale = mine_block.shape[2] ** (-0.5)
    swap_bit = lax.axis_size("narrow").bit_length() - 2
    other_block = from_partner(mine_block, "narrow", swap_bit)
    gram_rows = jnp.einsum(
        "sie,sje->sij", mine_block, other_block, preferred_element_type=jnp.float32
    )
    gram_rows = (
        (gram_rows * gram_scale)
        .astype(jnp.bfloat16)
        .reshape(sample_count, field_count * field_count)
    )
    weight_shard = w_top[0]
    top_weights = lax.all_gather(weight_shard, "wide", axis=0, tiled=True)
    partial_value = jnp.dot(gram_rows, top_weights, preferred_element_type=jnp.float32)
    share_width = grad_hidden.shape[1]
    share_start = lax.axis_index("narrow") * share_width
    pre_act = lax.psum(partial_value, "narrow") + bias[None, :]
    hidden = lax.dynamic_slice_in_dim(jax.nn.silu(pre_act), share_start, share_width, 1).astype(
        jnp.bfloat16
    )
    cot_whole = lax.all_gather(grad_hidden, "narrow", axis=1, tiled=True)
    grad_pre = (cot_whole.astype(jnp.float32) * gate_slope(pre_act)).astype(jnp.bfloat16)
    contract_units = (((1,), (1,)), ((), ()))
    grad_flat = lax.dot_general(
        grad_pre, top_weights, contract_units, preferred_element_type=jnp.float32
    )
    grad_gram = grad_flat.astype(jnp.bfloat16).reshape(sample_count, field_count, field_count)
    direct_part = jnp.einsum(
        "sij,sje->sie", grad_gram, other_block, preferred_element_type=jnp.float32
    )
    returned = from_partner(grad_gram, "narrow", swap_bit)
    mirror_part = jnp.einsum(
        "sji,sje->sie", returned, other_block, preferred_element_type=jnp.float32
    )
    grad_pooled = ((direct_part + mirror_part) * gram_scale).astype(jnp.bfloat16)[:, None]
    return (hidden, grad_pooled)


def solution(mesh):
    in_specs = (
        P(None, "narrow", "wide", None),
        P("narrow", "wide", None),
        P(),
        P("wide", "narrow"),
    )
    out_specs = (P("wide", "narrow"), P("wide", "narrow", None, None))
    return jax.shard_map(body, mesh=mesh, in_specs=in_specs, out_specs=out_specs, check_vma=False)
```

profile of v0, /device:TPU:1, one launch (start us, length us, event | category | flops | bytes accessed | tf_op | source)
XLA Modules:
  0.0 452.9 jit_solution(6612648824377021818)
XLA Ops:
  7.2 0.0 all-gather.3.cloned.1.call-start
  7.2 0.7 all-gather.3.cloned.1.call-update
  7.9 0.0 all-reduce.2.cloned.1.call-start
  7.9 0.5 broadcast.4
  8.5 3.1 reduce
  11.5 2.1 reshape.15
  13.7 81.8 %all_to_all.15 = bf16[64,2,9216]{2,1,0:T(2,128)(2,1)S(1)} all-to-all(bf16[64,2,9216]{2,1,0:T(2,128)(2,1)} %reshape.15), channel_id=1, replica_groups=mesh['wide'=64,'narrow'=8] {'wide'}, dimensions={0} | all-to-all | bytes 4718592 | tf_op jit(solution)/shard_map/all_to_all | solution.py:17
  95.4 6.8 %reshape.16 = bf16[9216,1,1,128]{3,2,1,0:T(2,128)(2,1)} reshape(bf16[64,2,9216]{2,1,0:T(2,128)(2,1)S(1)} %all_to_all.15) | data formatting | bytes 4718592
  102.2 3.0 copy.22
  105.2 0.6 copy.25
  105.8 4.4 collective-permute-start
  110.3 133.7 %collective-permute-done = bf16[144,64,128]{2,1,0:T(8,128)(2,1)S(1)} collective-permute-done((bf16[144,64,128]{2,1,0:T(8,128)(2,1)S(1)}, bf16[144,64,128]{2,1,0:T(8,128)(2,1)S(1)}, u32[]{:S(2)}, u32[]{:S(2)}) %collective-permute-start) | collective-permute-done | bytes 2359328 | tf_op jit(solution)/shard_map/ppermute | solution.py:8
  244.0 2.8 multiply_convert_fusion.1
  246.8 3.6 reshape.12
  250.4 0.0 copy-start.2
  250.4 0.0 all-gather.3.cloned.1.call-done
  250.4 3.7 fusion.1
  254.1 0.0 all-reduce.2.cloned.1.call-update
  254.1 15.3 %all_gather.7 = bf16[144,512]{0,1:T(8,128)(2,1)S(1)} all-gather(bf16[144,64]{0,1:T(8,128)(2,1)} %param.7), channel_id=1, replica_groups=mesh['wide'=64,'narrow'=8] {'narrow'}, dimensions={1}, use_global_device_ids=true | all-gather | bytes 165888 | tf_op jit(solution)/shard_map/all_gather | solution.py:41
  269.4 0.8 copy.17
  270.2 56.1 %all-reduce.2.cloned.1.call-done = f32[144,512]{1,0:T(8,128)} async-done(((f32[144,512]{1,0:T(8,128)}), f32[144,512]{1,0:T(8,128)}) %all-reduce.2.cloned.1.call-update) | async-done | bytes 294928 | tf_op jit(solution)/shard_map/psum | solution.py:37
  326.3 0.0 copy-done.2
  326.3 1.8 add_divide_fusion
  328.1 0.0 copy-start.1
  328.1 0.7 copy-done.1
  328.8 3.8 convolution_convert_fusion
  332.6 3.5 reshape.13
  336.1 4.7 %copy.18 = bf16[144,64,64]{0,2,1:T(8,128)(2,1)} copy(bf16[144,64,64]{2,1,0:T(8,128)(2,1)} %reshape.13) | data formatting | bytes 2359296 | tf_op jit(solution)/shard_map/reshape | solution.py:47
  340.8 3.0 collective-permute-start.1
  343.9 1.0 fusion.5
  344.9 0.7 copy.20
  345.6 89.6 %collective-permute-done.1 = bf16[144,64,64]{0,2,1:T(8,128)(2,1)} collective-permute-done((bf16[144,64,64]{0,2,1:T(8,128)(2,1)}, bf16[144,64,64]{0,2,1:T(8,128)(2,1)}, u32[]{:S(2)}, u32[]{:S(2)}) %collective-permute-start.1) | collective-permute-done | bytes 1179680 | tf_op jit(solution)/shard_map/ppermute | solution.py:8
  435.2 6.0 %copy.19 = bf16[144,64,64]{1,2,0:T(8,128)(2,1)} copy(bf16[144,64,64]{0,2,1:T(8,128)(2,1)} %collective-permute-done.1) | data formatting | bytes 2359296 | tf_op jit(solution)/shard_map/ppermute | solution.py:8
  441.2 0.0 copy-start
  441.2 2.6 fusion.7
  443.7 0.0 copy-done
  443.8 2.3 fusion.3
Async XLA Ops:
  7.2 243.2 %all-gather.3.cloned.1.call-start = ((), (), s32[]{:S(2)}) async-start(), calls=%async_computation.2 | async-start | bytes 4259840 | tf_op jit(solution)/shard_map/all_gather | solution.py:33
  7.9 318.4 %all-reduce.2.cloned.1.call-start = ((), (), s32[]{:S(2)}) async-start(), calls=%async_computation.1 | async-start | bytes 589824 | tf_op jit(solution)/shard_map/psum | solution.py:37
  105.8 138.2 %collective-permute-start = (bf16[144,64,128]{2,1,0:T(8,128)(2,1)S(1)}, bf16[144,64,128]{2,1,0:T(8,128)(2,1)S(1)}, u32[]{:S(2)}, u32[]{:S(2)}) collective-permute-start(bf16[144,64,128]{2,1,0:T(8,128)(2,1)S(1)} %bitcast.24), channel_id=1, source_target_pairs={{0,4},{1,5},{2,6},{3,7},{4,0},{5,1},{6,2},{7,3},{8,12},{9,13},{10,... | collective-permute-start | bytes 7077896 | tf_op jit(solution)/shard_map/ppermute | solution.py:8
  250.4 76.0 %copy-start.2 = (f32[512]{0:T(512)S(1)}, f32[512]{0:T(512)}, u32[]{:S(2)}) copy-start(f32[512]{0:T(512)} %param.6) | copy-start | bytes 6148
  328.1 0.7 copy-start.1
  340.8 94.4 %collective-permute-start.1 = (bf16[144,64,64]{0,2,1:T(8,128)(2,1)}, bf16[144,64,64]{0,2,1:T(8,128)(2,1)}, u32[]{:S(2)}, u32[]{:S(2)}) collective-permute-start(bf16[144,64,64]{0,2,1:T(8,128)(2,1)} %copy.18), channel_id=1, source_target_pairs={{0,4},{1,5},{2,6},{3,7},{4,0},{5,1},{6,2},{7,3},{8,12},{9,13},{10,... | collective-permute-start | bytes 3538952 | tf_op jit(solution)/shard_map/ppermute | solution.py:8
  441.2 2.6 copy-start
Sparse Core Ops, SparseCore 0:
  12.5 202.7 all-gather.2
  254.2 72.0 all-reduce.1
where the time goes:
time: 454 us; the launch traced here: 453 us
  waiting for transfers between devices  280 us (62%)
  blocking collectives  97.1 us (21%)
  local copies, waits for them, and re-layouts  33 us (7%)
  matrix products  15.1 us (3%)
  between operations  14.1 us (3%)
  starting transfers between devices  7.56 us (2%)
  other arithmetic  5.87 us (1%)
    ppermute x2, waiting for transfers between devices, from_partner(): lax.ppermute(x, axis, [(i, i ^ 1 << bit) for i in range(lax.axis_size(axi...  223 us
    all_to_all x1, blocking collectives, body(): lax.all_to_all(pooled, 'wide', split_axis=0, concat_axis=2, tiled=True)  81.8 us
    psum x1, waiting for transfers between devices, body(): pre_act = lax.psum(partial_value, 'narrow') + bias[None, :]  56.1 us
    all_gather x1, blocking collectives, body(): cot_whole = lax.all_gather(grad_hidden, 'narrow', axis=1, tiled=True)  15.3 us
    unnamed x11, local copies, waits for them, and re-layouts  13.9 us
  transfers between devices with their start and end apart: 4, of which 3 were waited for; matrix products, arithmetic and copies ran while one was open for 6% of the time, Pallas kernels for 0%

commit v1 on v0

v1 whole, which is shorter than its diff:
```python
import jax
import jax.numpy as jnp
from jax import lax
from jax.sharding import Mesh, PartitionSpec as P

X, ZH, Y = 4, 2, 8
BF = jnp.bfloat16
F32 = jnp.float32


def swap_block(v):
    return lax.ppermute(v, "nw", [(i, i ^ 4) for i in range(8)])


def cross_block(v):
    pairs = [(a * 8 + b, (a ^ 1) * 8 + (b ^ 4)) for a in range(ZH) for b in range(8)]
    return lax.ppermute(v, ("zh", "nw"), pairs)


def cross_same(v):
    return lax.ppermute(v, "zh", [(0, 1), (1, 0)])


def in_order(own, other, zh, axis):
    first = zh == 0
    return jnp.stack([jnp.where(first, own, other), jnp.where(first, other, own)], axis)


def folded_weights(w, zh):
    hidden = w.shape[-1]
    raw = w.reshape(X, ZH, Y, hidden)
    raw_other = cross_same(w).reshape(X, ZH, Y, hidden)
    mine = in_order(raw, raw_other, zh, 0)
    send = raw.transpose(0, 2, 1, 3).reshape(X * Y, ZH, hidden)
    turned = lax.all_to_all(send, ("x", "y"), 0, 0, tiled=True)
    near = swap_block(turned)
    far = cross_block(turned)
    theirs = in_order(near, far, zh, 0)
    theirs = theirs.reshape(ZH, X, Y, ZH, hidden).transpose(3, 1, 0, 2, 4)
    fold = (mine.astype(F32) + theirs.astype(F32)).astype(BF)
    fold = fold.reshape(ZH, 64, hidden)
    along_y = lax.all_gather(fold, "y", axis=1, tiled=False)
    along_x = lax.all_gather(along_y, "x", axis=0, tiled=False)
    return along_x.reshape(64 * 64, hidden)


def body(pooled, w_top, bias, grad_hidden):
    zh = lax.axis_index("zh")
    nw = lax.axis_index("nw")
    half = nw // 4
    count = pooled.shape[0] // (X * ZH * Y)
    hc = count // 2
    width = pooled.shape[-1]
    scale = width ** (-0.5)

    weights = folded_weights(w_top[0], zh)

    by_dest = pooled.reshape(X, ZH, Y, count, width).transpose(1, 0, 2, 3, 4)
    by_dest = by_dest.reshape(ZH, X * Y, count, width)
    mine = lax.dynamic_index_in_dim(by_dest, zh, 0, keepdims=False)
    theirs = lax.dynamic_index_in_dim(by_dest, 1 - zh, 0, keepdims=False)
    both = jnp.concatenate([mine, theirs], 1)
    both = lax.all_to_all(both, ("x", "y"), 0, 0, tiled=True)
    own = both[:, :count]
    away = both[:, count:]
    pair_own = swap_block(own)
    pair_away = cross_block(away)
    away_half = lax.dynamic_slice_in_dim(away, half * hc, hc, 1)
    same_away = cross_same(away_half)

    def fields(a, b):
        n = a.shape[1]
        v = in_order(a.reshape(X, Y, n, width), b.reshape(X, Y, n, width), zh, 1)
        return v.reshape(X * ZH * Y, n, width).transpose(1, 0, 2)

    left = fields(lax.dynamic_slice_in_dim(own, half * hc, hc, 1), same_away)
    right = fields(pair_own, pair_away)
    right_half = lax.dynamic_slice_in_dim(right, half * hc, hc, 0)
    gram = jnp.einsum("sie,sje->sij", left, right_half, preferred_element_type=F32)
    gram = (gram * scale).astype(BF).reshape(hc, 64 * 64)
    part = jnp.dot(gram, weights, preferred_element_type=F32).astype(BF)
    parts = lax.all_gather(part, "nw", axis=0, tiled=False)
    pre_act = parts.reshape(2, 4, hc, -1).astype(F32).sum(1).reshape(count, -1) + bias[None, :]

    share = grad_hidden.shape[1]
    mine_pre = lax.dynamic_slice_in_dim(pre_act, nw * share, share, 1)
    hidden = jax.nn.silu(mine_pre).astype(BF)
    cot = lax.all_gather(grad_hidden, "nw", axis=1, tiled=True)
    sig = jax.nn.sigmoid(pre_act)
    grad_pre = (cot.astype(F32) * (sig * (1.0 + pre_act * (1.0 - sig)))).astype(BF)
    both_grads = lax.dot_general(
        grad_pre, weights, (((1,), (1,)), ((), ())), preferred_element_type=F32
    )
    both_grads = both_grads.astype(BF).reshape(count, 64, 64)
    grad_pooled = jnp.einsum("sij,sje->sie", both_grads, right, preferred_element_type=F32)
    return hidden, (grad_pooled * scale).astype(BF)[:, None]


def solution(mesh):
    fine = Mesh(mesh.devices.reshape(X, ZH, Y, 8), ("x", "zh", "y", "nw"))
    wide = ("x", "zh", "y")
    in_specs = (P(None, "nw", wide, None), P("nw", wide, None), P(), P(wide, "nw"))
    out_specs = (P(wide, "nw"), P(wide, "nw", None, None))
    return jax.shard_map(body, mesh=fine, in_specs=in_specs, out_specs=out_specs, check_vma=False)
```

time: 454 us -> 259 us (0.57)
  waiting for transfers between devices: 280 us -> 64.5 us
  starting transfers between devices: 7.56 us -> 51.3 us
  local copies, waits for them, and re-layouts: 33 us -> 14 us
    ppermute x2 -> x6, waiting for transfers between devices: 223 us -> 0.88 us  [the longest x2 0.87 us: cross_block(): return lax.ppermute(v, ('zh', 'nw'), pairs)]
    all_gather x1 -> x2, blocking collectives: 15.3 us -> 97.6 us  [the longest x1 82.3 us: body(): cot = lax.all_gather(grad_hidden, 'nw', axis=1, tiled=True)]
    all_to_all x1 -> x0, blocking collectives: 81.8 us -> none  [body(): lax.all_to_all(pooled, 'wide', split_axis=0, concat_axis=2, tiled=True)]
    psum x1 -> x0, waiting for transfers between devices: 56.1 us -> none  [body(): pre_act = lax.psum(partial_value, 'narrow') + bias[None, :]]
    all_gather x1 -> x2, waiting for transfers between devices: 0.02 us -> 38.6 us  [the longest x1 38.6 us: folded_weights(): along_y = lax.all_gather(fold, 'y', axis=1, tiled=False)]
    ppermute x2 -> x6, starting transfers between devices: 7.48 us -> 33 us  [the longest x2 17 us: cross_same(): return lax.ppermute(v, 'zh', [(0, 1), (1, 0)])]
    all_to_all x0 -> x2, waiting for transfers between devices: none -> 25 us  [the longest x1 25 us: body(): both = lax.all_to_all(both, ('x', 'y'), 0, 0, tiled=True)]
    all_to_all x0 -> x2, starting transfers between devices: none -> 18.2 us  [the longest x1 10.5 us: folded_weights(): turned = lax.all_to_all(send, ('x', 'y'), 0, 0, tiled=True)]
  transfers between devices with their start and end apart: 4 -> 10, of which waited for: 3 -> 3; matrix products, arithmetic and copies ran while one was open for 6% -> 5% of each run, Pallas kernels for 0% -> 0%
where the time goes in v1:
time: 259 us; the launch traced here: 258 us
  blocking collectives  97.6 us (38%)
  waiting for transfers between devices  64.5 us (25%)
  starting transfers between devices  51.3 us (20%)
  between operations  14.3 us (6%)
  local copies, waits for them, and re-layouts  14 us (5%)
  matrix products  11.3 us (4%)
  other arithmetic  5.17 us (2%)
    all_gather x1, blocking collectives, body(): cot = lax.all_gather(grad_hidden, 'nw', axis=1, tiled=True)  82.3 us
    all_gather x1, waiting for transfers between devices, folded_weights(): along_y = lax.all_gather(fold, 'y', axis=1, tiled=False)  38.6 us
    all_to_all x1, waiting for transfers between devices, body(): both = lax.all_to_all(both, ('x', 'y'), 0, 0, tiled=True)  25 us
    ppermute x2, starting transfers between devices, cross_same(): return lax.ppermute(v, 'zh', [(0, 1), (1, 0)])  17 us
    all_gather x1, blocking collectives, body(): parts = lax.all_gather(part, 'nw', axis=0, tiled=False)  15.3 us
    all_to_all x1, starting transfers between devices, folded_weights(): turned = lax.all_to_all(send, ('x', 'y'), 0, 0, tiled=True)  10.5 us
    ppermute x2, starting transfers between devices, cross_block(): return lax.ppermute(v, ('zh', 'nw'), pairs)  8.86 us
    all_to_all x1, starting transfers between devices, body(): both = lax.all_to_all(both, ('x', 'y'), 0, 0, tiled=True)  7.71 us
  transfers between devices with their start and end apart: 10, of which 3 were waited for; matrix products, arithmetic and copies ran while one was open for 5% of the time, Pallas kernels for 0%

profile of v1, /device:TPU:1, one launch (start us, length us, event | category | flops | bytes accessed | tf_op | source)
XLA Modules:
  0.0 258.1 jit_solution(4151250187174134296)
XLA Ops:
  7.2 0.8 copy.68
  8.0 0.7 copy.56
  8.7 10.5 %all-to-all-start.1 = ((bf16[32,2,512]{2,1,0:T(2,128)(2,1)}), bf16[32,2,512]{2,1,0:T(2,128)(2,1)S(1)}, u32[]{:S(2)}, u32[]{:S(2)}) async-start(bf16[32,2,512]{2,1,0:T(2,128)(2,1)} %copy.56), calls=%async_computation.1 | async-start | bytes 131072 | tf_op jit(solution)/shard_map/all_to_all | solution.py:35
  19.2 0.0 all-gather.5.cloned.1.call-start
  19.3 10.6 %collective-permute-start.3 = (bf16[64,512]{1,0:T(8,128)(2,1)}, bf16[64,512]{1,0:T(8,128)(2,1)S(1)}, u32[]{:S(2)}, u32[]{:S(2)}) collective-permute-start(bf16[64,512]{1,0:T(8,128)(2,1)} %bitcast.75), channel_id=1, source_target_pairs={{0,64},{64,0},{1,65},{65,1},{2,66},{66,2},{3,67},{67,3},{4,68},{68... | collective-permute-start | bytes 196616 | tf_op jit(solution)/shard_map/ppermute | solution.py:21
  29.9 4.0 %collective-permute-start.4 = (bf16[32,2,512]{2,1,0:T(2,128)(2,1)S(1)}, bf16[32,2,512]{2,1,0:T(2,128)(2,1)S(1)}, u32[]{:S(2)}, u32[]{:S(2)}) collective-permute-start(bf16[32,2,512]{2,1,0:T(2,128)(2,1)S(1)} %all-to-all-done.1), channel_id=1, source_target_pairs={{0,4},{1,5},{2,6},{3,7},{4,0},{5,1},{6,2},{7,3},{8,12},{9,13},{10,... | collective-permute-start | bytes 196616 | tf_op jit(solution)/shard_map/ppermute | solution.py:12
  33.9 7.0 %collective-permute-start.5 = (bf16[32,2,512]{2,1,0:T(2,128)(2,1)S(1)}, bf16[32,2,512]{2,1,0:T(2,128)(2,1)S(1)}, u32[]{:S(2)}, u32[]{:S(2)}) collective-permute-start(bf16[32,2,512]{2,1,0:T(2,128)(2,1)S(1)} %all-to-all-done.1), channel_id=1, source_target_pairs={{0,68},{1,69},{2,70},{3,71},{4,64},{5,65},{6,66},{7,67},{64,4},{65... | collective-permute-start | bytes 196616 | tf_op jit(solution)/shard_map/ppermute | solution.py:17
  40.9 0.9 broadcast_select_fusion.7
  41.8 0.9 collective-permute-done.5
  42.7 0.7 fusion.3
  43.4 0.0 all-gather.5.cloned.1.call-update
  43.4 1.8 copy.50
  45.3 0.2 dynamic-slice_bitcast_fusion.1
  45.4 1.6 pad_maximum_fusion
  47.0 7.7 %all-to-all-start = ((bf16[32,288,128]{2,1,0:T(8,128)(2,1)}), bf16[32,288,128]{2,1,0:T(8,128)(2,1)S(1)}, u32[]{:S(2)}, u32[]{:S(2)}) async-start(bf16[32,288,128]{2,1,0:T(8,128)(2,1)} %pad_maximum_fusion), calls=%async_computation | async-start | bytes 4718592 | tf_op jit(solution)/shard_map/all_to_all | solution.py:63
  54.7 0.0 all-gather.7.cloned.1.call-start
  54.8 38.6 %all-gather.5.cloned.1.call-done = bf16[2,8,64,512]{3,2,1,0:T(8,128)(2,1)} async-done(((bf16[2,1,64,512]{3,2,1,0:T(8,128)(2,1)}), bf16[2,8,64,512]{3,2,1,0:T(8,128)(2,1)}) %all-gather.5.cloned.1.call-update) | async-done | bytes 1048592 | tf_op jit(solution)/shard_map/all_gather | solution.py:42
  93.3 0.0 all-gather.7.cloned.1.call-update
  93.4 25.0 %all-to-all-done = bf16[32,288,128]{2,1,0:T(8,128)(2,1)S(1)} async-done(((bf16[32,288,128]{2,1,0:T(8,128)(2,1)}), bf16[32,288,128]{2,1,0:T(8,128)(2,1)S(1)}, u32[]{:S(2)}, u32[]{:S(2)}) %all-to-all-start) | async-done | bytes 2359328 | tf_op jit(solution)/shard_map/all_to_all | solution.py:63
  118.3 1.2 fusion.7
  119.5 1.9 collective-permute-start.2
  121.4 3.1 %collective-permute-start.1 = (bf16[32,144,128]{2,1,0:T(8,128)(2,1)}, bf16[32,144,128]{2,1,0:T(8,128)(2,1)S(1)}, u32[]{:S(2)}, u32[]{:S(2)}) collective-permute-start(bf16[32,144,128]{2,1,0:T(8,128)(2,1)} %get-tuple-element.14), channel_id=1, source_target_pairs={{0,4},{1,5},{2,6},{3,7},{4,0},{5,1},{6,2},{7,3},{8,12},{9,13},{10,... | collective-permute-start | bytes 3538952 | tf_op jit(solution)/shard_map/ppermute | solution.py:12
  124.5 0.9 constant_dynamic-slice_fusion
  125.4 6.4 %collective-permute-start = (bf16[32,72,128]{2,1,0:T(8,128)(2,1)}, bf16[32,72,128]{2,1,0:T(8,128)(2,1)}, u32[]{:S(2)}, u32[]{:S(2)}) collective-permute-start(bf16[32,72,128]{2,1,0:T(8,128)(2,1)} %constant_dynamic-slice_fusion), channel_id=1, source_target_pairs={{0,64},{64,0},{1,65},{65,1},{2,66},{66,2},{3,67},{67,3},{4,68},{68... | collective-permute-start | bytes 1769480 | tf_op jit(solution)/shard_map/ppermute | solution.py:21
  131.8 82.3 %all_gather.23 = bf16[144,512]{0,1:T(8,128)(2,1)} all-gather(bf16[144,64]{0,1:T(8,128)(2,1)} %param.7), channel_id=1, replica_groups=mesh['x'=4,'zh'=2,'y'=8,'nw'=8] {'nw'}, dimensions={1}, use_global_device_ids=true | all-gather | bytes 165888 | tf_op jit(solution)/shard_map/all_gather | solution.py:88
  214.1 1.7 copy.60
  215.8 1.5 broadcast_select_fusion.3
  217.3 0.1 copy.52
  217.4 0.1 copy.51
  217.5 0.2 pad_maximum_fusion.1
  217.7 0.0 collective-permute-done.2
  217.7 0.0 collective-permute-done.1
  217.7 0.2 broadcast_select_fusion
  217.9 0.3 copy_dynamic-update-slice_fusion.1
  218.2 0.5 copy_dynamic-update-slice_fusion
  218.7 1.5 copy-done
  220.1 0.7 multiply_convert_fusion.1
  220.9 0.9 reshape.161
  221.8 0.0 all-gather.7.cloned.1.call-done
  221.8 0.0 copy-start.2
  221.8 3.0 %convolution_convert_fusion.1 = bf16[72,512]{1,0:T(8,128)(2,1)S(1)} fusion(bf16[72,4096]{1,0:T(8,128)(2,1)S(1)} %reshape.161, bf16[4096,512]{1,0:T(8,128)(2,1)} %bitcast.60), kind=kOutput, calls=%fused_computation.15 | convolution fusion | flops 302026752 | bytes 4857856 | tf_op jit(solution)/shard_map/dot_general | solution.py:81
  224.9 15.3 %all-gather.1 = bf16[576,512]{1,0:T(8,128)(2,1)S(1)} all-gather(bf16[72,512]{1,0:T(8,128)(2,1)S(1)} %convolution_convert_fusion.1), channel_id=3, replica_groups=mesh['x'=4,'zh'=2,'y'=8,'nw'=8] {'nw'}, dimensions={0}, use_global_device_ids=true | all-gather | bytes 663552 | tf_op jit(solution)/shard_map/all_gather | solution.py:82
  240.2 0.1 convert_reduce_fusion
  240.3 0.1 multiply_convert_fusion.4
  240.5 0.7 copy.61
  241.2 3.7 %convolution_convert_fusion = bf16[144,4096]{1,0:T(8,128)(2,1)S(1)} fusion(bf16[4096,512]{1,0:T(8,128)(2,1)} %bitcast.61, f32[144,512]{1,0:T(8,128)S(1)} %bitcast_add_fusion, bf16[144,512]{1,0:T(8,128)(2,1)S(1)} %copy-done.1), kind=kOutput, calls=%fused_computation | convolution fusion | flops 605306880 | bytes 5816320 | tf_op jit(solution)/shard_map/dot_general | solution.py:91
  244.9 2.6 reshape.166
  247.5 3.8 %fusion = bf16[144,1,64,128]{3,2,1,0:T(8,128)(2,1)} fusion(bf16[144,64,64]{2,1,0:T(8,128)(2,1)S(1)} %reshape.166, bf16[144,64,128]{2,1,0:T(8,128)(2,1)} %bitcast.64), kind=kOutput, calls=%fused_computation.2 | convolution fusion | flops 153354240 | bytes 5898240 | tf_op jit(solution)/shard_map/sij,sje->sie/dot_general | solution.py:95
  (11 shorter events, 0.1 us)
Async XLA Ops:
  8.7 21.2 %all-to-all-start.1 = ((bf16[32,2,512]{2,1,0:T(2,128)(2,1)}), bf16[32,2,512]{2,1,0:T(2,128)(2,1)S(1)}, u32[]{:S(2)}, u32[]{:S(2)}) async-start(bf16[32,2,512]{2,1,0:T(2,128)(2,1)} %copy.56), calls=%async_computation.1 | async-start | bytes 131072 | tf_op jit(solution)/shard_map/all_to_all | solution.py:35
  19.2 74.1 %all-gather.5.cloned.1.call-start = ((), (), s32[]{:S(2)}) async-start(), calls=%async_computation.2 | async-start | bytes 1179648 | tf_op jit(solution)/shard_map/all_gather | solution.py:42
  19.3 21.6 %collective-permute-start.3 = (bf16[64,512]{1,0:T(8,128)(2,1)}, bf16[64,512]{1,0:T(8,128)(2,1)S(1)}, u32[]{:S(2)}, u32[]{:S(2)}) collective-permute-start(bf16[64,512]{1,0:T(8,128)(2,1)} %bitcast.75), channel_id=1, source_target_pairs={{0,64},{64,0},{1,65},{65,1},{2,66},{66,2},{3,67},{67,3},{4,68},{68... | collective-permute-start | bytes 196616 | tf_op jit(solution)/shard_map/ppermute | solution.py:21
  29.9 11.8 %collective-permute-start.4 = (bf16[32,2,512]{2,1,0:T(2,128)(2,1)S(1)}, bf16[32,2,512]{2,1,0:T(2,128)(2,1)S(1)}, u32[]{:S(2)}, u32[]{:S(2)}) collective-permute-start(bf16[32,2,512]{2,1,0:T(2,128)(2,1)S(1)} %all-to-all-done.1), channel_id=1, source_target_pairs={{0,4},{1,5},{2,6},{3,7},{4,0},{5,1},{6,2},{7,3},{8,12},{9,13},{10,... | collective-permute-start | bytes 196616 | tf_op jit(solution)/shard_map/ppermute | solution.py:12
  33.9 8.7 %collective-permute-start.5 = (bf16[32,2,512]{2,1,0:T(2,128)(2,1)S(1)}, bf16[32,2,512]{2,1,0:T(2,128)(2,1)S(1)}, u32[]{:S(2)}, u32[]{:S(2)}) collective-permute-start(bf16[32,2,512]{2,1,0:T(2,128)(2,1)S(1)} %all-to-all-done.1), channel_id=1, source_target_pairs={{0,68},{1,69},{2,70},{3,71},{4,64},{5,65},{6,66},{7,67},{64,4},{65... | collective-permute-start | bytes 196616 | tf_op jit(solution)/shard_map/ppermute | solution.py:17
  47.0 71.3 %all-to-all-start = ((bf16[32,288,128]{2,1,0:T(8,128)(2,1)}), bf16[32,288,128]{2,1,0:T(8,128)(2,1)S(1)}, u32[]{:S(2)}, u32[]{:S(2)}) async-start(bf16[32,288,128]{2,1,0:T(8,128)(2,1)} %pad_maximum_fusion), calls=%async_computation | async-start | bytes 4718592 | tf_op jit(solution)/shard_map/all_to_all | solution.py:63
  54.7 167.1 %all-gather.7.cloned.1.call-start = ((), (), s32[]{:S(2)}) async-start(), calls=%async_computation.3 | async-start | bytes 5242880 | tf_op jit(solution)/shard_map/all_gather | solution.py:43
  119.5 98.2 %collective-permute-start.2 = (bf16[32,144,128]{2,1,0:T(8,128)(2,1)S(1)}, bf16[32,144,128]{2,1,0:T(8,128)(2,1)S(1)}, u32[]{:S(2)}, u32[]{:S(2)}) collective-permute-start(bf16[32,144,128]{2,1,0:T(8,128)(2,1)S(1)} %get-tuple-element.15), channel_id=1, source_target_pairs={{0,68},{1,69},{2,70},{3,71},{4,64},{5,65},{6,66},{7,67},{64,4},{65... | collective-permute-start | bytes 3538952 | tf_op jit(solution)/shard_map/ppermute | solution.py:17
  121.4 96.3 %collective-permute-start.1 = (bf16[32,144,128]{2,1,0:T(8,128)(2,1)}, bf16[32,144,128]{2,1,0:T(8,128)(2,1)S(1)}, u32[]{:S(2)}, u32[]{:S(2)}) collective-permute-start(bf16[32,144,128]{2,1,0:T(8,128)(2,1)} %get-tuple-element.14), channel_id=1, source_target_pairs={{0,4},{1,5},{2,6},{3,7},{4,0},{5,1},{6,2},{7,3},{8,12},{9,13},{10,... | collective-permute-start | bytes 3538952 | tf_op jit(solution)/shard_map/ppermute | solution.py:12
  125.4 90.4 %collective-permute-start = (bf16[32,72,128]{2,1,0:T(8,128)(2,1)}, bf16[32,72,128]{2,1,0:T(8,128)(2,1)}, u32[]{:S(2)}, u32[]{:S(2)}) collective-permute-start(bf16[32,72,128]{2,1,0:T(8,128)(2,1)} %constant_dynamic-slice_fusion), channel_id=1, source_target_pairs={{0,64},{64,0},{1,65},{65,1},{2,66},{66,2},{3,67},{67,3},{4,68},{68... | collective-permute-start | bytes 1769480 | tf_op jit(solution)/shard_map/ppermute | solution.py:21
  218.7 1.5 copy-start
  221.8 18.5 %copy-start.2 = (f32[512]{0:T(512)S(1)}, f32[512]{0:T(512)}, u32[]{:S(2)}) copy-start(f32[512]{0:T(512)} %param.6) | copy-start | bytes 6148
  224.9 16.3 %copy-start.1 = (bf16[144,512]{1,0:T(8,128)(2,1)S(1)}, bf16[144,512]{1,0:T(8,128)(2,1)}, u32[]{:S(2)}) copy-start(bf16[144,512]{1,0:T(8,128)(2,1)} %copy.60) | copy-start | bytes 442372
Sparse Core Ops, SparseCore 0:
  43.5 49.7 all-gather.4
  95.4 59.1 all-gather.6

commit v2 on v1

v2 whole, which is shorter than its diff:
```python
import jax
import jax.numpy as jnp
from jax import lax
from jax.sharding import Mesh, PartitionSpec as P

X, ZH, Y = 4, 2, 8
XY = X * Y
CHUNKS = (16, 64, 64)
BF = jnp.bfloat16
F32 = jnp.float32


def swap_block(v):
    return lax.ppermute(v, "nw", [(i, i ^ 4) for i in range(8)])


def cross_block(v):
    pairs = [(a * 8 + b, (a ^ 1) * 8 + (b ^ 4)) for a in range(ZH) for b in range(8)]
    return lax.ppermute(v, ("zh", "nw"), pairs)


def cross_same(v):
    return lax.ppermute(v, "zh", [(0, 1), (1, 0)])


def in_order(own, other, zh, axis):
    first = zh == 0
    return jnp.stack([jnp.where(first, own, other), jnp.where(first, other, own)], axis)


def after(v, other, zh):
    return jnp.where(zh > 1, other[(0,) * other.ndim].astype(v.dtype), v)


def folded_weights(raw, raw_other, turned, zh):
    units = raw.shape[-1]
    mine = in_order(raw, raw_other, zh, 0)
    near = swap_block(turned)
    far = cross_block(turned)
    theirs = in_order(near, far, zh, 0).reshape(ZH, X, Y, ZH, units)
    theirs = theirs.transpose(3, 1, 0, 2, 4)
    fold = (mine.astype(F32) + theirs.astype(F32)).astype(BF)
    return fold.reshape(ZH * 64, units)


def body(pooled, w_top, bias, grad_hidden):
    zh = lax.axis_index("zh")
    nw = lax.axis_index("nw")
    half = nw // 4
    count = pooled.shape[0] // (XY * ZH)
    width = pooled.shape[-1]
    scale = width ** (-0.5)
    w = w_top[0]
    units = w.shape[-1]

    by_dest = pooled.reshape(X, ZH, Y, count, width).transpose(1, 0, 2, 3, 4)
    by_dest = by_dest.reshape(ZH, XY, count, width)
    mine = lax.dynamic_index_in_dim(by_dest, zh, 0, keepdims=False)
    theirs = lax.dynamic_index_in_dim(by_dest, 1 - zh, 0, keepdims=False)

    raw = w.reshape(X, ZH, Y, units)
    w_rows = raw.transpose(0, 2, 1, 3).reshape(XY, ZH * units // width, width)
    raw_other = cross_same(w).reshape(X, ZH, Y, units)
    cot = lax.all_gather(grad_hidden, "nw", axis=1, tiled=True)

    at = 0
    arrived = None
    lefts, rights, right_halves = [], [], []
    for index, n in enumerate(CHUNKS):
        pieces = [mine[:, at : at + n], theirs[:, at : at + n]]
        at += n
        if index == 0:
            pieces.append(w_rows)
        send = jnp.concatenate(pieces, 1)
        if arrived is not None:
            send = after(send, arrived, zh)
        got = lax.all_to_all(send, ("x", "y"), 0, 0, tiled=True)
        arrived = got
        if index == 0:
            turned = after(got[:, 2 * n :].reshape(XY, ZH, units), cot, zh)
            fold = folded_weights(raw, raw_other, turned, zh)
            weights = lax.all_gather(fold, ("x", "y"), axis=0, tiled=True)
        own, away = got[:, :n], got[:, n : 2 * n]
        pair_own = swap_block(own)
        pair_away = cross_block(away)
        h = n // 2
        same_away = cross_same(lax.dynamic_slice_in_dim(away, half * h, h, 1))

        def rows(a, b):
            m = a.shape[1]
            return in_order(a, b, zh, 1).reshape(XY * ZH, m, width).transpose(1, 0, 2)

        def columns(a, b):
            m = a.shape[1]
            v = in_order(a.reshape(X, Y, m, width), b.reshape(X, Y, m, width), zh, 1)
            return v.reshape(XY * ZH, m, width).transpose(1, 0, 2)

        lefts.append(rows(lax.dynamic_slice_in_dim(own, half * h, h, 1), same_away))
        right = columns(pair_own, pair_away)
        rights.append(right)
        right_halves.append(lax.dynamic_slice_in_dim(right, half * h, h, 0))

    left = jnp.concatenate(lefts, 0)
    right = jnp.concatenate(rights, 0)
    right_half = jnp.concatenate(right_halves, 0)
    hc = count // 2
    gram = jnp.einsum("sie,sje->sij", left, right_half, preferred_element_type=F32)
    gram = (gram * scale).astype(BF).reshape(hc, 64 * 64)
    part = jnp.dot(gram, weights, preferred_element_type=F32).astype(BF)
    parts = lax.all_gather(part, "nw", axis=0, tiled=False)
    sums = parts.reshape(2, 4, hc, units).astype(F32).sum(1)
    ordered = []
    at = 0
    for n in CHUNKS:
        h = n // 2
        ordered += [sums[0, at : at + h], sums[1, at : at + h]]
        at += h
    pre_act = jnp.concatenate(ordered, 0) + bias[None, :]

    share = grad_hidden.shape[1]
    mine_pre = lax.dynamic_slice_in_dim(pre_act, nw * share, share, 1)
    hidden = jax.nn.silu(mine_pre).astype(BF)
    sig = jax.nn.sigmoid(pre_act)
    grad_pre = (cot.astype(F32) * (sig * (1.0 + pre_act * (1.0 - sig)))).astype(BF)
    both_grads = lax.dot_general(
        grad_pre, weights, (((1,), (1,)), ((), ())), preferred_element_type=F32
    )
    both_grads = both_grads.astype(BF).reshape(count, X, Y, ZH, 64)
    both_grads = both_grads.transpose(0, 1, 3, 2, 4).reshape(count, 64, 64)
    grad_pooled = jnp.einsum("sij,sje->sie", both_grads, right, preferred_element_type=F32)
    return hidden, (grad_pooled * scale).astype(BF)[:, None]


def solution(mesh):
    fine = Mesh(mesh.devices.reshape(X, ZH, Y, 8), ("x", "zh", "y", "nw"))
    wide = ("x", "zh", "y")
    in_specs = (P(None, "nw", wide, None), P("nw", wide, None), P(), P(wide, "nw"))
    out_specs = (P(wide, "nw"), P(wide, "nw", None, None))
    return jax.shard_map(body, mesh=fine, in_specs=in_specs, out_specs=out_specs, check_vma=False)
```

time: 259 us -> 242 us (0.934)
  blocking collectives: 97.6 us -> 34.7 us
  starting transfers between devices: 51.3 us -> 79.4 us
  waiting for transfers between devices: 64.5 us -> 78.2 us
  local copies, waits for them, and re-layouts: 14 us -> 17.8 us
    all_gather x1, blocking collectives: 82.3 us -> 15.5 us  [body(): cot = lax.all_gather(grad_hidden, 'nw', axis=1, tiled=True)]
    ppermute x2 -> x4, waiting for transfers between devices: 0.87 us -> 42.8 us  [cross_block(): return lax.ppermute(v, ('zh', 'nw'), pairs)]
    all_gather x2 -> x1, waiting for transfers between devices: 38.6 us -> 0.02 us  [body(): weights = lax.all_gather(fold, ('x', 'y'), axis=0, tiled=True)]
    ppermute x2 -> x4, waiting for transfers between devices: 0.01 us -> 12.8 us  [swap_block(): return lax.ppermute(v, 'nw', [(i, i ^ 4) for i in range(8)])]
    ppermute x2 -> x4, starting transfers between devices: 17 us -> 27.7 us  [cross_same(): return lax.ppermute(v, 'zh', [(0, 1), (1, 0)])]
    all_to_all x2 -> x3, starting transfers between devices: 18.2 us -> 28.8 us  [body(): got = lax.all_to_all(send, ('x', 'y'), 0, 0, tiled=True)]
    all_to_all x2 -> x3, waiting for transfers between devices: 25 us -> 15.9 us  [body(): got = lax.all_to_all(send, ('x', 'y'), 0, 0, tiled=True)]
    ppermute x2 -> x4, waiting for transfers between devices: 0.01 us -> 6.65 us  [cross_same(): return lax.ppermute(v, 'zh', [(0, 1), (1, 0)])]
  transfers between devices with their start and end apart: 10 -> 16, of which waited for: 3 -> 9; matrix products, arithmetic and copies ran while one was open for 5% -> 6% of each run, Pallas kernels for 0% -> 0%
where the time goes in v2:
time: 242 us; the launch traced here: 241 us
  starting transfers between devices  79.4 us (33%)
  waiting for transfers between devices  78.2 us (32%)
  blocking collectives  34.7 us (14%)
  local copies, waits for them, and re-layouts  17.8 us (7%)
  between operations  14.8 us (6%)
  matrix products  9.65 us (4%)
  other arithmetic  6.73 us (3%)
    ppermute x4, waiting for transfers between devices, cross_block(): return lax.ppermute(v, ('zh', 'nw'), pairs)  42.8 us
    all_to_all x3, starting transfers between devices, body(): got = lax.all_to_all(send, ('x', 'y'), 0, 0, tiled=True)  28.8 us
    ppermute x4, starting transfers between devices, cross_same(): return lax.ppermute(v, 'zh', [(0, 1), (1, 0)])  27.7 us
    all_gather x1, blocking collectives, body(): parts = lax.all_gather(part, 'nw', axis=0, tiled=False)  19.2 us
    all_to_all x3, waiting for transfers between devices, body(): got = lax.all_to_all(send, ('x', 'y'), 0, 0, tiled=True)  15.9 us
    all_gather x1, blocking collectives, body(): cot = lax.all_gather(grad_hidden, 'nw', axis=1, tiled=True)  15.5 us
    ppermute x4, starting transfers between devices, cross_block(): return lax.ppermute(v, ('zh', 'nw'), pairs)  13 us
    ppermute x4, waiting for transfers between devices, swap_block(): return lax.ppermute(v, 'nw', [(i, i ^ 4) for i in range(8)])  12.8 us
  transfers between devices with their start and end apart: 16, of which 9 were waited for; matrix products, arithmetic and copies ran while one was open for 6% of the time, Pallas kernels for 0%

profile of v2, /device:TPU:1, one launch (start us, length us, event | category | flops | bytes accessed | tf_op | source)
XLA Modules:
  0.0 241.3 jit_solution(17213259549579915207)
XLA Ops:
  7.2 1.9 copy.60
  9.1 0.7 reshape.215
  10.0 1.0 copy-done
  11.0 0.8 pad_maximum_fusion.2
  11.8 10.5 %all-to-all-start = ((bf16[32,40,128]{2,1,0:T(8,128)(2,1)}), bf16[32,40,128]{2,1,0:T(8,128)(2,1)S(1)}, u32[]{:S(2)}, u32[]{:S(2)}) async-start(bf16[32,40,128]{2,1,0:T(8,128)(2,1)} %pad_maximum_fusion.2), calls=%async_computation | async-start | bytes 655360 | tf_op jit(solution)/shard_map/all_to_all | solution.py:77
  22.3 10.6 %collective-permute-start.9 = (bf16[64,512]{1,0:T(8,128)(2,1)}, bf16[64,512]{1,0:T(8,128)(2,1)S(1)}, u32[]{:S(2)}, u32[]{:S(2)}) collective-permute-start(bf16[64,512]{1,0:T(8,128)(2,1)} %bitcast.129), channel_id=1, source_target_pairs={{0,64},{64,0},{1,65},{65,1},{2,66},{66,2},{3,67},{67,3},{4,68},{68... | collective-permute-start | bytes 196616 | tf_op jit(solution)/shard_map/ppermute | solution.py:23
  33.0 15.5 %all_gather.12 = bf16[144,512]{0,1:T(8,128)(2,1)S(1)} all-gather(bf16[144,64]{0,1:T(8,128)(2,1)} %param.7), channel_id=1, replica_groups=mesh['x'=4,'zh'=2,'y'=8,'nw'=8] {'nw'}, dimensions={1}, use_global_device_ids=true | all-gather | bytes 165888 | tf_op jit(solution)/shard_map/all_gather | solution.py:64
  49.0 0.7 slice_select_fusion
  49.7 2.2 collective-permute-start.10
  52.0 2.0 collective-permute-start.11
  54.0 2.1 collective-permute-done.10
  56.1 3.0 %collective-permute-done.11 = bf16[32,2,512]{2,1,0:T(2,128)(2,1)S(1)} collective-permute-done((bf16[32,2,512]{2,1,0:T(2,128)(2,1)S(1)}, bf16[32,2,512]{2,1,0:T(2,128)(2,1)S(1)}, u32[]{:S(2)}, u32[]{:S(2)}) %collective-permute-start.11) | collective-permute-done | bytes 65568 | tf_op jit(solution)/shard_map/ppermute | solution.py:19
  59.2 0.7 fusion.19
  60.0 1.3 slice.92
  61.3 2.0 maximum_select_fusion
  63.3 9.5 %all-to-all-start.1 = ((bf16[32,128,128]{2,1,0:T(8,128)(2,1)}), bf16[32,128,128]{2,1,0:T(8,128)(2,1)S(1)}, u32[]{:S(2)}, u32[]{:S(2)}) async-start(bf16[32,128,128]{2,1,0:T(8,128)(2,1)} %maximum_select_fusion), calls=%async_computation.1 | async-start | bytes 2097152 | tf_op jit(solution)/shard_map/all_to_all | solution.py:77
  72.8 6.0 %collective-permute-start = (bf16[32,8,128]{2,1,0:T(8,128)(2,1)S(1)}, bf16[32,8,128]{2,1,0:T(8,128)(2,1)S(1)}, u32[]{:S(2)}, u32[]{:S(2)}) collective-permute-start(bf16[32,8,128]{2,1,0:T(8,128)(2,1)S(1)} %constant_dynamic-slice_fusion.2), channel_id=1, source_target_pairs={{0,64},{64,0},{1,65},{65,1},{2,66},{66,2},{3,67},{67,3},{4,68},{68... | collective-permute-start | bytes 196616 | tf_op jit(solution)/shard_map/ppermute | solution.py:23
  78.8 0.8 copy.73
  79.6 3.2 %collective-permute-start.4 = (bf16[32,16,128]{2,1,0:T(8,128)(2,1)S(1)}, bf16[32,16,128]{2,1,0:T(8,128)(2,1)S(1)}, u32[]{:S(2)}, u32[]{:S(2)}) collective-permute-start(bf16[32,16,128]{2,1,0:T(8,128)(2,1)S(1)} %get-tuple-element.31), channel_id=1, source_target_pairs={{0,68},{1,69},{2,70},{3,71},{4,64},{5,65},{6,66},{7,67},{64,4},{65... | collective-permute-start | bytes 393224 | tf_op jit(solution)/shard_map/ppermute | solution.py:19
  82.8 2.2 collective-permute-start.3
  85.3 15.9 %all-to-all-done.1 = bf16[32,128,128]{2,1,0:T(8,128)(2,1)S(1)} async-done(((bf16[32,128,128]{2,1,0:T(8,128)(2,1)}), bf16[32,128,128]{2,1,0:T(8,128)(2,1)S(1)}, u32[]{:S(2)}, u32[]{:S(2)}) %all-to-all-start.1) | async-done | bytes 1048608 | tf_op jit(solution)/shard_map/all_to_all | solution.py:77
  101.7 1.9 maximum_select_fusion.1
  103.6 8.8 %all-to-all-start.2 = ((bf16[32,128,128]{2,1,0:T(8,128)(2,1)}), bf16[32,128,128]{2,1,0:T(8,128)(2,1)S(1)}, u32[]{:S(2)}, u32[]{:S(2)}) async-start(bf16[32,128,128]{2,1,0:T(8,128)(2,1)} %maximum_select_fusion.1), calls=%async_computation.2 | async-start | bytes 2097152 | tf_op jit(solution)/shard_map/all_to_all | solution.py:77
  112.6 1.9 collective-permute-start.6
  114.6 6.3 %collective-permute-start.1 = (bf16[32,32,128]{2,1,0:T(8,128)(2,1)S(1)}, bf16[32,32,128]{2,1,0:T(8,128)(2,1)S(1)}, u32[]{:S(2)}, u32[]{:S(2)}) collective-permute-start(bf16[32,32,128]{2,1,0:T(8,128)(2,1)S(1)} %constant_dynamic-slice_fusion.1), channel_id=1, source_target_pairs={{0,64},{64,0},{1,65},{65,1},{2,66},{66,2},{3,67},{67,3},{4,68},{68... | collective-permute-start | bytes 786440 | tf_op jit(solution)/shard_map/ppermute | solution.py:23
  120.9 3.1 %collective-permute-start.5 = (bf16[32,64,128]{2,1,0:T(8,128)(2,1)S(1)}, bf16[32,64,128]{2,1,0:T(8,128)(2,1)S(1)}, u32[]{:S(2)}, u32[]{:S(2)}) collective-permute-start(bf16[32,64,128]{2,1,0:T(8,128)(2,1)S(1)} %get-tuple-element.22), channel_id=1, source_target_pairs={{0,4},{1,5},{2,6},{3,7},{4,0},{5,1},{6,2},{7,3},{8,12},{9,13},{10,... | collective-permute-start | bytes 1572872 | tf_op jit(solution)/shard_map/ppermute | solution.py:14
  124.2 2.9 %collective-permute-done.1 = bf16[32,32,128]{2,1,0:T(8,128)(2,1)S(1)} collective-permute-done((bf16[32,32,128]{2,1,0:T(8,128)(2,1)S(1)}, bf16[32,32,128]{2,1,0:T(8,128)(2,1)S(1)}, u32[]{:S(2)}, u32[]{:S(2)}) %collective-permute-start.1) | collective-permute-done | bytes 262176 | tf_op jit(solution)/shard_map/ppermute | solution.py:23
  127.3 1.4 copy.63
  128.6 17.8 %collective-permute-done.6 = bf16[32,64,128]{2,1,0:T(8,128)(2,1)S(1)} collective-permute-done((bf16[32,64,128]{2,1,0:T(8,128)(2,1)S(1)}, bf16[32,64,128]{2,1,0:T(8,128)(2,1)S(1)}, u32[]{:S(2)}, u32[]{:S(2)}) %collective-permute-start.6) | collective-permute-done | bytes 524320 | tf_op jit(solution)/shard_map/ppermute | solution.py:19
  146.4 7.5 %collective-permute-done.5 = bf16[32,64,128]{2,1,0:T(8,128)(2,1)S(1)} collective-permute-done((bf16[32,64,128]{2,1,0:T(8,128)(2,1)S(1)}, bf16[32,64,128]{2,1,0:T(8,128)(2,1)S(1)}, u32[]{:S(2)}, u32[]{:S(2)}) %collective-permute-start.5) | collective-permute-done | bytes 524320 | tf_op jit(solution)/shard_map/ppermute | solution.py:14
  154.4 5.9 %collective-permute-start.8 = (bf16[32,64,128]{2,1,0:T(8,128)(2,1)S(1)}, bf16[32,64,128]{2,1,0:T(8,128)(2,1)S(1)}, u32[]{:S(2)}, u32[]{:S(2)}) collective-permute-start(bf16[32,64,128]{2,1,0:T(8,128)(2,1)S(1)} %get-tuple-element.25), channel_id=1, source_target_pairs={{0,68},{1,69},{2,70},{3,71},{4,64},{5,65},{6,66},{7,67},{64,4},{65... | collective-permute-start | bytes 1572872 | tf_op jit(solution)/shard_map/ppermute | solution.py:19
  160.4 4.8 %collective-permute-start.2 = (bf16[32,32,128]{2,1,0:T(8,128)(2,1)S(1)}, bf16[32,32,128]{2,1,0:T(8,128)(2,1)S(1)}, u32[]{:S(2)}, u32[]{:S(2)}) collective-permute-start(bf16[32,32,128]{2,1,0:T(8,128)(2,1)S(1)} %constant_dynamic-slice_fusion), channel_id=1, source_target_pairs={{0,64},{64,0},{1,65},{65,1},{2,66},{66,2},{3,67},{67,3},{4,68},{68... | collective-permute-start | bytes 786440 | tf_op jit(solution)/shard_map/ppermute | solution.py:23
  165.3 2.2 collective-permute-start.7
  168.0 3.7 %collective-permute-done.2 = bf16[32,32,128]{2,1,0:T(8,128)(2,1)S(1)} collective-permute-done((bf16[32,32,128]{2,1,0:T(8,128)(2,1)S(1)}, bf16[32,32,128]{2,1,0:T(8,128)(2,1)S(1)}, u32[]{:S(2)}, u32[]{:S(2)}) %collective-permute-start.2) | collective-permute-done | bytes 262176 | tf_op jit(solution)/shard_map/ppermute | solution.py:23
  171.8 0.5 copy.64
  172.4 21.9 %collective-permute-done.8 = bf16[32,64,128]{2,1,0:T(8,128)(2,1)S(1)} collective-permute-done((bf16[32,64,128]{2,1,0:T(8,128)(2,1)S(1)}, bf16[32,64,128]{2,1,0:T(8,128)(2,1)S(1)}, u32[]{:S(2)}, u32[]{:S(2)}) %collective-permute-start.8) | collective-permute-done | bytes 524320 | tf_op jit(solution)/shard_map/ppermute | solution.py:19
  194.3 3.3 %collective-permute-done.7 = bf16[32,64,128]{2,1,0:T(8,128)(2,1)S(1)} collective-permute-done((bf16[32,64,128]{2,1,0:T(8,128)(2,1)S(1)}, bf16[32,64,128]{2,1,0:T(8,128)(2,1)S(1)}, u32[]{:S(2)}, u32[]{:S(2)}) %collective-permute-start.7) | collective-permute-done | bytes 524320 | tf_op jit(solution)/shard_map/ppermute | solution.py:14
  198.5 0.9 copy-done.8
  199.5 0.7 multiply_convert_fusion.1
  200.2 0.9 reshape.222
  201.2 3.0 %convolution_convert_fusion.1 = bf16[72,512]{1,0:T(8,128)(2,1)S(1)} fusion(bf16[72,4096]{1,0:T(8,128)(2,1)S(1)} %reshape.222, bf16[4096,512]{1,0:T(8,128)(2,1)} %all-gather.3.cloned.1.call-done), kind=kOutput, calls=%fused_computation.23 | convolution fusion | flops 302026752 | bytes 4857856 | tf_op jit(solution)/shard_map/dot_general | solution.py:109
  204.2 19.2 %all-gather = bf16[576,512]{1,0:T(8,128)(2,1)S(1)} all-gather(bf16[72,512]{1,0:T(8,128)(2,1)S(1)} %convolution_convert_fusion.1), channel_id=2, replica_groups=mesh['x'=4,'zh'=2,'y'=8,'nw'=8] {'nw'}, dimensions={0}, use_global_device_ids=true | all-gather | bytes 663552 | tf_op jit(solution)/shard_map/all_gather | solution.py:110
  223.8 0.7 copy.76
  224.5 3.7 %convolution_convert_fusion = bf16[144,4096]{1,0:T(8,128)(2,1)S(1)} fusion(bf16[4096,512]{1,0:T(8,128)(2,1)} %all-gather.3.cloned.1.call-done, f32[144,512]{1,0:T(8,128)S(1)} %broadcast_add_fusion, bf16[144,512]{1,0:T(8,128)(2,1)S(1)} %copy-done.10), kind=kOutput, calls=%fused_computation | convolution fusion | flops 605306880 | bytes 5816320 | tf_op jit(solution)/shard_map/dot_general | solution.py:125
  228.2 2.6 %reshape.225 = bf16[144,4,8,2,64]{4,3,2,1,0:T(2,128)(2,1)S(1)} reshape(bf16[144,4096]{1,0:T(8,128)(2,1)S(1)} %convolution_convert_fusion) | data formatting | bytes 2359296 | tf_op jit(solution)/shard_map/reshape | solution.py:128
  230.8 0.5 copy.78
  231.3 0.6 copy-done.7
  232.3 2.2 fusion
  (88 shorter events, 5.0 us)
Async XLA Ops:
  7.2 1.9 copy-start.15
  9.8 1.2 copy-start.12
  10.0 1.0 copy-start
  10.0 44.0 %copy-start.16 = (bf16[1,64,512]{2,1,0:T(8,128)(2,1)S(1)}, bf16[1,64,512]{2,1,0:T(8,128)(2,1)}, u32[]{:S(2)}) copy-start(bf16[1,64,512]{2,1,0:T(8,128)(2,1)} %param.5) | copy-start | bytes 196612
  11.0 48.9 %copy-start.1 = (bf16[32,144,128]{2,1,0:T(8,128)(2,1)S(1)}, bf16[32,144,128]{2,1,0:T(8,128)(2,1)}, u32[]{:S(2)}) copy-start(bf16[32,144,128]{2,1,0:T(8,128)(2,1)} %copy-done) | copy-start | bytes 3538948
  11.8 37.3 %all-to-all-start = ((bf16[32,40,128]{2,1,0:T(8,128)(2,1)}), bf16[32,40,128]{2,1,0:T(8,128)(2,1)S(1)}, u32[]{:S(2)}, u32[]{:S(2)}) async-start(bf16[32,40,128]{2,1,0:T(8,128)(2,1)} %pad_maximum_fusion.2), calls=%async_computation | async-start | bytes 655360 | tf_op jit(solution)/shard_map/all_to_all | solution.py:77
  22.3 178.9 %all-gather.3.cloned.1.call-start = ((), (), s32[]{:S(2)}) async-start(), calls=%async_computation.3 | async-start | bytes 4325376 | tf_op jit(solution)/shard_map/all_gather | solution.py:82
  22.3 31.6 %collective-permute-start.9 = (bf16[64,512]{1,0:T(8,128)(2,1)}, bf16[64,512]{1,0:T(8,128)(2,1)S(1)}, u32[]{:S(2)}, u32[]{:S(2)}) collective-permute-start(bf16[64,512]{1,0:T(8,128)(2,1)} %bitcast.129), channel_id=1, source_target_pairs={{0,64},{64,0},{1,65},{65,1},{2,66},{66,2},{3,67},{67,3},{4,68},{68... | collective-permute-start | bytes 196616 | tf_op jit(solution)/shard_map/ppermute | solution.py:23
  48.5 11.3 %copy-start.4 = (bf16[144,512]{0,1:T(8,128)(2,1)}, bf16[144,512]{0,1:T(8,128)(2,1)S(1)}, u32[]{:S(2)}) copy-start(bf16[144,512]{0,1:T(8,128)(2,1)S(1)} %all_gather.12) | copy-start | bytes 442372
  49.0 10.8 %copy-start.2 = (bf16[32,40,128]{2,1,0:T(8,128)(2,1)}, bf16[32,40,128]{2,1,0:T(8,128)(2,1)S(1)}, u32[]{:S(2)}) copy-start(bf16[32,40,128]{2,1,0:T(8,128)(2,1)S(1)} %all-to-all-done) | copy-start | bytes 983044
  49.7 6.3 %collective-permute-start.10 = (bf16[32,2,512]{2,1,0:T(2,128)(2,1)S(1)}, bf16[32,2,512]{2,1,0:T(2,128)(2,1)S(1)}, u32[]{:S(2)}, u32[]{:S(2)}) collective-permute-start(bf16[32,2,512]{2,1,0:T(2,128)(2,1)S(1)} %select_n.249), channel_id=1, source_target_pairs={{0,4},{1,5},{2,6},{3,7},{4,0},{5,1},{6,2},{7,3},{8,12},{9,13},{10,... | collective-permute-start | bytes 196616 | tf_op jit(solution)/shard_map/ppermute | solution.py:14
  52.0 7.1 %collective-permute-start.11 = (bf16[32,2,512]{2,1,0:T(2,128)(2,1)S(1)}, bf16[32,2,512]{2,1,0:T(2,128)(2,1)S(1)}, u32[]{:S(2)}, u32[]{:S(2)}) collective-permute-start(bf16[32,2,512]{2,1,0:T(2,128)(2,1)S(1)} %select_n.249), channel_id=1, source_target_pairs={{0,68},{1,69},{2,70},{3,71},{4,64},{5,65},{6,66},{7,67},{64,4},{65... | collective-permute-start | bytes 196616 | tf_op jit(solution)/shard_map/ppermute | solution.py:19
  60.0 12.8 %copy-start.3 = (bf16[32,40,128]{2,1,0:T(8,128)(2,1)S(1)}, bf16[32,40,128]{2,1,0:T(8,128)(2,1)}, u32[]{:S(2)}) copy-start(bf16[32,40,128]{2,1,0:T(8,128)(2,1)} %copy-done.2) | copy-start | bytes 983044
  61.3 17.5 %copy-start.5 = (bf16[144,512]{0,1:T(8,128)(2,1)S(1)}, bf16[144,512]{0,1:T(8,128)(2,1)}, u32[]{:S(2)}) copy-start(bf16[144,512]{0,1:T(8,128)(2,1)} %copy-done.4) | copy-start | bytes 442372
  63.3 37.9 %all-to-all-start.1 = ((bf16[32,128,128]{2,1,0:T(8,128)(2,1)}), bf16[32,128,128]{2,1,0:T(8,128)(2,1)S(1)}, u32[]{:S(2)}, u32[]{:S(2)}) async-start(bf16[32,128,128]{2,1,0:T(8,128)(2,1)} %maximum_select_fusion), calls=%async_computation.1 | async-start | bytes 2097152 | tf_op jit(solution)/shard_map/all_to_all | solution.py:77
  72.8 12.2 %collective-permute-start = (bf16[32,8,128]{2,1,0:T(8,128)(2,1)S(1)}, bf16[32,8,128]{2,1,0:T(8,128)(2,1)S(1)}, u32[]{:S(2)}, u32[]{:S(2)}) collective-permute-start(bf16[32,8,128]{2,1,0:T(8,128)(2,1)S(1)} %constant_dynamic-slice_fusion.2), channel_id=1, source_target_pairs={{0,64},{64,0},{1,65},{65,1},{2,66},{66,2},{3,67},{67,3},{4,68},{68... | collective-permute-start | bytes 196616 | tf_op jit(solution)/shard_map/ppermute | solution.py:23
  79.6 32.8 %collective-permute-start.4 = (bf16[32,16,128]{2,1,0:T(8,128)(2,1)S(1)}, bf16[32,16,128]{2,1,0:T(8,128)(2,1)S(1)}, u32[]{:S(2)}, u32[]{:S(2)}) collective-permute-start(bf16[32,16,128]{2,1,0:T(8,128)(2,1)S(1)} %get-tuple-element.31), channel_id=1, source_target_pairs={{0,68},{1,69},{2,70},{3,71},{4,64},{5,65},{6,66},{7,67},{64,4},{65... | collective-permute-start | bytes 393224 | tf_op jit(solution)/shard_map/ppermute | solution.py:19
  82.8 29.7 %collective-permute-start.3 = (bf16[32,16,128]{2,1,0:T(8,128)(2,1)S(1)}, bf16[32,16,128]{2,1,0:T(8,128)(2,1)S(1)}, u32[]{:S(2)}, u32[]{:S(2)}) collective-permute-start(bf16[32,16,128]{2,1,0:T(8,128)(2,1)S(1)} %get-tuple-element.30), channel_id=1, source_target_pairs={{0,4},{1,5},{2,6},{3,7},{4,0},{5,1},{6,2},{7,3},{8,12},{9,13},{10,... | collective-permute-start | bytes 393224 | tf_op jit(solution)/shard_map/ppermute | solution.py:14
  103.6 50.7 %all-to-all-start.2 = ((bf16[32,128,128]{2,1,0:T(8,128)(2,1)}), bf16[32,128,128]{2,1,0:T(8,128)(2,1)S(1)}, u32[]{:S(2)}, u32[]{:S(2)}) async-start(bf16[32,128,128]{2,1,0:T(8,128)(2,1)} %maximum_select_fusion.1), calls=%async_computation.2 | async-start | bytes 2097152 | tf_op jit(solution)/shard_map/all_to_all | solution.py:77
  112.6 33.8 %collective-permute-start.6 = (bf16[32,64,128]{2,1,0:T(8,128)(2,1)S(1)}, bf16[32,64,128]{2,1,0:T(8,128)(2,1)S(1)}, u32[]{:S(2)}, u32[]{:S(2)}) collective-permute-start(bf16[32,64,128]{2,1,0:T(8,128)(2,1)S(1)} %get-tuple-element.23), channel_id=1, source_target_pairs={{0,68},{1,69},{2,70},{3,71},{4,64},{5,65},{6,66},{7,67},{64,4},{65... | collective-permute-start | bytes 1572872 | tf_op jit(solution)/shard_map/ppermute | solution.py:19
  114.6 12.5 %collective-permute-start.1 = (bf16[32,32,128]{2,1,0:T(8,128)(2,1)S(1)}, bf16[32,32,128]{2,1,0:T(8,128)(2,1)S(1)}, u32[]{:S(2)}, u32[]{:S(2)}) collective-permute-start(bf16[32,32,128]{2,1,0:T(8,128)(2,1)S(1)} %constant_dynamic-slice_fusion.1), channel_id=1, source_target_pairs={{0,64},{64,0},{1,65},{65,1},{2,66},{66,2},{3,67},{67,3},{4,68},{68... | collective-permute-start | bytes 786440 | tf_op jit(solution)/shard_map/ppermute | solution.py:23
  120.9 33.0 %collective-permute-start.5 = (bf16[32,64,128]{2,1,0:T(8,128)(2,1)S(1)}, bf16[32,64,128]{2,1,0:T(8,128)(2,1)S(1)}, u32[]{:S(2)}, u32[]{:S(2)}) collective-permute-start(bf16[32,64,128]{2,1,0:T(8,128)(2,1)S(1)} %get-tuple-element.22), channel_id=1, source_target_pairs={{0,4},{1,5},{2,6},{3,7},{4,0},{5,1},{6,2},{7,3},{8,12},{9,13},{10,... | collective-permute-start | bytes 1572872 | tf_op jit(solution)/shard_map/ppermute | solution.py:14
  124.1 29.9 %copy-start.13 = (bf16[4,2,8,16,128]{4,2,1,0,3:T(8,128)(2,1)}, bf16[4,2,8,16,128]{4,2,1,0,3:T(8,128)(2,1)S(1)}, u32[]{:S(2)}) copy-start(bf16[4,2,8,16,128]{4,2,1,0,3:T(8,128)(2,1)S(1)} %copy_dynamic-update-slice_fusion.4) | copy-start | bytes 786436
  154.4 39.9 %collective-permute-start.8 = (bf16[32,64,128]{2,1,0:T(8,128)(2,1)S(1)}, bf16[32,64,128]{2,1,0:T(8,128)(2,1)S(1)}, u32[]{:S(2)}, u32[]{:S(2)}) collective-permute-start(bf16[32,64,128]{2,1,0:T(8,128)(2,1)S(1)} %get-tuple-element.25), channel_id=1, source_target_pairs={{0,68},{1,69},{2,70},{3,71},{4,64},{5,65},{6,66},{7,67},{64,4},{65... | collective-permute-start | bytes 1572872 | tf_op jit(solution)/shard_map/ppermute | solution.py:19
  160.4 11.2 %collective-permute-start.2 = (bf16[32,32,128]{2,1,0:T(8,128)(2,1)S(1)}, bf16[32,32,128]{2,1,0:T(8,128)(2,1)S(1)}, u32[]{:S(2)}, u32[]{:S(2)}) collective-permute-start(bf16[32,32,128]{2,1,0:T(8,128)(2,1)S(1)} %constant_dynamic-slice_fusion), channel_id=1, source_target_pairs={{0,64},{64,0},{1,65},{65,1},{2,66},{66,2},{3,67},{67,3},{4,68},{68... | collective-permute-start | bytes 786440 | tf_op jit(solution)/shard_map/ppermute | solution.py:23
  165.3 32.3 %collective-permute-start.7 = (bf16[32,64,128]{2,1,0:T(8,128)(2,1)S(1)}, bf16[32,64,128]{2,1,0:T(8,128)(2,1)S(1)}, u32[]{:S(2)}, u32[]{:S(2)}) collective-permute-start(bf16[32,64,128]{2,1,0:T(8,128)(2,1)S(1)} %get-tuple-element.24), channel_id=1, source_target_pairs={{0,4},{1,5},{2,6},{3,7},{4,0},{5,1},{6,2},{7,3},{8,12},{9,13},{10,... | collective-permute-start | bytes 1572872 | tf_op jit(solution)/shard_map/ppermute | solution.py:14
  167.9 29.8 %copy-start.6 = (bf16[4,2,8,64,128]{4,2,1,0,3:T(8,128)(2,1)}, bf16[4,2,8,64,128]{4,2,1,0,3:T(8,128)(2,1)S(1)}, u32[]{:S(2)}) copy-start(bf16[4,2,8,64,128]{4,2,1,0,3:T(8,128)(2,1)S(1)} %copy_dynamic-update-slice_fusion.2) | copy-start | bytes 3145732
  172.4 27.1 %copy-start.11 = (bf16[32,2,32,128]{3,1,0,2:T(2,128)(2,1)S(1)}, bf16[32,2,32,128]{3,1,0,2:T(2,128)(2,1)}, u32[]{:S(2)}) copy-start(bf16[32,2,32,128]{3,1,0,2:T(2,128)(2,1)} %copy.63) | copy-start | bytes 1572868
  198.5 1.0 copy-start.8
  201.1 22.5 %copy-start.17 = (f32[512]{0:T(512)S(1)}, f32[512]{0:T(512)}, u32[]{:S(2)}) copy-start(f32[512]{0:T(512)} %param.6) | copy-start | bytes 6148
  204.2 20.3 %copy-start.10 = (bf16[144,512]{1,0:T(8,128)(2,1)S(1)}, bf16[144,512]{1,0:T(8,128)(2,1)}, u32[]{:S(2)}) copy-start(bf16[144,512]{1,0:T(8,128)(2,1)} %copy.73) | copy-start | bytes 442372
  230.7 1.2 copy-start.7
  230.8 1.5 copy-start.9
  230.8 1.6 copy-start.14
Sparse Core Ops, SparseCore 0:
  60.0 100.6 all-gather.2

commit v3 on v1

v3 whole, which is shorter than its diff:
```python
import jax
import jax.numpy as jnp
from jax import lax
from jax.sharding import Mesh, PartitionSpec as P

X, ZH, Y = 4, 2, 8
XY = X * Y
FIRST = 80
BF = jnp.bfloat16
F32 = jnp.float32


def swap_block(v):
    return lax.ppermute(v, "nw", [(i, i ^ 4) for i in range(8)])


def cross_block(v):
    pairs = [(a * 8 + b, (a ^ 1) * 8 + (b ^ 4)) for a in range(ZH) for b in range(8)]
    return lax.ppermute(v, ("zh", "nw"), pairs)


def cross_same(v):
    return lax.ppermute(v, "zh", [(0, 1), (1, 0)])


def in_order(own, other, zh):
    first = zh == 0
    return jnp.stack([jnp.where(first, own, other), jnp.where(first, other, own)], 0)


def copies_to_all(v, axis):
    sent = jnp.broadcast_to(v[None], (lax.axis_size(axis),) + v.shape)
    return lax.all_to_all(sent, axis, 0, 0, tiled=True)


def along_xy(v):
    return lax.all_to_all(v, ("x", "y"), 0, 0, tiled=True)


def after(v, others, zh):
    for other in others:
        v = jnp.where(zh > 1, other[(0,) * other.ndim].astype(v.dtype), v)
    return v


def folded_weights(w, turned, zh):
    units = w.shape[-1]
    raw_other = cross_same(w)
    near = swap_block(turned)
    far = cross_block(turned)
    theirs = in_order(near, far, zh).transpose(2, 0, 1, 3)
    mine = in_order(w, raw_other, zh).reshape(ZH, X, ZH, Y, units)
    mine = mine.transpose(0, 2, 1, 3, 4).reshape(ZH, ZH, XY, units)
    fold = (mine.astype(F32) + theirs.astype(F32)).astype(BF)
    return fold.reshape(ZH * 64, units)


def body(pooled, w_top, bias, grad_hidden):
    zh = lax.axis_index("zh")
    nw = lax.axis_index("nw")
    half = nw // 4
    count = pooled.shape[0] // (XY * ZH)
    width = pooled.shape[-1]
    units = w_top.shape[-1]
    scale = width ** (-0.5)
    n = FIRST
    rest = count - n

    def my_half(v):
        h = v.shape[1] // 2
        return lax.dynamic_slice_in_dim(v, half * h, h, 1)

    by_dest = pooled.reshape(X, ZH, Y, count, width).transpose(1, 0, 2, 3, 4)
    by_dest = by_dest.reshape(ZH, XY, count, width)
    mine = lax.dynamic_index_in_dim(by_dest, zh, 0, keepdims=False)
    theirs = lax.dynamic_index_in_dim(by_dest, 1 - zh, 0, keepdims=False)

    def move_z(own, away):
        x_away, y_own, y_away = cross_same(my_half(away)), swap_block(own), cross_block(away)
        return my_half(own), x_away, y_own, y_away

    moved_1 = move_z(mine[:, n:], theirs[:, n:])

    w = w_top[0]
    w_rows = w.reshape(X, ZH, Y, units).transpose(0, 2, 1, 3).reshape(XY, -1, width)
    turned = along_xy(w_rows)
    turned_after = after(turned, [moved_1[1]], zh).reshape(XY, ZH, units)
    fold = folded_weights(w, turned_after, zh)
    weights = lax.all_gather(fold, ("x", "y"), axis=0, tiled=True)

    first = jnp.concatenate([mine[:, :n], theirs[:, :n]], 1)
    got = along_xy(after(first, [turned], zh))
    moved_0 = move_z(got[:, :n], got[:, n:])
    last = along_xy(after(jnp.concatenate(moved_1, 1), [got], zh))
    h = rest // 2
    moved_1 = last[:, :h], last[:, h:rest], last[:, rest : 2 * rest], last[:, 2 * rest :]

    cot = copies_to_all(after(grad_hidden, [last], zh), "nw").transpose(1, 0, 2).reshape(count, units)

    def rows_of(own, other):
        v = in_order(own, other, zh).transpose(1, 0, 2, 3)
        return v.reshape(XY * ZH, v.shape[2], width).transpose(1, 0, 2)

    def columns_of(own, other):
        v = in_order(own, other, zh)
        return v.reshape(ZH * XY, v.shape[2], width).transpose(1, 0, 2)

    moved = moved_0, moved_1
    left = jnp.concatenate([rows_of(v[0], v[1]) for v in moved], 0)
    right = [columns_of(v[2], v[3]) for v in moved]
    sizes = [v.shape[0] // 2 for v in right]
    right_half = [lax.dynamic_slice_in_dim(v, half * h, h, 0) for v, h in zip(right, sizes)]
    right, right_half = jnp.concatenate(right, 0), jnp.concatenate(right_half, 0)

    hc = count // 2
    gram = jnp.einsum("sie,sje->sij", left, right_half, preferred_element_type=F32)
    gram = (gram * scale).astype(BF).reshape(hc, 64 * 64)
    part = jnp.dot(gram, weights, preferred_element_type=F32)
    parts = lax.all_gather(part.astype(BF), "nw", axis=0, tiled=False)
    sums = parts.reshape(2, 4, hc, units).astype(F32).sum(1)
    ordered, at = [], 0
    for h in sizes:
        ordered += [sums[0, at : at + h], sums[1, at : at + h]]
        at += h
    pre_act = jnp.concatenate(ordered, 0) + bias[None, :]

    share = grad_hidden.shape[1]
    mine_pre = lax.dynamic_slice_in_dim(pre_act, nw * share, share, 1)
    hidden = jax.nn.silu(mine_pre).astype(BF)
    sig = jax.nn.sigmoid(pre_act)
    grad_pre = (cot.astype(F32) * (sig * (1.0 + pre_act * (1.0 - sig)))).astype(BF)

    rows = lax.dot_general(
        grad_pre, weights, (((1,), (1,)), ((), ())), preferred_element_type=F32
    )
    rows = rows.astype(BF).reshape(count, X, Y, ZH, 64).transpose(0, 1, 3, 2, 4)
    rows = rows.reshape(count, 64, 64)
    grad_pooled = jnp.einsum("sij,sje->sie", rows, right, preferred_element_type=F32)
    return hidden, (grad_pooled * scale).astype(BF)[:, None]


def solution(mesh):
    fine = Mesh(mesh.devices.reshape(X, ZH, Y, 8), ("x", "zh", "y", "nw"))
    wide = ("x", "zh", "y")
    in_specs = (P(None, "nw", wide, None), P("nw", wide, None), P(), P(wide, "nw"))
    out_specs = (P(wide, "nw"), P(wide, "nw", None, None))
    return jax.shard_map(body, mesh=fine, in_specs=in_specs, out_specs=out_specs, check_vma=False)
```

time: 259 us -> 219 us (0.85)
  blocking collectives: 97.6 us -> 16.3 us
  starting transfers between devices: 51.3 us -> 66.9 us
  local copies, waits for them, and re-layouts: 14 us -> 23.8 us
  waiting for transfers between devices: 64.5 us -> 73.2 us
  other arithmetic: 5.17 us -> 12.2 us
    all_gather x2 -> x1, blocking collectives: 97.6 us -> 16.3 us  [body(): parts = lax.all_gather(part.astype(BF), 'nw', axis=0, tiled=False)]
    all_gather x2 -> x1, waiting for transfers between devices: 38.6 us -> 0.01 us  [body(): weights = lax.all_gather(fold, ('x', 'y'), axis=0, tiled=True)]
    ppermute x2 -> x3, waiting for transfers between devices: 0.01 us -> 33.3 us  [swap_block(): return lax.ppermute(v, 'nw', [(i, i ^ 4) for i in range(8)])]
    all_to_all x2 -> x4, starting transfers between devices: 18.2 us -> 27.6 us  [the longest x3 23.4 us: along_xy(): return lax.all_to_all(v, ('x', 'y'), 0, 0, tiled=True)]
    all_to_all x2 -> x4, waiting for transfers between devices: 25 us -> 32.2 us  [the longest x3 26.3 us: along_xy(): return lax.all_to_all(v, ('x', 'y'), 0, 0, tiled=True)]
    select_n x1 -> x4, other arithmetic: 0.16 us -> 6.58 us  [after(): v = jnp.where(zh > 1, other[(0,) * other.ndim].astype(v.dtype), v)]
    ppermute x2 -> x3, waiting for transfers between devices: 0.87 us -> 4.36 us  [cross_block(): return lax.ppermute(v, ('zh', 'nw'), pairs)]
    ppermute x2 -> x3, waiting for transfers between devices: 0.01 us -> 3.24 us  [cross_same(): return lax.ppermute(v, 'zh', [(0, 1), (1, 0)])]
  transfers between devices with their start and end apart: 10 -> 14, of which waited for: 3 -> 6; matrix products, arithmetic and copies ran while one was open for 5% -> 12% of each run, Pallas kernels for 0% -> 0%
where the time goes in v3:
time: 219 us; the launch traced here: 218 us
  waiting for transfers between devices  73.2 us (33%)
  starting transfers between devices  66.9 us (31%)
  local copies, waits for them, and re-layouts  23.8 us (11%)
  blocking collectives  16.3 us (7%)
  between operations  14.6 us (7%)
  other arithmetic  12.2 us (6%)
  matrix products  10.7 us (5%)
    ppermute x3, waiting for transfers between devices, swap_block(): return lax.ppermute(v, 'nw', [(i, i ^ 4) for i in range(8)])  33.3 us
    all_to_all x3, waiting for transfers between devices, along_xy(): return lax.all_to_all(v, ('x', 'y'), 0, 0, tiled=True)  26.3 us
    all_to_all x3, starting transfers between devices, along_xy(): return lax.all_to_all(v, ('x', 'y'), 0, 0, tiled=True)  23.4 us
    ppermute x3, starting transfers between devices, cross_same(): return lax.ppermute(v, 'zh', [(0, 1), (1, 0)])  19.9 us
    all_gather x1, blocking collectives, body(): parts = lax.all_gather(part.astype(BF), 'nw', axis=0, tiled=False)  16.3 us
    ppermute x3, starting transfers between devices, cross_block(): return lax.ppermute(v, ('zh', 'nw'), pairs)  10.5 us
    ppermute x3, starting transfers between devices, swap_block(): return lax.ppermute(v, 'nw', [(i, i ^ 4) for i in range(8)])  8.86 us
    select_n x4, other arithmetic, after(): v = jnp.where(zh > 1, other[(0,) * other.ndim].astype(v.dtype), v)  6.58 us
  transfers between devices with their start and end apart: 14, of which 6 were waited for; matrix products, arithmetic and copies ran while one was open for 12% of the time, Pallas kernels for 0%

profile of v3, /device:TPU:1, one launch (start us, length us, event | category | flops | bytes accessed | tf_op | source)
XLA Modules:
  0.0 217.6 jit_solution(6171811070693157532)
XLA Ops:
  7.2 1.8 copy.65
  9.2 1.0 copy-done.2
  10.4 11.6 %collective-permute-start.1 = (bf16[32,32,128]{2,1,0:T(8,128)(2,1)S(1)}, bf16[32,32,128]{2,1,0:T(8,128)(2,1)S(1)}, u32[]{:S(2)}, u32[]{:S(2)}) collective-permute-start(bf16[32,32,128]{2,1,0:T(8,128)(2,1)S(1)} %constant_dynamic-slice_fusion), channel_id=1, source_target_pairs={{0,64},{64,0},{1,65},{65,1},{2,66},{66,2},{3,67},{67,3},{4,68},{68... | collective-permute-start | bytes 786440 | tf_op jit(solution)/shard_map/ppermute | solution.py:23
  22.0 0.9 copy.83
  23.5 9.7 %all-to-all-start = ((bf16[32,8,128]{2,1,0:T(8,128)(2,1)}), bf16[32,8,128]{2,1,0:T(8,128)(2,1)S(1)}, u32[]{:S(2)}, u32[]{:S(2)}) async-start(bf16[32,8,128]{2,1,0:T(8,128)(2,1)} %reshape.56), calls=%async_computation | async-start | bytes 131072 | tf_op jit(solution)/shard_map/all_to_all | solution.py:37
  33.2 1.9 collective-permute-start.6
  35.8 6.3 %all-to-all-done = bf16[32,8,128]{2,1,0:T(8,128)(2,1)S(1)} async-done(((bf16[32,8,128]{2,1,0:T(8,128)(2,1)}), bf16[32,8,128]{2,1,0:T(8,128)(2,1)S(1)}, u32[]{:S(2)}, u32[]{:S(2)}) %all-to-all-start) | async-done | bytes 65568 | tf_op jit(solution)/shard_map/all_to_all | solution.py:37
  42.8 4.0 %collective-permute-start.7 = (bf16[32,2,512]{2,0,1:T(8,128)(2,1)S(1)}, bf16[32,2,512]{2,0,1:T(8,128)(2,1)S(1)}, u32[]{:S(2)}, u32[]{:S(2)}) collective-permute-start(bf16[32,2,512]{2,0,1:T(8,128)(2,1)S(1)} %copy.71), channel_id=1, source_target_pairs={{0,4},{1,5},{2,6},{3,7},{4,0},{5,1},{6,2},{7,3},{8,12},{9,13},{10,... | collective-permute-start | bytes 196616 | tf_op jit(solution)/shard_map/ppermute | solution.py:14
  46.8 1.9 collective-permute-start.8
  48.7 0.9 broadcast_select_fusion.2
  49.6 4.4 %collective-permute-done.8 = bf16[32,2,512]{2,0,1:T(8,128)(2,1)S(1)} collective-permute-done((bf16[32,2,512]{2,0,1:T(8,128)(2,1)S(1)}, bf16[32,2,512]{2,0,1:T(8,128)(2,1)S(1)}, u32[]{:S(2)}, u32[]{:S(2)}) %collective-permute-start.8) | collective-permute-done | bytes 65568 | tf_op jit(solution)/shard_map/ppermute | solution.py:19
  54.0 0.7 fusion.13
  55.4 2.0 maximum_select_fusion.1
  57.3 4.1 %all-to-all-start.1 = ((bf16[32,160,128]{2,1,0:T(8,128)(2,1)}), bf16[32,160,128]{2,1,0:T(8,128)(2,1)S(1)}, u32[]{:S(2)}, u32[]{:S(2)}) async-start(bf16[32,160,128]{2,1,0:T(8,128)(2,1)} %maximum_select_fusion.1), calls=%async_computation.1 | async-start | bytes 2621440 | tf_op jit(solution)/shard_map/all_to_all | solution.py:37
  61.4 1.1 slice.78
  62.5 2.9 %collective-permute-start.2 = (bf16[32,64,128]{2,1,0:T(8,128)(2,1)S(1)}, bf16[32,64,128]{2,1,0:T(8,128)(2,1)S(1)}, u32[]{:S(2)}, u32[]{:S(2)}) collective-permute-start(bf16[32,64,128]{2,1,0:T(8,128)(2,1)S(1)} %slice.78), channel_id=1, source_target_pairs={{0,4},{1,5},{2,6},{3,7},{4,0},{5,1},{6,2},{7,3},{8,12},{9,13},{10,... | collective-permute-start | bytes 1572872 | tf_op jit(solution)/shard_map/ppermute | solution.py:14
  65.4 5.5 %collective-permute-start.3 = (bf16[32,64,128]{2,1,0:T(8,128)(2,1)S(1)}, bf16[32,64,128]{2,1,0:T(8,128)(2,1)}, u32[]{:S(2)}, u32[]{:S(2)}) collective-permute-start(bf16[32,64,128]{2,1,0:T(8,128)(2,1)S(1)} %copy-done.8), channel_id=1, source_target_pairs={{0,68},{1,69},{2,70},{3,71},{4,64},{5,65},{6,66},{7,67},{64,4},{65... | collective-permute-start | bytes 1572872 | tf_op jit(solution)/shard_map/ppermute | solution.py:19
  71.0 20.0 %all-to-all-done.1 = bf16[32,160,128]{2,1,0:T(8,128)(2,1)S(1)} async-done(((bf16[32,160,128]{2,1,0:T(8,128)(2,1)}), bf16[32,160,128]{2,1,0:T(8,128)(2,1)S(1)}, u32[]{:S(2)}, u32[]{:S(2)}) %all-to-all-start.1) | async-done | bytes 1310752 | tf_op jit(solution)/shard_map/all_to_all | solution.py:37
  91.6 3.3 %maximum_select_fusion = bf16[32,192,128]{2,1,0:T(8,128)(2,1)} fusion(bf16[32,64,128]{2,1,0:T(8,128)(2,1)} %collective-permute-done.3, bf16[32,64,128]{2,1,0:T(8,128)(2,1)S(1)} %collective-permute-done.2, bf16[32,32,128]{2,1,0:T(8,128)(2,1)S(1)} %copy-done.12, bf16[32,32,128]{2,1,0:T(8,128)(2,1)S(1)} %constant_dynamic-slice_fusion.1, pred[]{:T(512)S(6)} %gt.2, ...), kind=kLoop, calls=%fused_computation.8 | loop fusion | flops 7077888 | bytes 3145731 | tf_op jit(solution)/shard_map/jit(_where)/select_n | solution.py:42
  94.8 9.6 %all-to-all-start.2 = ((bf16[32,192,128]{2,1,0:T(8,128)(2,1)}), bf16[32,192,128]{2,1,0:T(8,128)(2,1)S(1)}, u32[]{:S(2)}, u32[]{:S(2)}) async-start(bf16[32,192,128]{2,1,0:T(8,128)(2,1)} %maximum_select_fusion), calls=%async_computation.2 | async-start | bytes 3145728 | tf_op jit(solution)/shard_map/all_to_all | solution.py:37
  104.5 0.9 fusion.18
  105.5 6.4 %collective-permute-start = (bf16[32,40,128]{2,1,0:T(8,128)(2,1)S(1)}, bf16[32,40,128]{2,1,0:T(8,128)(2,1)}, u32[]{:S(2)}, u32[]{:S(2)}) collective-permute-start(bf16[32,40,128]{2,1,0:T(8,128)(2,1)S(1)} %constant_dynamic-slice_fusion.2), channel_id=1, source_target_pairs={{0,64},{64,0},{1,65},{65,1},{2,66},{66,2},{3,67},{67,3},{4,68},{68... | collective-permute-start | bytes 983048 | tf_op jit(solution)/shard_map/ppermute | solution.py:23
  111.8 2.0 collective-permute-start.4
  113.8 3.1 %collective-permute-start.5 = (bf16[32,80,128]{2,1,0:T(8,128)(2,1)S(1)}, bf16[32,80,128]{2,1,0:T(8,128)(2,1)}, u32[]{:S(2)}, u32[]{:S(2)}) collective-permute-start(bf16[32,80,128]{2,1,0:T(8,128)(2,1)S(1)} %get-tuple-element.23), channel_id=1, source_target_pairs={{0,68},{1,69},{2,70},{3,71},{4,64},{5,65},{6,66},{7,67},{64,4},{65... | collective-permute-start | bytes 1966088 | tf_op jit(solution)/shard_map/ppermute | solution.py:19
  116.9 3.2 %collective-permute-done = bf16[32,40,128]{2,1,0:T(8,128)(2,1)} collective-permute-done((bf16[32,40,128]{2,1,0:T(8,128)(2,1)S(1)}, bf16[32,40,128]{2,1,0:T(8,128)(2,1)}, u32[]{:S(2)}, u32[]{:S(2)}) %collective-permute-start) | collective-permute-done | bytes 327712 | tf_op jit(solution)/shard_map/ppermute | solution.py:23
  120.1 1.2 select_bitcast_fusion.5
  121.4 1.5 copy.66
  122.9 33.3 %collective-permute-done.4 = bf16[32,80,128]{2,1,0:T(8,128)(2,1)S(1)} collective-permute-done((bf16[32,80,128]{2,1,0:T(8,128)(2,1)}, bf16[32,80,128]{2,1,0:T(8,128)(2,1)S(1)}, u32[]{:S(2)}, u32[]{:S(2)}) %collective-permute-start.4) | collective-permute-done | bytes 655392 | tf_op jit(solution)/shard_map/ppermute | solution.py:14
  156.2 1.2 select_bitcast_fusion.1
  157.6 1.4 copy.68
  159.0 2.0 dynamic-slice_bitcast_fusion.2
  161.2 0.7 copy.69
  162.0 1.3 copy.67
  163.9 0.7 broadcast_select_fusion.3
  164.6 0.7 broadcast_in_dim.30
  165.3 4.2 %all-to-all-start.3 = ((bf16[8,144,64]{1,2,0:T(8,128)(2,1)}), bf16[8,144,64]{1,2,0:T(8,128)(2,1)S(1)}, u32[]{:S(2)}, u32[]{:S(2)}) async-start(bf16[8,144,64]{1,2,0:T(8,128)(2,1)} %broadcast_in_dim.30), calls=%async_computation.3 | async-start | bytes 524288 | tf_op jit(solution)/shard_map/all_to_all | solution.py:33
  169.5 1.8 multiply_convert_fusion.1
  171.4 0.9 reshape.63
  172.3 5.9 %all-to-all-done.3 = bf16[8,144,64]{1,2,0:T(8,128)(2,1)S(1)} async-done(((bf16[8,144,64]{1,2,0:T(8,128)(2,1)}), bf16[8,144,64]{1,2,0:T(8,128)(2,1)S(1)}, u32[]{:S(2)}, u32[]{:S(2)}) %all-to-all-start.3) | async-done | bytes 147488 | tf_op jit(solution)/shard_map/all_to_all | solution.py:33
  178.4 3.2 %convolution_convert_fusion.1 = bf16[72,512]{1,0:T(8,128)(2,1)S(1)} fusion(bf16[72,4096]{1,0:T(8,128)(2,1)S(1)} %reshape.63, bf16[4096,512]{1,0:T(8,128)(2,1)} %all-gather.3.cloned.1.call-done), kind=kOutput, calls=%fused_computation.20 | convolution fusion | flops 302026752 | bytes 4857856 | tf_op jit(solution)/shard_map/dot_general | solution.py:118
  181.6 16.3 %all-gather = bf16[576,512]{1,0:T(8,128)(2,1)S(1)} all-gather(bf16[72,512]{1,0:T(8,128)(2,1)S(1)} %convolution_convert_fusion.1), channel_id=2, replica_groups=mesh['x'=4,'zh'=2,'y'=8,'nw'=8] {'nw'}, dimensions={0}, use_global_device_ids=true | all-gather | bytes 663552 | tf_op jit(solution)/shard_map/all_gather | solution.py:119
  198.1 0.7 copy-done.6
  198.8 1.5 convolution_convert_fusion
  200.3 2.6 %reshape.66 = bf16[144,4,8,2,64]{4,3,2,1,0:T(2,128)(2,1)S(1)} reshape(bf16[144,4096]{1,0:T(8,128)(2,1)S(1)} %convolution_convert_fusion) | data formatting | bytes 2359296 | tf_op jit(solution)/shard_map/reshape | solution.py:136
  202.9 2.0 copy.80
  204.8 1.0 multiply_convert_fusion.4
  205.8 0.7 copy.77
  206.5 4.2 %fusion = bf16[144,1,64,128]{3,2,1,0:T(8,128)(2,1)} fusion(bf16[144,64,64]{2,1,0:T(8,128)(2,1)} %bitcast.100, bf16[64,64,128]{2,1,0:T(8,128)(2,1)S(1)} %bitcast.103, bf16[80,64,128]{2,1,0:T(8,128)(2,1)} %bitcast.49), kind=kOutput, calls=%fused_computation.2 | convolution fusion | flops 154533888 | bytes 5898240 | tf_op jit(solution)/shard_map/sij,sje->sie/dot_general | solution.py:138
  (67 shorter events, 4.8 us)
Async XLA Ops:
  9.2 1.0 copy-start.2
  9.2 45.6 %copy-start.1 = (bf16[32,144,128]{2,1,0:T(8,128)(2,1)}, bf16[32,144,128]{2,1,0:T(8,128)(2,1)S(1)}, u32[]{:S(2)}) copy-start(bf16[32,144,128]{2,1,0:T(8,128)(2,1)S(1)} %get-tuple-element.14) | copy-start | bytes 3538948
  10.3 44.4 %copy-start.7 = (bf16[32,64,128]{2,1,0:T(8,128)(2,1)}, bf16[32,64,128]{2,1,0:T(8,128)(2,1)S(1)}, u32[]{:S(2)}) copy-start(bf16[32,64,128]{2,1,0:T(8,128)(2,1)S(1)} %slice.79) | copy-start | bytes 1572868
  10.3 44.4 %copy-start.3 = (bf16[32,144,128]{2,1,0:T(8,128)(2,1)S(1)}, bf16[32,144,128]{2,1,0:T(8,128)(2,1)}, u32[]{:S(2)}) copy-start(bf16[32,144,128]{2,1,0:T(8,128)(2,1)} %copy-done.2) | copy-start | bytes 3538948
  10.4 24.8 %collective-permute-start.1 = (bf16[32,32,128]{2,1,0:T(8,128)(2,1)S(1)}, bf16[32,32,128]{2,1,0:T(8,128)(2,1)S(1)}, u32[]{:S(2)}, u32[]{:S(2)}) collective-permute-start(bf16[32,32,128]{2,1,0:T(8,128)(2,1)S(1)} %constant_dynamic-slice_fusion), channel_id=1, source_target_pairs={{0,64},{64,0},{1,65},{65,1},{2,66},{66,2},{3,67},{67,3},{4,68},{68... | collective-permute-start | bytes 786440 | tf_op jit(solution)/shard_map/ppermute | solution.py:23
  23.5 18.5 %all-to-all-start = ((bf16[32,8,128]{2,1,0:T(8,128)(2,1)}), bf16[32,8,128]{2,1,0:T(8,128)(2,1)S(1)}, u32[]{:S(2)}, u32[]{:S(2)}) async-start(bf16[32,8,128]{2,1,0:T(8,128)(2,1)} %reshape.56), calls=%async_computation | async-start | bytes 131072 | tf_op jit(solution)/shard_map/all_to_all | solution.py:37
  33.2 145.2 %all-gather.3.cloned.1.call-start = ((), (), s32[]{:S(2)}) async-start(), calls=%async_computation.4 | async-start | bytes 4325376 | tf_op jit(solution)/shard_map/all_gather | solution.py:89
  33.2 15.5 %collective-permute-start.6 = (bf16[64,512]{1,0:T(8,128)(2,1)}, bf16[64,512]{1,0:T(8,128)(2,1)}, u32[]{:S(2)}, u32[]{:S(2)}) collective-permute-start(bf16[64,512]{1,0:T(8,128)(2,1)} %bitcast.27), channel_id=1, source_target_pairs={{0,64},{64,0},{1,65},{65,1},{2,66},{66,2},{3,67},{67,3},{4,68},{68... | collective-permute-start | bytes 196616 | tf_op jit(solution)/shard_map/ppermute | solution.py:23
  35.2 19.5 %copy-start.11 = (bf16[32,32,128]{2,1,0:T(8,128)(2,1)}, bf16[32,32,128]{2,1,0:T(8,128)(2,1)S(1)}, u32[]{:S(2)}) copy-start(bf16[32,32,128]{2,1,0:T(8,128)(2,1)S(1)} %collective-permute-done.1) | copy-start | bytes 786436
  42.8 6.9 %collective-permute-start.7 = (bf16[32,2,512]{2,0,1:T(8,128)(2,1)S(1)}, bf16[32,2,512]{2,0,1:T(8,128)(2,1)S(1)}, u32[]{:S(2)}, u32[]{:S(2)}) collective-permute-start(bf16[32,2,512]{2,0,1:T(8,128)(2,1)S(1)} %copy.71), channel_id=1, source_target_pairs={{0,4},{1,5},{2,6},{3,7},{4,0},{5,1},{6,2},{7,3},{8,12},{9,13},{10,... | collective-permute-start | bytes 196616 | tf_op jit(solution)/shard_map/ppermute | solution.py:14
  46.8 7.2 %collective-permute-start.8 = (bf16[32,2,512]{2,0,1:T(8,128)(2,1)S(1)}, bf16[32,2,512]{2,0,1:T(8,128)(2,1)S(1)}, u32[]{:S(2)}, u32[]{:S(2)}) collective-permute-start(bf16[32,2,512]{2,0,1:T(8,128)(2,1)S(1)} %copy.71), channel_id=1, source_target_pairs={{0,68},{1,69},{2,70},{3,71},{4,64},{5,65},{6,66},{7,67},{64,4},{65... | collective-permute-start | bytes 196616 | tf_op jit(solution)/shard_map/ppermute | solution.py:19
  57.3 8.1 %copy-start.8 = (bf16[32,64,128]{2,1,0:T(8,128)(2,1)S(1)}, bf16[32,64,128]{2,1,0:T(8,128)(2,1)}, u32[]{:S(2)}) copy-start(bf16[32,64,128]{2,1,0:T(8,128)(2,1)} %copy-done.7) | copy-start | bytes 1572868
  57.3 34.2 %copy-start.12 = (bf16[32,32,128]{2,1,0:T(8,128)(2,1)S(1)}, bf16[32,32,128]{2,1,0:T(8,128)(2,1)}, u32[]{:S(2)}) copy-start(bf16[32,32,128]{2,1,0:T(8,128)(2,1)} %copy-done.11) | copy-start | bytes 786436
  57.3 33.7 %all-to-all-start.1 = ((bf16[32,160,128]{2,1,0:T(8,128)(2,1)}), bf16[32,160,128]{2,1,0:T(8,128)(2,1)S(1)}, u32[]{:S(2)}, u32[]{:S(2)}) async-start(bf16[32,160,128]{2,1,0:T(8,128)(2,1)} %maximum_select_fusion.1), calls=%async_computation.1 | async-start | bytes 2621440 | tf_op jit(solution)/shard_map/all_to_all | solution.py:37
  62.5 29.1 %collective-permute-start.2 = (bf16[32,64,128]{2,1,0:T(8,128)(2,1)S(1)}, bf16[32,64,128]{2,1,0:T(8,128)(2,1)S(1)}, u32[]{:S(2)}, u32[]{:S(2)}) collective-permute-start(bf16[32,64,128]{2,1,0:T(8,128)(2,1)S(1)} %slice.78), channel_id=1, source_target_pairs={{0,4},{1,5},{2,6},{3,7},{4,0},{5,1},{6,2},{7,3},{8,12},{9,13},{10,... | collective-permute-start | bytes 1572872 | tf_op jit(solution)/shard_map/ppermute | solution.py:14
  65.4 26.1 %collective-permute-start.3 = (bf16[32,64,128]{2,1,0:T(8,128)(2,1)S(1)}, bf16[32,64,128]{2,1,0:T(8,128)(2,1)}, u32[]{:S(2)}, u32[]{:S(2)}) collective-permute-start(bf16[32,64,128]{2,1,0:T(8,128)(2,1)S(1)} %copy-done.8), channel_id=1, source_target_pairs={{0,68},{1,69},{2,70},{3,71},{4,64},{5,65},{6,66},{7,67},{64,4},{65... | collective-permute-start | bytes 1572872 | tf_op jit(solution)/shard_map/ppermute | solution.py:19
  94.8 66.1 %all-to-all-start.2 = ((bf16[32,192,128]{2,1,0:T(8,128)(2,1)}), bf16[32,192,128]{2,1,0:T(8,128)(2,1)S(1)}, u32[]{:S(2)}, u32[]{:S(2)}) async-start(bf16[32,192,128]{2,1,0:T(8,128)(2,1)} %maximum_select_fusion), calls=%async_computation.2 | async-start | bytes 3145728 | tf_op jit(solution)/shard_map/all_to_all | solution.py:37
  105.5 14.6 %collective-permute-start = (bf16[32,40,128]{2,1,0:T(8,128)(2,1)S(1)}, bf16[32,40,128]{2,1,0:T(8,128)(2,1)}, u32[]{:S(2)}, u32[]{:S(2)}) collective-permute-start(bf16[32,40,128]{2,1,0:T(8,128)(2,1)S(1)} %constant_dynamic-slice_fusion.2), channel_id=1, source_target_pairs={{0,64},{64,0},{1,65},{65,1},{2,66},{66,2},{3,67},{67,3},{4,68},{68... | collective-permute-start | bytes 983048 | tf_op jit(solution)/shard_map/ppermute | solution.py:23
  111.8 44.4 %collective-permute-start.4 = (bf16[32,80,128]{2,1,0:T(8,128)(2,1)}, bf16[32,80,128]{2,1,0:T(8,128)(2,1)S(1)}, u32[]{:S(2)}, u32[]{:S(2)}) collective-permute-start(bf16[32,80,128]{2,1,0:T(8,128)(2,1)} %get-tuple-element.22), channel_id=1, source_target_pairs={{0,4},{1,5},{2,6},{3,7},{4,0},{5,1},{6,2},{7,3},{8,12},{9,13},{10,... | collective-permute-start | bytes 1966088 | tf_op jit(solution)/shard_map/ppermute | solution.py:14
  113.8 42.4 %collective-permute-start.5 = (bf16[32,80,128]{2,1,0:T(8,128)(2,1)S(1)}, bf16[32,80,128]{2,1,0:T(8,128)(2,1)}, u32[]{:S(2)}, u32[]{:S(2)}) collective-permute-start(bf16[32,80,128]{2,1,0:T(8,128)(2,1)S(1)} %get-tuple-element.23), channel_id=1, source_target_pairs={{0,68},{1,69},{2,70},{3,71},{4,64},{5,65},{6,66},{7,67},{64,4},{65... | collective-permute-start | bytes 1966088 | tf_op jit(solution)/shard_map/ppermute | solution.py:19
  161.9 7.6 %copy-start.4 = (bf16[2,32,64,128]{3,1,0,2:T(8,128)(2,1)}, bf16[2,32,64,128]{3,1,0,2:T(8,128)(2,1)S(1)}, u32[]{:S(2)}) copy-start(bf16[2,32,64,128]{3,1,0,2:T(8,128)(2,1)S(1)} %copy.69) | copy-start | bytes 3145732
  161.9 2.0 copy-start.13
  162.0 7.5 %copy-start.9 = (bf16[32,2,40,128]{3,1,0,2:T(2,128)(2,1)S(1)}, bf16[32,2,40,128]{3,1,0,2:T(2,128)(2,1)}, u32[]{:S(2)}) copy-start(bf16[32,2,40,128]{3,1,0,2:T(2,128)(2,1)} %copy.66) | copy-start | bytes 1966084
  163.9 5.7 %copy-start.10 = (bf16[32,2,32,128]{3,1,0,2:T(2,128)(2,1)S(1)}, bf16[32,2,32,128]{3,1,0,2:T(2,128)(2,1)}, u32[]{:S(2)}) copy-start(bf16[32,2,32,128]{3,1,0,2:T(2,128)(2,1)} %copy.67) | copy-start | bytes 1572868
  165.3 12.9 %all-to-all-start.3 = ((bf16[8,144,64]{1,2,0:T(8,128)(2,1)}), bf16[8,144,64]{1,2,0:T(8,128)(2,1)S(1)}, u32[]{:S(2)}, u32[]{:S(2)}) async-start(bf16[8,144,64]{1,2,0:T(8,128)(2,1)} %broadcast_in_dim.30), calls=%async_computation.3 | async-start | bytes 524288 | tf_op jit(solution)/shard_map/all_to_all | solution.py:33
  178.4 20.4 %copy-start = (bf16[4096,512]{1,0:T(8,128)(2,1)S(1)}, bf16[4096,512]{1,0:T(8,128)(2,1)}, u32[]{:S(2)}) copy-start(bf16[4096,512]{1,0:T(8,128)(2,1)} %all-gather.3.cloned.1.call-done) | copy-start | bytes 12582916
  181.6 16.4 %copy-start.14 = (f32[512]{0:T(512)S(1)}, f32[512]{0:T(512)}, u32[]{:S(2)}) copy-start(f32[512]{0:T(512)} %param.6) | copy-start | bytes 6148
  198.0 0.7 copy-start.6
  202.9 3.7 %copy-start.5 = (bf16[2,32,64,128]{3,1,0,2:T(8,128)(2,1)S(1)}, bf16[2,32,64,128]{3,1,0,2:T(8,128)(2,1)}, u32[]{:S(2)}) copy-start(bf16[2,32,64,128]{3,1,0,2:T(8,128)(2,1)} %copy-done.4) | copy-start | bytes 3145732
Sparse Core Ops, SparseCore 0:
  54.9 106.8 all-gather.2

commit v4 on v3

--- a/solution.py
+++ b/solution.py
@@ -26,11 +26,6 @@
 def in_order(own, other, zh):
     first = zh == 0
     return jnp.stack([jnp.where(first, own, other), jnp.where(first, other, own)], 0)
-
-
-def copies_to_all(v, axis):
-    sent = jnp.broadcast_to(v[None], (lax.axis_size(axis),) + v.shape)
-    return lax.all_to_all(sent, axis, 0, 0, tiled=True)
 
 
 def along_xy(v):
@@ -82,10 +77,9 @@
     moved_1 = move_z(mine[:, n:], theirs[:, n:])
 
     w = w_top[0]
-    w_rows = w.reshape(X, ZH, Y, units).transpose(0, 2, 1, 3).reshape(XY, -1, width)
+    w_rows = w.reshape(X, ZH, Y, units).transpose(0, 2, 1, 3).reshape(XY, ZH, units)
     turned = along_xy(w_rows)
-    turned_after = after(turned, [moved_1[1]], zh).reshape(XY, ZH, units)
-    fold = folded_weights(w, turned_after, zh)
+    fold = folded_weights(w, turned, zh)
     weights = lax.all_gather(fold, ("x", "y"), axis=0, tiled=True)
 
     first = jnp.concatenate([mine[:, :n], theirs[:, :n]], 1)
@@ -94,8 +88,6 @@
     last = along_xy(after(jnp.concatenate(moved_1, 1), [got], zh))
     h = rest // 2
     moved_1 = last[:, :h], last[:, h:rest], last[:, rest : 2 * rest], last[:, 2 * rest :]
-
-    cot = copies_to_all(after(grad_hidden, [last], zh), "nw").transpose(1, 0, 2).reshape(count, units)
 
     def rows_of(own, other):
         v = in_order(own, other, zh).transpose(1, 0, 2, 3)
@@ -116,15 +108,18 @@
     gram = jnp.einsum("sie,sje->sij", left, right_half, preferred_element_type=F32)
     gram = (gram * scale).astype(BF).reshape(hc, 64 * 64)
     part = jnp.dot(gram, weights, preferred_element_type=F32)
-    parts = lax.all_gather(part.astype(BF), "nw", axis=0, tiled=False)
-    sums = parts.reshape(2, 4, hc, units).astype(F32).sum(1)
+    share = grad_hidden.shape[1]
+    cot = grad_hidden.reshape(2, hc, share).transpose(1, 0, 2).reshape(hc, 2 * share)
+    parts = lax.all_gather(jnp.concatenate([part.astype(BF), cot], 1), "nw", axis=0, tiled=False)
+    sums = parts[:, :, :units].reshape(2, 4, hc, units).astype(F32).sum(1)
+    cot = parts[:, :, units:].reshape(8, hc, 2, share).transpose(2, 1, 0, 3)
+    cot = cot.reshape(count, units)
     ordered, at = [], 0
     for h in sizes:
         ordered += [sums[0, at : at + h], sums[1, at : at + h]]
         at += h
     pre_act = jnp.concatenate(ordered, 0) + bias[None, :]
 
-    share = grad_hidden.shape[1]
     mine_pre = lax.dynamic_slice_in_dim(pre_act, nw * share, share, 1)
     hidden = jax.nn.silu(mine_pre).astype(BF)
     sig = jax.nn.sigmoid(pre_act)

time: 219 us -> 207 us (0.945)
  waiting for transfers between devices: 73.2 us -> 59 us
  starting transfers between devices: 66.9 us -> 71.6 us
  other arithmetic: 12.2 us -> 9.95 us
  blocking collectives: 16.3 us -> 18.5 us
    all_to_all x3, waiting for transfers between devices: 26.3 us -> 20.3 us  [along_xy(): return lax.all_to_all(v, ('x', 'y'), 0, 0, tiled=True)]
    all_to_all x1 -> x0, waiting for transfers between devices: 5.9 us -> none  [copies_to_all(): return lax.all_to_all(sent, axis, 0, 0, tiled=True)]
    ppermute x3, starting transfers between devices: 10.5 us -> 15.2 us  [cross_block(): return lax.ppermute(v, ('zh', 'nw'), pairs)]
    all_to_all x1 -> x0, starting transfers between devices: 4.17 us -> none  [copies_to_all(): return lax.all_to_all(sent, axis, 0, 0, tiled=True)]
    ppermute x3, waiting for transfers between devices: 3.24 us -> 7.17 us  [cross_same(): return lax.ppermute(v, 'zh', [(0, 1), (1, 0)])]
    all_to_all x3, starting transfers between devices: 23.4 us -> 27.2 us  [along_xy(): return lax.all_to_all(v, ('x', 'y'), 0, 0, tiled=True)]
    ppermute x3, waiting for transfers between devices: 4.36 us -> 0.87 us  [cross_block(): return lax.ppermute(v, ('zh', 'nw'), pairs)]
    unnamed x31 -> x17, local copies, waits for them, and re-layouts: 2.47 us -> 5.17 us
  transfers between devices with their start and end apart: 14 -> 13, of which waited for: 6 -> 4; matrix products, arithmetic and copies ran while one was open for 12% -> 11% of each run, Pallas kernels for 0% -> 0%
where the time goes in v4:
time: 207 us; the launch traced here: 206 us
  starting transfers between devices  71.6 us (35%)
  waiting for transfers between devices  59 us (29%)
  local copies, waits for them, and re-layouts  22.5 us (11%)
  blocking collectives  18.5 us (9%)
  between operations  14.6 us (7%)
  other arithmetic  9.95 us (5%)
  matrix products  9.65 us (5%)
    ppermute x3, waiting for transfers between devices, swap_block(): return lax.ppermute(v, 'nw', [(i, i ^ 4) for i in range(8)])  30.6 us
    all_to_all x3, starting transfers between devices, along_xy(): return lax.all_to_all(v, ('x', 'y'), 0, 0, tiled=True)  27.2 us
    all_to_all x3, waiting for transfers between devices, along_xy(): return lax.all_to_all(v, ('x', 'y'), 0, 0, tiled=True)  20.3 us
    ppermute x3, starting transfers between devices, cross_same(): return lax.ppermute(v, 'zh', [(0, 1), (1, 0)])  19.4 us
    all_gather x1, blocking collectives, body(): lax.all_gather(jnp.concatenate([part.astype(BF), cot], 1), 'nw', axis=0,...  18.5 us
    ppermute x3, starting transfers between devices, cross_block(): return lax.ppermute(v, ('zh', 'nw'), pairs)  15.2 us
    ppermute x3, starting transfers between devices, swap_block(): return lax.ppermute(v, 'nw', [(i, i ^ 4) for i in range(8)])  9.71 us
    ppermute x3, waiting for transfers between devices, cross_same(): return lax.ppermute(v, 'zh', [(0, 1), (1, 0)])  7.17 us
  transfers between devices with their start and end apart: 13, of which 4 were waited for; matrix products, arithmetic and copies ran while one was open for 11% of the time, Pallas kernels for 0%

profile of v4, /device:TPU:1, one launch (start us, length us, event | category | flops | bytes accessed | tf_op | source)
XLA Modules:
  0.0 205.7 jit_solution(10757578596523211067)
XLA Ops:
  7.2 0.8 copy.59
  8.0 0.7 copy.40
  8.7 10.5 %all-to-all-start = ((bf16[32,2,512]{2,1,0:T(2,128)(2,1)}), bf16[32,2,512]{2,1,0:T(2,128)(2,1)S(1)}, u32[]{:S(2)}, u32[]{:S(2)}) async-start(bf16[32,2,512]{2,1,0:T(2,128)(2,1)} %copy.40), calls=%async_computation | async-start | bytes 131072 | tf_op jit(solution)/shard_map/all_to_all | solution.py:32
  19.3 10.6 %collective-permute-start.6 = (bf16[64,512]{1,0:T(8,128)(2,1)}, bf16[64,512]{1,0:T(8,128)(2,1)S(1)}, u32[]{:S(2)}, u32[]{:S(2)}) collective-permute-start(bf16[64,512]{1,0:T(8,128)(2,1)} %bitcast.118), channel_id=1, source_target_pairs={{0,64},{64,0},{1,65},{65,1},{2,66},{66,2},{3,67},{67,3},{4,68},{68... | collective-permute-start | bytes 196616 | tf_op jit(solution)/shard_map/ppermute | solution.py:23
  29.9 4.0 %collective-permute-start.7 = (bf16[32,2,512]{2,0,1:T(8,128)(2,1)S(1)}, bf16[32,2,512]{2,0,1:T(8,128)(2,1)S(1)}, u32[]{:S(2)}, u32[]{:S(2)}) collective-permute-start(bf16[32,2,512]{2,0,1:T(8,128)(2,1)S(1)} %copy.47), channel_id=1, source_target_pairs={{0,4},{1,5},{2,6},{3,7},{4,0},{5,1},{6,2},{7,3},{8,12},{9,13},{10,... | collective-permute-start | bytes 196616 | tf_op jit(solution)/shard_map/ppermute | solution.py:14
  34.0 7.0 %collective-permute-start.8 = (bf16[32,2,512]{2,0,1:T(8,128)(2,1)S(1)}, bf16[32,2,512]{2,0,1:T(8,128)(2,1)S(1)}, u32[]{:S(2)}, u32[]{:S(2)}) collective-permute-start(bf16[32,2,512]{2,0,1:T(8,128)(2,1)S(1)} %copy.47), channel_id=1, source_target_pairs={{0,68},{1,69},{2,70},{3,71},{4,64},{5,65},{6,66},{7,67},{64,4},{65... | collective-permute-start | bytes 196616 | tf_op jit(solution)/shard_map/ppermute | solution.py:19
  40.9 0.9 broadcast_select_fusion.1
  41.8 0.9 collective-permute-done.8
  42.7 0.7 fusion.13
  43.4 1.8 copy.41
  45.5 1.0 copy-done
  47.4 2.0 maximum_select_fusion.1
  49.3 7.7 %all-to-all-start.1 = ((bf16[32,160,128]{2,1,0:T(8,128)(2,1)}), bf16[32,160,128]{2,1,0:T(8,128)(2,1)S(1)}, u32[]{:S(2)}, u32[]{:S(2)}) async-start(bf16[32,160,128]{2,1,0:T(8,128)(2,1)} %maximum_select_fusion.1), calls=%async_computation.1 | async-start | bytes 2621440 | tf_op jit(solution)/shard_map/all_to_all | solution.py:32
  57.0 1.1 slice.79
  58.1 1.9 collective-permute-start.3
  60.1 1.1 slice.78
  61.2 3.8 %collective-permute-start.2 = (bf16[32,64,128]{2,1,0:T(8,128)(2,1)S(1)}, bf16[32,64,128]{2,1,0:T(8,128)(2,1)}, u32[]{:S(2)}, u32[]{:S(2)}) collective-permute-start(bf16[32,64,128]{2,1,0:T(8,128)(2,1)S(1)} %slice.78), channel_id=1, source_target_pairs={{0,4},{1,5},{2,6},{3,7},{4,0},{5,1},{6,2},{7,3},{8,12},{9,13},{10,... | collective-permute-start | bytes 1572872 | tf_op jit(solution)/shard_map/ppermute | solution.py:14
  65.0 0.7 constant_dynamic-slice_fusion
  65.7 5.7 %collective-permute-start.1 = (bf16[32,32,128]{2,1,0:T(8,128)(2,1)}, bf16[32,32,128]{2,1,0:T(8,128)(2,1)S(1)}, u32[]{:S(2)}, u32[]{:S(2)}) collective-permute-start(bf16[32,32,128]{2,1,0:T(8,128)(2,1)} %constant_dynamic-slice_fusion), channel_id=1, source_target_pairs={{0,64},{64,0},{1,65},{65,1},{2,66},{66,2},{3,67},{67,3},{4,68},{68... | collective-permute-start | bytes 786440 | tf_op jit(solution)/shard_map/ppermute | solution.py:23
  71.4 20.3 %all-to-all-done.1 = bf16[32,160,128]{2,1,0:T(8,128)(2,1)S(1)} async-done(((bf16[32,160,128]{2,1,0:T(8,128)(2,1)}), bf16[32,160,128]{2,1,0:T(8,128)(2,1)S(1)}, u32[]{:S(2)}, u32[]{:S(2)}) %all-to-all-start.1) | async-done | bytes 1310752 | tf_op jit(solution)/shard_map/all_to_all | solution.py:32
  91.7 0.5 slice.77
  92.2 7.2 %collective-permute-done.1 = bf16[32,32,128]{2,1,0:T(8,128)(2,1)S(1)} collective-permute-done((bf16[32,32,128]{2,1,0:T(8,128)(2,1)}, bf16[32,32,128]{2,1,0:T(8,128)(2,1)S(1)}, u32[]{:S(2)}, u32[]{:S(2)}) %collective-permute-start.1) | collective-permute-done | bytes 262176 | tf_op jit(solution)/shard_map/ppermute | solution.py:23
  99.4 3.3 %maximum_select_fusion = bf16[32,192,128]{2,1,0:T(8,128)(2,1)} fusion(bf16[32,64,128]{2,1,0:T(8,128)(2,1)S(1)} %collective-permute-done.3, bf16[32,64,128]{2,1,0:T(8,128)(2,1)} %collective-permute-done.2, bf16[32,32,128]{2,1,0:T(8,128)(2,1)S(1)} %collective-permute-done.1, bf16[32,32,128]{2,1,0:T(8,128)(2,1)S(1)} %constant_dynamic-slice_fusion.1, pred[]{:T(512)S(6)} %gt.4, ...), kind=kLoop, calls=%fused_computation.8 | loop fusion | flops 7077888 | bytes 3145731 | tf_op jit(solution)/shard_map/jit(_where)/select_n | solution.py:37
  102.7 9.0 %all-to-all-start.2 = ((bf16[32,192,128]{2,1,0:T(8,128)(2,1)}), bf16[32,192,128]{2,1,0:T(8,128)(2,1)S(1)}, u32[]{:S(2)}, u32[]{:S(2)}) async-start(bf16[32,192,128]{2,1,0:T(8,128)(2,1)} %maximum_select_fusion), calls=%async_computation.2 | async-start | bytes 3145728 | tf_op jit(solution)/shard_map/all_to_all | solution.py:32
  111.7 0.9 fusion.18
  112.6 3.1 %collective-permute-start = (bf16[32,40,128]{2,1,0:T(8,128)(2,1)S(1)}, bf16[32,40,128]{2,1,0:T(8,128)(2,1)S(1)}, u32[]{:S(2)}, u32[]{:S(2)}) collective-permute-start(bf16[32,40,128]{2,1,0:T(8,128)(2,1)S(1)} %constant_dynamic-slice_fusion.2), channel_id=1, source_target_pairs={{0,64},{64,0},{1,65},{65,1},{2,66},{66,2},{3,67},{67,3},{4,68},{68... | collective-permute-start | bytes 983048 | tf_op jit(solution)/shard_map/ppermute | solution.py:23
  115.8 1.9 collective-permute-start.4
  117.7 6.3 %collective-permute-start.5 = (bf16[32,80,128]{2,1,0:T(8,128)(2,1)S(1)}, bf16[32,80,128]{2,1,0:T(8,128)(2,1)}, u32[]{:S(2)}, u32[]{:S(2)}) collective-permute-start(bf16[32,80,128]{2,1,0:T(8,128)(2,1)S(1)} %get-tuple-element.19), channel_id=1, source_target_pairs={{0,68},{1,69},{2,70},{3,71},{4,64},{5,65},{6,66},{7,67},{64,4},{65... | collective-permute-start | bytes 1966088 | tf_op jit(solution)/shard_map/ppermute | solution.py:19
  124.0 0.8 reshape.70
  125.0 0.7 reshape.71
  125.7 1.1 select_bitcast_fusion.5
  126.9 0.7 copy.42
  127.6 30.6 %collective-permute-done.4 = bf16[32,80,128]{2,1,0:T(8,128)(2,1)} collective-permute-done((bf16[32,80,128]{2,1,0:T(8,128)(2,1)}, bf16[32,80,128]{2,1,0:T(8,128)(2,1)}, u32[]{:S(2)}, u32[]{:S(2)}) %collective-permute-start.4) | collective-permute-done | bytes 655392 | tf_op jit(solution)/shard_map/ppermute | solution.py:14
  158.2 1.4 select_bitcast_fusion.1
  160.0 1.1 copy-done.2
  161.3 0.5 copy.43
  162.0 0.7 copy.45
  162.7 1.0 copy-done.4
  163.7 0.7 multiply_convert_fusion.1
  164.5 0.9 reshape.68
  165.4 3.0 %convolution_convert_fusion.1 = bf16[72,512]{1,0:T(8,128)(2,1)S(1)} fusion(bf16[72,4096]{1,0:T(8,128)(2,1)S(1)} %reshape.68, bf16[4096,512]{1,0:T(8,128)(2,1)} %all-gather.3.cloned.1.call-done), kind=kOutput, calls=%fused_computation.20 | convolution fusion | flops 302026752 | bytes 4857856 | tf_op jit(solution)/shard_map/dot_general | solution.py:110
  168.5 18.5 %all-gather = bf16[576,640]{1,0:T(8,128)(2,1)S(1)} all-gather(bf16[72,640]{1,0:T(8,128)(2,1)S(1)} %pad_maximum_fusion.2), channel_id=2, replica_groups=mesh['x'=4,'zh'=2,'y'=8,'nw'=8] {'nw'}, dimensions={0}, use_global_device_ids=true | all-gather | bytes 829440 | tf_op jit(solution)/shard_map/all_gather | solution.py:113
  187.3 0.7 copy.54
  188.8 3.7 %convolution_convert_fusion = bf16[144,4096]{1,0:T(8,128)(2,1)S(1)} fusion(bf16[4096,512]{1,0:T(8,128)(2,1)} %all-gather.3.cloned.1.call-done, f32[144,512]{1,0:T(8,128)S(1)} %reshape.76, f32[144,512]{1,0:T(8,128)S(1)} %maximum_add_fusion), kind=kOutput, calls=%fused_computation | convolution fusion | flops 605233152 | bytes 5963776 | tf_op jit(solution)/shard_map/dot_general | solution.py:128
  192.5 2.6 %reshape.72 = bf16[144,4,8,2,64]{4,3,2,1,0:T(2,128)(2,1)S(1)} reshape(bf16[144,4096]{1,0:T(8,128)(2,1)S(1)} %convolution_convert_fusion) | data formatting | bytes 2359296 | tf_op jit(solution)/shard_map/reshape | solution.py:131
  195.1 0.5 copy.56
  195.6 0.7 copy-done.3
  196.7 2.2 %fusion = bf16[144,1,64,128]{3,2,1,0:T(8,128)(2,1)} fusion(bf16[144,64,64]{2,1,0:T(8,128)(2,1)S(1)} %bitcast.109, bf16[64,64,128]{2,1,0:T(8,128)(2,1)S(1)} %bitcast.112, bf16[80,64,128]{2,1,0:T(8,128)(2,1)S(1)} %bitcast.107), kind=kOutput, calls=%fused_computation.2 | convolution fusion | flops 154533888 | bytes 5898240 | tf_op jit(solution)/shard_map/sij,sje->sie/dot_general | solution.py:133
  (51 shorter events, 3.6 us)
Async XLA Ops:
  8.7 21.2 %all-to-all-start = ((bf16[32,2,512]{2,1,0:T(2,128)(2,1)}), bf16[32,2,512]{2,1,0:T(2,128)(2,1)S(1)}, u32[]{:S(2)}, u32[]{:S(2)}) async-start(bf16[32,2,512]{2,1,0:T(2,128)(2,1)} %copy.40), calls=%async_computation | async-start | bytes 131072 | tf_op jit(solution)/shard_map/all_to_all | solution.py:32
  19.2 146.2 %all-gather.3.cloned.1.call-start = ((), (), s32[]{:S(2)}) async-start(), calls=%async_computation.3 | async-start | bytes 4325376 | tf_op jit(solution)/shard_map/all_gather | solution.py:83
  19.3 21.7 %collective-permute-start.6 = (bf16[64,512]{1,0:T(8,128)(2,1)}, bf16[64,512]{1,0:T(8,128)(2,1)S(1)}, u32[]{:S(2)}, u32[]{:S(2)}) collective-permute-start(bf16[64,512]{1,0:T(8,128)(2,1)} %bitcast.118), channel_id=1, source_target_pairs={{0,64},{64,0},{1,65},{65,1},{2,66},{66,2},{3,67},{67,3},{4,68},{68... | collective-permute-start | bytes 196616 | tf_op jit(solution)/shard_map/ppermute | solution.py:23
  29.9 11.9 %collective-permute-start.7 = (bf16[32,2,512]{2,0,1:T(8,128)(2,1)S(1)}, bf16[32,2,512]{2,0,1:T(8,128)(2,1)S(1)}, u32[]{:S(2)}, u32[]{:S(2)}) collective-permute-start(bf16[32,2,512]{2,0,1:T(8,128)(2,1)S(1)} %copy.47), channel_id=1, source_target_pairs={{0,4},{1,5},{2,6},{3,7},{4,0},{5,1},{6,2},{7,3},{8,12},{9,13},{10,... | collective-permute-start | bytes 196616 | tf_op jit(solution)/shard_map/ppermute | solution.py:14
  34.0 8.7 %collective-permute-start.8 = (bf16[32,2,512]{2,0,1:T(8,128)(2,1)S(1)}, bf16[32,2,512]{2,0,1:T(8,128)(2,1)S(1)}, u32[]{:S(2)}, u32[]{:S(2)}) collective-permute-start(bf16[32,2,512]{2,0,1:T(8,128)(2,1)S(1)} %copy.47), channel_id=1, source_target_pairs={{0,68},{1,69},{2,70},{3,71},{4,64},{5,65},{6,66},{7,67},{64,4},{65... | collective-permute-start | bytes 196616 | tf_op jit(solution)/shard_map/ppermute | solution.py:19
  45.4 1.1 copy-start
  45.4 1.4 copy-start.1
  49.3 42.4 %all-to-all-start.1 = ((bf16[32,160,128]{2,1,0:T(8,128)(2,1)}), bf16[32,160,128]{2,1,0:T(8,128)(2,1)S(1)}, u32[]{:S(2)}, u32[]{:S(2)}) async-start(bf16[32,160,128]{2,1,0:T(8,128)(2,1)} %maximum_select_fusion.1), calls=%async_computation.1 | async-start | bytes 2621440 | tf_op jit(solution)/shard_map/all_to_all | solution.py:32
  58.1 41.3 %collective-permute-start.3 = (bf16[32,64,128]{2,1,0:T(8,128)(2,1)S(1)}, bf16[32,64,128]{2,1,0:T(8,128)(2,1)S(1)}, u32[]{:S(2)}, u32[]{:S(2)}) collective-permute-start(bf16[32,64,128]{2,1,0:T(8,128)(2,1)S(1)} %slice.79), channel_id=1, source_target_pairs={{0,68},{1,69},{2,70},{3,71},{4,64},{5,65},{6,66},{7,67},{64,4},{65... | collective-permute-start | bytes 1572872 | tf_op jit(solution)/shard_map/ppermute | solution.py:19
  61.2 38.3 %collective-permute-start.2 = (bf16[32,64,128]{2,1,0:T(8,128)(2,1)S(1)}, bf16[32,64,128]{2,1,0:T(8,128)(2,1)}, u32[]{:S(2)}, u32[]{:S(2)}) collective-permute-start(bf16[32,64,128]{2,1,0:T(8,128)(2,1)S(1)} %slice.78), channel_id=1, source_target_pairs={{0,4},{1,5},{2,6},{3,7},{4,0},{5,1},{6,2},{7,3},{8,12},{9,13},{10,... | collective-permute-start | bytes 1572872 | tf_op jit(solution)/shard_map/ppermute | solution.py:14
  65.7 33.7 %collective-permute-start.1 = (bf16[32,32,128]{2,1,0:T(8,128)(2,1)}, bf16[32,32,128]{2,1,0:T(8,128)(2,1)S(1)}, u32[]{:S(2)}, u32[]{:S(2)}) collective-permute-start(bf16[32,32,128]{2,1,0:T(8,128)(2,1)} %constant_dynamic-slice_fusion), channel_id=1, source_target_pairs={{0,64},{64,0},{1,65},{65,1},{2,66},{66,2},{3,67},{67,3},{4,68},{68... | collective-permute-start | bytes 786440 | tf_op jit(solution)/shard_map/ppermute | solution.py:23
  102.7 58.5 %all-to-all-start.2 = ((bf16[32,192,128]{2,1,0:T(8,128)(2,1)}), bf16[32,192,128]{2,1,0:T(8,128)(2,1)S(1)}, u32[]{:S(2)}, u32[]{:S(2)}) async-start(bf16[32,192,128]{2,1,0:T(8,128)(2,1)} %maximum_select_fusion), calls=%async_computation.2 | async-start | bytes 3145728 | tf_op jit(solution)/shard_map/all_to_all | solution.py:32
  112.6 13.1 %collective-permute-start = (bf16[32,40,128]{2,1,0:T(8,128)(2,1)S(1)}, bf16[32,40,128]{2,1,0:T(8,128)(2,1)S(1)}, u32[]{:S(2)}, u32[]{:S(2)}) collective-permute-start(bf16[32,40,128]{2,1,0:T(8,128)(2,1)S(1)} %constant_dynamic-slice_fusion.2), channel_id=1, source_target_pairs={{0,64},{64,0},{1,65},{65,1},{2,66},{66,2},{3,67},{67,3},{4,68},{68... | collective-permute-start | bytes 983048 | tf_op jit(solution)/shard_map/ppermute | solution.py:23
  115.8 42.4 %collective-permute-start.4 = (bf16[32,80,128]{2,1,0:T(8,128)(2,1)}, bf16[32,80,128]{2,1,0:T(8,128)(2,1)}, u32[]{:S(2)}, u32[]{:S(2)}) collective-permute-start(bf16[32,80,128]{2,1,0:T(8,128)(2,1)} %get-tuple-element.18), channel_id=1, source_target_pairs={{0,4},{1,5},{2,6},{3,7},{4,0},{5,1},{6,2},{7,3},{8,12},{9,13},{10,... | collective-permute-start | bytes 1966088 | tf_op jit(solution)/shard_map/ppermute | solution.py:14
  117.7 40.5 %collective-permute-start.5 = (bf16[32,80,128]{2,1,0:T(8,128)(2,1)S(1)}, bf16[32,80,128]{2,1,0:T(8,128)(2,1)}, u32[]{:S(2)}, u32[]{:S(2)}) collective-permute-start(bf16[32,80,128]{2,1,0:T(8,128)(2,1)S(1)} %get-tuple-element.19), channel_id=1, source_target_pairs={{0,68},{1,69},{2,70},{3,71},{4,64},{5,65},{6,66},{7,67},{64,4},{65... | collective-permute-start | bytes 1966088 | tf_op jit(solution)/shard_map/ppermute | solution.py:19
  160.0 1.1 copy-start.2
  162.7 1.0 copy-start.4
  165.4 3.1 %copy-start.6 = (bf16[72,128]{1,0:T(8,128)(2,1)S(1)}, bf16[72,128]{1,0:T(8,128)(2,1)}, u32[]{:S(2)}) copy-start(bf16[72,128]{1,0:T(8,128)(2,1)} %reshape.71) | copy-start | bytes 55300
  168.5 18.7 %copy-start.7 = (f32[512]{0:T(512)S(1)}, f32[512]{0:T(512)}, u32[]{:S(2)}) copy-start(f32[512]{0:T(512)} %param.6) | copy-start | bytes 6148
  195.1 1.3 copy-start.3
  195.1 1.6 copy-start.5
Sparse Core Ops, SparseCore 0:
  43.5 111.2 all-gather.2

commit v5 on v4

--- a/solution.py
+++ b/solution.py
@@ -32,20 +32,15 @@
     return lax.all_to_all(v, ("x", "y"), 0, 0, tiled=True)
 
 
-def after(v, others, zh):
-    for other in others:
-        v = jnp.where(zh > 1, other[(0,) * other.ndim].astype(v.dtype), v)
-    return v
-
-
 def folded_weights(w, turned, zh):
     units = w.shape[-1]
-    raw_other = cross_same(w)
-    near = swap_block(turned)
-    far = cross_block(turned)
-    theirs = in_order(near, far, zh).transpose(2, 0, 1, 3)
-    mine = in_order(w, raw_other, zh).reshape(ZH, X, ZH, Y, units)
-    mine = mine.transpose(0, 2, 1, 3, 4).reshape(ZH, ZH, XY, units)
+    by_zh = w.reshape(X, ZH, Y, units)
+    first, second = by_zh[:, 0], by_zh[:, 1]
+    raw = in_order(first, second, zh).reshape(ZH * XY, units)
+    raw_other = cross_same(in_order(second, first, zh).reshape(ZH * XY, units))
+    theirs = jnp.stack([swap_block(turned), cross_block(turned)], 0)
+    theirs = theirs.transpose(2, 0, 1, 3)
+    mine = in_order(raw, raw_other, zh).reshape(ZH, ZH, XY, units)
     fold = (mine.astype(F32) + theirs.astype(F32)).astype(BF)
     return fold.reshape(ZH * 64, units)
 
@@ -65,16 +60,20 @@
         h = v.shape[1] // 2
         return lax.dynamic_slice_in_dim(v, half * h, h, 1)
 
-    by_dest = pooled.reshape(X, ZH, Y, count, width).transpose(1, 0, 2, 3, 4)
-    by_dest = by_dest.reshape(ZH, XY, count, width)
-    mine = lax.dynamic_index_in_dim(by_dest, zh, 0, keepdims=False)
-    theirs = lax.dynamic_index_in_dim(by_dest, 1 - zh, 0, keepdims=False)
+    by_dest = pooled.reshape(X, ZH, Y, count, width)
+
+    def samples_of(which, start, stop):
+        v = lax.dynamic_index_in_dim(by_dest[:, :, :, start:stop], which, 1, keepdims=False)
+        return v.reshape(XY, stop - start, width)
+
+    mine = samples_of(zh, 0, n), samples_of(zh, n, count)
+    theirs = samples_of(1 - zh, 0, n), samples_of(1 - zh, n, count)
 
     def move_z(own, away):
         x_away, y_own, y_away = cross_same(my_half(away)), swap_block(own), cross_block(away)
         return my_half(own), x_away, y_own, y_away
 
-    moved_1 = move_z(mine[:, n:], theirs[:, n:])
+    moved_1 = move_z(mine[1], theirs[1])
 
     w = w_top[0]
     w_rows = w.reshape(X, ZH, Y, units).transpose(0, 2, 1, 3).reshape(XY, ZH, units)
@@ -82,10 +81,10 @@
     fold = folded_weights(w, turned, zh)
     weights = lax.all_gather(fold, ("x", "y"), axis=0, tiled=True)
 
-    first = jnp.concatenate([mine[:, :n], theirs[:, :n]], 1)
-    got = along_xy(after(first, [turned], zh))
+    first = jnp.concatenate([mine[0], theirs[0]], 1)
+    got = along_xy(first)
     moved_0 = move_z(got[:, :n], got[:, n:])
-    last = along_xy(after(jnp.concatenate(moved_1, 1), [got], zh))
+    last = along_xy(jnp.concatenate(moved_1, 1))
     h = rest // 2
     moved_1 = last[:, :h], last[:, h:rest], last[:, rest : 2 * rest], last[:, 2 * rest :]
 
@@ -94,8 +93,7 @@
         return v.reshape(XY * ZH, v.shape[2], width).transpose(1, 0, 2)
 
     def columns_of(own, other):
-        v = in_order(own, other, zh)
-        return v.reshape(ZH * XY, v.shape[2], width).transpose(1, 0, 2)
+        return jnp.concatenate([own, other], 0).transpose(1, 0, 2)
 
     moved = moved_0, moved_1
     left = jnp.concatenate([rows_of(v[0], v[1]) for v in moved], 0)

time: 207 us -> 205 us (level); the launches traced: 206 us -> 201 us
  waiting for transfers between devices: 59 us -> 64.2 us
  other arithmetic: 9.95 us -> 5.21 us
  starting transfers between devices: 71.6 us -> 67.4 us
    ppermute x3, waiting for transfers between devices: 7.17 us -> 35.5 us  [cross_same(): return lax.ppermute(v, 'zh', [(0, 1), (1, 0)])]
    all_to_all x3, waiting for transfers between devices: 20.3 us -> 0.01 us  [along_xy(): return lax.all_to_all(v, ('x', 'y'), 0, 0, tiled=True)]
    select_n x2 -> x1, other arithmetic: 5.22 us -> 0.78 us  [in_order(): jnp.where(first, other, own)]
    all_to_all x3, starting transfers between devices: 27.2 us -> 23.4 us  [along_xy(): return lax.all_to_all(v, ('x', 'y'), 0, 0, tiled=True)]
    ppermute x3, starting transfers between devices: 15.2 us -> 18.3 us  [cross_block(): return lax.ppermute(v, ('zh', 'nw'), pairs)]
    ppermute x3, starting transfers between devices: 9.71 us -> 6.8 us  [swap_block(): return lax.ppermute(v, 'nw', [(i, i ^ 4) for i in range(8)])]
    reshape x3, local copies, waits for them, and re-layouts: 1.65 us -> 4.4 us  [body(): grad_hidden.reshape(2, hc, share).transpose(1, 0, 2).reshape(hc, 2 * share)]
    another operation x7 -> x4, other arithmetic: 2.83 us -> 0.15 us  [in_order(): jnp.stack([jnp.where(first, own, other), jnp.where(first, other, own)], 0)]
  transfers between devices with their start and end apart: 13 -> 13, of which waited for: 4 -> 4; matrix products, arithmetic and copies ran while one was open for 11% -> 9% of each run, Pallas kernels for 0% -> 0%
where the time goes in v5:
time: 205 us; the launch traced here: 201 us
  starting transfers between devices  67.4 us (33%)
  waiting for transfers between devices  64.2 us (31%)
  local copies, waits for them, and re-layouts  22.4 us (11%)
  blocking collectives  17.8 us (9%)
  between operations  14.6 us (7%)
  matrix products  9.65 us (5%)
  other arithmetic  5.21 us (3%)
    ppermute x3, waiting for transfers between devices, cross_same(): return lax.ppermute(v, 'zh', [(0, 1), (1, 0)])  35.5 us
    ppermute x3, waiting for transfers between devices, swap_block(): return lax.ppermute(v, 'nw', [(i, i ^ 4) for i in range(8)])  28.6 us
    all_to_all x3, starting transfers between devices, along_xy(): return lax.all_to_all(v, ('x', 'y'), 0, 0, tiled=True)  23.4 us
    ppermute x3, starting transfers between devices, cross_same(): return lax.ppermute(v, 'zh', [(0, 1), (1, 0)])  18.9 us
    ppermute x3, starting transfers between devices, cross_block(): return lax.ppermute(v, ('zh', 'nw'), pairs)  18.3 us
    all_gather x1, blocking collectives, body(): lax.all_gather(jnp.concatenate([part.astype(BF), cot], 1), 'nw', axis=0,...  17.8 us
    ppermute x3, starting transfers between devices, swap_block(): return lax.ppermute(v, 'nw', [(i, i ^ 4) for i in range(8)])  6.8 us
    unnamed x19, local copies, waits for them, and re-layouts  5.46 us
  transfers between devices with their start and end apart: 13, of which 4 were waited for; matrix products, arithmetic and copies ran while one was open for 9% of the time, Pallas kernels for 0%

profile of v5, /device:TPU:1, one launch (start us, length us, event | category | flops | bytes accessed | tf_op | source)
XLA Modules:
  0.0 201.3 jit_solution(1086420331126668023)
XLA Ops:
  7.2 0.8 copy.87
  8.0 0.7 copy.60
  8.7 10.5 %all-to-all-start.2 = ((bf16[32,2,512]{2,1,0:T(2,128)(2,1)}), bf16[32,2,512]{2,1,0:T(2,128)(2,1)S(1)}, u32[]{:S(2)}, u32[]{:S(2)}) async-start(bf16[32,2,512]{2,1,0:T(2,128)(2,1)} %copy.60), calls=%async_computation.2 | async-start | bytes 131072 | tf_op jit(solution)/shard_map/all_to_all | solution.py:32
  19.3 0.8 fusion.15
  20.1 0.8 fusion.16
  20.9 10.6 %collective-permute-start.6 = (bf16[64,512]{1,0:T(8,128)(2,1)S(1)}, bf16[64,512]{1,0:T(8,128)(2,1)S(1)}, u32[]{:S(2)}, u32[]{:S(2)}) collective-permute-start(bf16[64,512]{1,0:T(8,128)(2,1)S(1)} %bitcast.130), channel_id=1, source_target_pairs={{0,64},{64,0},{1,65},{65,1},{2,66},{66,2},{3,67},{67,3},{4,68},{68... | collective-permute-start | bytes 196616 | tf_op jit(solution)/shard_map/ppermute | solution.py:23
  31.5 7.2 %collective-permute-start.8 = (bf16[32,2,512]{2,0,1:T(8,128)(2,1)S(1)}, bf16[32,2,512]{2,0,1:T(8,128)(2,1)S(1)}, u32[]{:S(2)}, u32[]{:S(2)}) collective-permute-start(bf16[32,2,512]{2,0,1:T(8,128)(2,1)S(1)} %copy.61), channel_id=1, source_target_pairs={{0,68},{1,69},{2,70},{3,71},{4,64},{5,65},{6,66},{7,67},{64,4},{65... | collective-permute-start | bytes 196616 | tf_op jit(solution)/shard_map/ppermute | solution.py:19
  38.8 2.2 %collective-permute-start.7 = (bf16[32,2,512]{2,0,1:T(8,128)(2,1)S(1)}, bf16[32,2,512]{2,0,1:T(8,128)(2,1)S(1)}, u32[]{:S(2)}, u32[]{:S(2)}) collective-permute-start(bf16[32,2,512]{2,0,1:T(8,128)(2,1)S(1)} %copy.61), channel_id=1, source_target_pairs={{0,4},{1,5},{2,6},{3,7},{4,0},{5,1},{6,2},{7,3},{8,12},{9,13},{10,... | collective-permute-start | bytes 196616 | tf_op jit(solution)/shard_map/ppermute | solution.py:14
  41.0 3.8 %collective-permute-done.7 = bf16[32,2,512]{2,0,1:T(8,128)(2,1)S(1)} collective-permute-done((bf16[32,2,512]{2,0,1:T(8,128)(2,1)S(1)}, bf16[32,2,512]{2,0,1:T(8,128)(2,1)S(1)}, u32[]{:S(2)}, u32[]{:S(2)}) %collective-permute-start.7) | collective-permute-done | bytes 65568 | tf_op jit(solution)/shard_map/ppermute | solution.py:14
  44.8 0.7 fusion.13
  45.5 1.4 slice.66
  47.0 1.2 pad_maximum_fusion.1
  48.2 4.0 %all-to-all-start = ((bf16[32,160,128]{2,1,0:T(8,128)(2,1)}), bf16[32,160,128]{2,1,0:T(8,128)(2,1)S(1)}, u32[]{:S(2)}, u32[]{:S(2)}) async-start(bf16[32,160,128]{2,1,0:T(8,128)(2,1)} %pad_maximum_fusion.1), calls=%async_computation | async-start | bytes 2621440 | tf_op jit(solution)/shard_map/all_to_all | solution.py:32
  52.2 1.3 slice.69
  53.6 6.6 %collective-permute-start.3 = (bf16[32,64,128]{2,1,0:T(8,128)(2,1)S(1)}, bf16[32,64,128]{2,1,0:T(8,128)(2,1)S(1)}, u32[]{:S(2)}, u32[]{:S(2)}) collective-permute-start(bf16[32,64,128]{2,1,0:T(8,128)(2,1)S(1)} %bitcast.118), channel_id=1, source_target_pairs={{0,68},{1,69},{2,70},{3,71},{4,64},{5,65},{6,66},{7,67},{64,4},{65... | collective-permute-start | bytes 1572872 | tf_op jit(solution)/shard_map/ppermute | solution.py:19
  60.3 2.7 %collective-permute-start.2 = (bf16[32,64,128]{2,1,0:T(8,128)(2,1)S(1)}, bf16[32,64,128]{2,1,0:T(8,128)(2,1)S(1)}, u32[]{:S(2)}, u32[]{:S(2)}) collective-permute-start(bf16[32,64,128]{2,1,0:T(8,128)(2,1)S(1)} %bitcast.116), channel_id=1, source_target_pairs={{0,4},{1,5},{2,6},{3,7},{4,0},{5,1},{6,2},{7,3},{8,12},{9,13},{10,... | collective-permute-start | bytes 1572872 | tf_op jit(solution)/shard_map/ppermute | solution.py:14
  63.0 3.2 %collective-permute-start.1 = (bf16[32,32,128]{2,1,0:T(8,128)(2,1)S(1)}, bf16[32,32,128]{2,1,0:T(8,128)(2,1)S(1)}, u32[]{:S(2)}, u32[]{:S(2)}) collective-permute-start(bf16[32,32,128]{2,1,0:T(8,128)(2,1)S(1)} %constant_dynamic-slice_fusion), channel_id=1, source_target_pairs={{0,64},{64,0},{1,65},{65,1},{2,66},{66,2},{3,67},{67,3},{4,68},{68... | collective-permute-start | bytes 786440 | tf_op jit(solution)/shard_map/ppermute | solution.py:23
  66.3 29.6 %collective-permute-done.1 = bf16[32,32,128]{2,1,0:T(8,128)(2,1)S(1)} collective-permute-done((bf16[32,32,128]{2,1,0:T(8,128)(2,1)S(1)}, bf16[32,32,128]{2,1,0:T(8,128)(2,1)S(1)}, u32[]{:S(2)}, u32[]{:S(2)}) %collective-permute-start.1) | collective-permute-done | bytes 262176 | tf_op jit(solution)/shard_map/ppermute | solution.py:23
  95.9 1.3 pad_maximum_fusion
  97.2 8.9 %all-to-all-start.1 = ((bf16[32,192,128]{2,1,0:T(8,128)(2,1)}), bf16[32,192,128]{2,1,0:T(8,128)(2,1)S(1)}, u32[]{:S(2)}, u32[]{:S(2)}) async-start(bf16[32,192,128]{2,1,0:T(8,128)(2,1)} %pad_maximum_fusion), calls=%async_computation.1 | async-start | bytes 3145728 | tf_op jit(solution)/shard_map/all_to_all | solution.py:32
  106.5 5.0 %collective-permute-start = (bf16[32,40,128]{2,0,1:T(8,128)(2,1)S(1)}, bf16[32,40,128]{2,0,1:T(8,128)(2,1)S(1)}, u32[]{:S(2)}, u32[]{:S(2)}) collective-permute-start(bf16[32,40,128]{2,0,1:T(8,128)(2,1)S(1)} %constant_dynamic-slice_fusion.4), channel_id=1, source_target_pairs={{0,64},{64,0},{1,65},{65,1},{2,66},{66,2},{3,67},{67,3},{4,68},{68... | collective-permute-start | bytes 983048 | tf_op jit(solution)/shard_map/ppermute | solution.py:23
  111.7 1.9 collective-permute-start.4
  113.6 4.4 %collective-permute-start.5 = (bf16[32,80,128]{2,0,1:T(8,128)(2,1)S(1)}, bf16[32,80,128]{2,0,1:T(8,128)(2,1)}, u32[]{:S(2)}, u32[]{:S(2)}) collective-permute-start(bf16[32,80,128]{2,0,1:T(8,128)(2,1)S(1)} %copy.74), channel_id=1, source_target_pairs={{0,68},{1,69},{2,70},{3,71},{4,64},{5,65},{6,66},{7,67},{64,4},{65... | collective-permute-start | bytes 1966088 | tf_op jit(solution)/shard_map/ppermute | solution.py:19
  118.0 1.5 reshape.121
  119.5 1.5 copy.63
  121.0 1.5 reshape.122
  122.4 5.9 %collective-permute-done = bf16[32,40,128]{2,0,1:T(8,128)(2,1)S(1)} collective-permute-done((bf16[32,40,128]{2,0,1:T(8,128)(2,1)S(1)}, bf16[32,40,128]{2,0,1:T(8,128)(2,1)S(1)}, u32[]{:S(2)}, u32[]{:S(2)}) %collective-permute-start) | collective-permute-done | bytes 327712 | tf_op jit(solution)/shard_map/ppermute | solution.py:23
  128.5 0.3 copy.48
  128.9 24.8 %collective-permute-done.4 = bf16[32,80,128]{2,0,1:T(8,128)(2,1)} collective-permute-done((bf16[32,80,128]{2,0,1:T(8,128)(2,1)S(1)}, bf16[32,80,128]{2,0,1:T(8,128)(2,1)}, u32[]{:S(2)}, u32[]{:S(2)}) %collective-permute-start.4) | collective-permute-done | bytes 655392 | tf_op jit(solution)/shard_map/ppermute | solution.py:14
  153.7 1.2 constant_dynamic-update-slice_fusion.1
  154.9 1.2 constant_dynamic-update-slice_fusion
  156.1 1.1 copy-done
  157.2 0.9 dynamic-slice_bitcast_fusion
  158.3 0.3 copy_dynamic-update-slice_fusion.1
  158.7 0.4 copy_dynamic-update-slice_fusion
  159.3 0.7 copy-done.2
  160.0 0.7 multiply_convert_fusion.1
  160.8 0.9 reshape.116
  161.7 3.0 %convolution_convert_fusion.1 = bf16[72,512]{1,0:T(8,128)(2,1)S(1)} fusion(bf16[72,4096]{1,0:T(8,128)(2,1)S(1)} %reshape.116, bf16[4096,512]{1,0:T(8,128)(2,1)} %all-gather.3.cloned.1.call-done), kind=kOutput, calls=%fused_computation.17 | convolution fusion | flops 302026752 | bytes 4857856 | tf_op jit(solution)/shard_map/dot_general | solution.py:108
  164.8 17.8 %all-gather = bf16[576,640]{1,0:T(8,128)(2,1)S(1)} all-gather(bf16[72,640]{1,0:T(8,128)(2,1)S(1)} %pad_maximum_fusion.3), channel_id=2, replica_groups=mesh['x'=4,'zh'=2,'y'=8,'nw'=8] {'nw'}, dimensions={0}, use_global_device_ids=true | all-gather | bytes 829440 | tf_op jit(solution)/shard_map/all_gather | solution.py:111
  182.9 0.7 copy.67
  183.6 0.4 reshape.127
  184.4 3.7 %convolution_convert_fusion = bf16[144,4096]{1,0:T(8,128)(2,1)S(1)} fusion(bf16[4096,512]{1,0:T(8,128)(2,1)} %all-gather.3.cloned.1.call-done, f32[144,512]{1,0:T(8,128)S(1)} %reshape.126, f32[144,512]{1,0:T(8,128)S(1)} %maximum_add_fusion), kind=kOutput, calls=%fused_computation | convolution fusion | flops 605233152 | bytes 5963776 | tf_op jit(solution)/shard_map/dot_general | solution.py:126
  188.1 2.6 %reshape.123 = bf16[144,4,8,2,64]{4,3,2,1,0:T(2,128)(2,1)S(1)} reshape(bf16[144,4096]{1,0:T(8,128)(2,1)S(1)} %convolution_convert_fusion) | data formatting | bytes 2359296 | tf_op jit(solution)/shard_map/reshape | solution.py:129
  190.7 0.5 copy.69
  191.2 0.7 copy-done.1
  192.0 0.3 copy-done.3
  192.3 2.2 %fusion = bf16[144,1,64,128]{3,2,1,0:T(8,128)(2,1)} fusion(bf16[144,64,64]{2,1,0:T(8,128)(2,1)S(1)} %bitcast.112, bf16[64,64,128]{2,1,0:T(8,128)(2,1)S(1)} %bitcast.120, bf16[80,64,128]{2,1,0:T(8,128)(2,1)S(1)} %bitcast.115), kind=kOutput, calls=%fused_computation.2 | convolution fusion | flops 154533888 | bytes 5898240 | tf_op jit(solution)/shard_map/sij,sje->sie/dot_general | solution.py:131
  (48 shorter events, 2.2 us)
Async XLA Ops:
  8.7 22.8 %all-to-all-start.2 = ((bf16[32,2,512]{2,1,0:T(2,128)(2,1)}), bf16[32,2,512]{2,1,0:T(2,128)(2,1)S(1)}, u32[]{:S(2)}, u32[]{:S(2)}) async-start(bf16[32,2,512]{2,1,0:T(2,128)(2,1)} %copy.60), calls=%async_computation.2 | async-start | bytes 131072 | tf_op jit(solution)/shard_map/all_to_all | solution.py:32
  19.2 142.5 %all-gather.3.cloned.1.call-start = ((), (), s32[]{:S(2)}) async-start(), calls=%async_computation.3 | async-start | bytes 4325376 | tf_op jit(solution)/shard_map/all_gather | solution.py:82
  20.9 20.1 %collective-permute-start.6 = (bf16[64,512]{1,0:T(8,128)(2,1)S(1)}, bf16[64,512]{1,0:T(8,128)(2,1)S(1)}, u32[]{:S(2)}, u32[]{:S(2)}) collective-permute-start(bf16[64,512]{1,0:T(8,128)(2,1)S(1)} %bitcast.130), channel_id=1, source_target_pairs={{0,64},{64,0},{1,65},{65,1},{2,66},{66,2},{3,67},{67,3},{4,68},{68... | collective-permute-start | bytes 196616 | tf_op jit(solution)/shard_map/ppermute | solution.py:23
  31.5 9.4 %collective-permute-start.8 = (bf16[32,2,512]{2,0,1:T(8,128)(2,1)S(1)}, bf16[32,2,512]{2,0,1:T(8,128)(2,1)S(1)}, u32[]{:S(2)}, u32[]{:S(2)}) collective-permute-start(bf16[32,2,512]{2,0,1:T(8,128)(2,1)S(1)} %copy.61), channel_id=1, source_target_pairs={{0,68},{1,69},{2,70},{3,71},{4,64},{5,65},{6,66},{7,67},{64,4},{65... | collective-permute-start | bytes 196616 | tf_op jit(solution)/shard_map/ppermute | solution.py:19
  38.8 6.0 %collective-permute-start.7 = (bf16[32,2,512]{2,0,1:T(8,128)(2,1)S(1)}, bf16[32,2,512]{2,0,1:T(8,128)(2,1)S(1)}, u32[]{:S(2)}, u32[]{:S(2)}) collective-permute-start(bf16[32,2,512]{2,0,1:T(8,128)(2,1)S(1)} %copy.61), channel_id=1, source_target_pairs={{0,4},{1,5},{2,6},{3,7},{4,0},{5,1},{6,2},{7,3},{8,12},{9,13},{10,... | collective-permute-start | bytes 196616 | tf_op jit(solution)/shard_map/ppermute | solution.py:14
  48.2 49.0 %all-to-all-start = ((bf16[32,160,128]{2,1,0:T(8,128)(2,1)}), bf16[32,160,128]{2,1,0:T(8,128)(2,1)S(1)}, u32[]{:S(2)}, u32[]{:S(2)}) async-start(bf16[32,160,128]{2,1,0:T(8,128)(2,1)} %pad_maximum_fusion.1), calls=%async_computation | async-start | bytes 2621440 | tf_op jit(solution)/shard_map/all_to_all | solution.py:32
  53.6 42.3 %collective-permute-start.3 = (bf16[32,64,128]{2,1,0:T(8,128)(2,1)S(1)}, bf16[32,64,128]{2,1,0:T(8,128)(2,1)S(1)}, u32[]{:S(2)}, u32[]{:S(2)}) collective-permute-start(bf16[32,64,128]{2,1,0:T(8,128)(2,1)S(1)} %bitcast.118), channel_id=1, source_target_pairs={{0,68},{1,69},{2,70},{3,71},{4,64},{5,65},{6,66},{7,67},{64,4},{65... | collective-permute-start | bytes 1572872 | tf_op jit(solution)/shard_map/ppermute | solution.py:19
  60.3 35.6 %collective-permute-start.2 = (bf16[32,64,128]{2,1,0:T(8,128)(2,1)S(1)}, bf16[32,64,128]{2,1,0:T(8,128)(2,1)S(1)}, u32[]{:S(2)}, u32[]{:S(2)}) collective-permute-start(bf16[32,64,128]{2,1,0:T(8,128)(2,1)S(1)} %bitcast.116), channel_id=1, source_target_pairs={{0,4},{1,5},{2,6},{3,7},{4,0},{5,1},{6,2},{7,3},{8,12},{9,13},{10,... | collective-permute-start | bytes 1572872 | tf_op jit(solution)/shard_map/ppermute | solution.py:14
  63.0 32.9 %collective-permute-start.1 = (bf16[32,32,128]{2,1,0:T(8,128)(2,1)S(1)}, bf16[32,32,128]{2,1,0:T(8,128)(2,1)S(1)}, u32[]{:S(2)}, u32[]{:S(2)}) collective-permute-start(bf16[32,32,128]{2,1,0:T(8,128)(2,1)S(1)} %constant_dynamic-slice_fusion), channel_id=1, source_target_pairs={{0,64},{64,0},{1,65},{65,1},{2,66},{66,2},{3,67},{67,3},{4,68},{68... | collective-permute-start | bytes 786440 | tf_op jit(solution)/shard_map/ppermute | solution.py:23
  97.2 61.0 %all-to-all-start.1 = ((bf16[32,192,128]{2,1,0:T(8,128)(2,1)}), bf16[32,192,128]{2,1,0:T(8,128)(2,1)S(1)}, u32[]{:S(2)}, u32[]{:S(2)}) async-start(bf16[32,192,128]{2,1,0:T(8,128)(2,1)} %pad_maximum_fusion), calls=%async_computation.1 | async-start | bytes 3145728 | tf_op jit(solution)/shard_map/all_to_all | solution.py:32
  106.5 21.9 %collective-permute-start = (bf16[32,40,128]{2,0,1:T(8,128)(2,1)S(1)}, bf16[32,40,128]{2,0,1:T(8,128)(2,1)S(1)}, u32[]{:S(2)}, u32[]{:S(2)}) collective-permute-start(bf16[32,40,128]{2,0,1:T(8,128)(2,1)S(1)} %constant_dynamic-slice_fusion.4), channel_id=1, source_target_pairs={{0,64},{64,0},{1,65},{65,1},{2,66},{66,2},{3,67},{67,3},{4,68},{68... | collective-permute-start | bytes 983048 | tf_op jit(solution)/shard_map/ppermute | solution.py:23
  111.7 42.1 %collective-permute-start.4 = (bf16[32,80,128]{2,0,1:T(8,128)(2,1)S(1)}, bf16[32,80,128]{2,0,1:T(8,128)(2,1)}, u32[]{:S(2)}, u32[]{:S(2)}) collective-permute-start(bf16[32,80,128]{2,0,1:T(8,128)(2,1)S(1)} %copy.73), channel_id=1, source_target_pairs={{0,4},{1,5},{2,6},{3,7},{4,0},{5,1},{6,2},{7,3},{8,12},{9,13},{10,... | collective-permute-start | bytes 1966088 | tf_op jit(solution)/shard_map/ppermute | solution.py:14
  113.6 41.4 %collective-permute-start.5 = (bf16[32,80,128]{2,0,1:T(8,128)(2,1)S(1)}, bf16[32,80,128]{2,0,1:T(8,128)(2,1)}, u32[]{:S(2)}, u32[]{:S(2)}) collective-permute-start(bf16[32,80,128]{2,0,1:T(8,128)(2,1)S(1)} %copy.74), channel_id=1, source_target_pairs={{0,68},{1,69},{2,70},{3,71},{4,64},{5,65},{6,66},{7,67},{64,4},{65... | collective-permute-start | bytes 1966088 | tf_op jit(solution)/shard_map/ppermute | solution.py:19
  156.1 1.1 copy-start
  158.7 1.4 copy-start.4
  159.1 1.0 copy-start.2
  161.7 3.1 %copy-start.5 = (bf16[72,128]{1,0:T(8,128)(2,1)S(1)}, bf16[72,128]{1,0:T(8,128)(2,1)}, u32[]{:S(2)}) copy-start(bf16[72,128]{1,0:T(8,128)(2,1)} %reshape.122) | copy-start | bytes 55300
  164.8 18.0 %copy-start.6 = (f32[512]{0:T(512)S(1)}, f32[512]{0:T(512)}, u32[]{:S(2)}) copy-start(f32[512]{0:T(512)} %param.6) | copy-start | bytes 6148
  190.6 1.3 copy-start.1
  190.7 1.6 copy-start.3
Sparse Core Ops, SparseCore 0:
  45.6 114.5 all-gather.2

commit v6 on v5

--- a/solution.py
+++ b/solution.py
@@ -5,7 +5,7 @@
 
 X, ZH, Y = 4, 2, 8
 XY = X * Y
-FIRST = 80
+FIRST = 96
 BF = jnp.bfloat16
 F32 = jnp.float32
 
@@ -84,7 +84,8 @@
     first = jnp.concatenate([mine[0], theirs[0]], 1)
     got = along_xy(first)
     moved_0 = move_z(got[:, :n], got[:, n:])
-    last = along_xy(jnp.concatenate(moved_1, 1))
+    x_own = jnp.where(zh > 1, got[0, 0, 0], moved_1[0])
+    last = along_xy(jnp.concatenate([x_own, *moved_1[1:]], 1))
     h = rest // 2
     moved_1 = last[:, :h], last[:, h:rest], last[:, rest : 2 * rest], last[:, 2 * rest :]
 

time: 205 us -> 211 us (1.029); the launches traced: 201 us -> 210 us
  starting transfers between devices: 67.4 us -> 71.8 us
  waiting for transfers between devices: 64.2 us -> 66.7 us
    all_to_all x3, waiting for transfers between devices: 0.01 us -> 23.1 us  [along_xy(): return lax.all_to_all(v, ('x', 'y'), 0, 0, tiled=True)]
    ppermute x3, waiting for transfers between devices: 28.6 us -> 13.5 us  [swap_block(): return lax.ppermute(v, 'nw', [(i, i ^ 4) for i in range(8)])]
    ppermute x3, waiting for transfers between devices: 35.5 us -> 24.1 us  [cross_same(): return lax.ppermute(v, 'zh', [(0, 1), (1, 0)])]
    ppermute x3, waiting for transfers between devices: 0.01 us -> 5.97 us  [cross_block(): return lax.ppermute(v, ('zh', 'nw'), pairs)]
    ppermute x3, starting transfers between devices: 6.8 us -> 10.5 us  [swap_block(): return lax.ppermute(v, 'nw', [(i, i ^ 4) for i in range(8)])]
    ppermute x3, starting transfers between devices: 18.3 us -> 15.8 us  [cross_block(): return lax.ppermute(v, ('zh', 'nw'), pairs)]
  transfers between devices with their start and end apart: 13 -> 13, of which waited for: 4 -> 5; matrix products, arithmetic and copies ran while one was open for 9% -> 10% of each run, Pallas kernels for 0% -> 0%
where the time goes in v6:
time: 211 us; the launch traced here: 210 us
  starting transfers between devices  71.8 us (34%)
  waiting for transfers between devices  66.7 us (32%)
  local copies, waits for them, and re-layouts  22.6 us (11%)
  blocking collectives  17.3 us (8%)
  between operations  14.6 us (7%)
  matrix products  9.64 us (5%)
  other arithmetic  6.92 us (3%)
    all_to_all x3, starting transfers between devices, along_xy(): return lax.all_to_all(v, ('x', 'y'), 0, 0, tiled=True)  24.7 us
    ppermute x3, waiting for transfers between devices, cross_same(): return lax.ppermute(v, 'zh', [(0, 1), (1, 0)])  24.1 us
    all_to_all x3, waiting for transfers between devices, along_xy(): return lax.all_to_all(v, ('x', 'y'), 0, 0, tiled=True)  23.1 us
    ppermute x3, starting transfers between devices, cross_same(): return lax.ppermute(v, 'zh', [(0, 1), (1, 0)])  20.9 us
    all_gather x1, blocking collectives, body(): lax.all_gather(jnp.concatenate([part.astype(BF), cot], 1), 'nw', axis=0,...  17.3 us
    ppermute x3, starting transfers between devices, cross_block(): return lax.ppermute(v, ('zh', 'nw'), pairs)  15.8 us
    ppermute x3, waiting for transfers between devices, swap_block(): return lax.ppermute(v, 'nw', [(i, i ^ 4) for i in range(8)])  13.5 us
    ppermute x3, starting transfers between devices, swap_block(): return lax.ppermute(v, 'nw', [(i, i ^ 4) for i in range(8)])  10.5 us
  transfers between devices with their start and end apart: 13, of which 5 were waited for; matrix products, arithmetic and copies ran while one was open for 10% of the time, Pallas kernels for 0%

profile of v6, /device:TPU:1, one launch (start us, length us, event | category | flops | bytes accessed | tf_op | source)
XLA Modules:
  0.0 209.6 jit_solution(15985951318008773249)
XLA Ops:
  7.2 0.8 copy.87
  8.0 0.7 copy.60
  8.7 10.5 %all-to-all-start.2 = ((bf16[32,2,512]{2,1,0:T(2,128)(2,1)}), bf16[32,2,512]{2,1,0:T(2,128)(2,1)S(1)}, u32[]{:S(2)}, u32[]{:S(2)}) async-start(bf16[32,2,512]{2,1,0:T(2,128)(2,1)} %copy.60), calls=%async_computation.2 | async-start | bytes 131072 | tf_op jit(solution)/shard_map/all_to_all | solution.py:32
  19.3 0.8 fusion.15
  20.1 0.8 fusion.16
  20.9 10.6 %collective-permute-start.6 = (bf16[64,512]{1,0:T(8,128)(2,1)S(1)}, bf16[64,512]{1,0:T(8,128)(2,1)S(1)}, u32[]{:S(2)}, u32[]{:S(2)}) collective-permute-start(bf16[64,512]{1,0:T(8,128)(2,1)S(1)} %bitcast.131), channel_id=1, source_target_pairs={{0,64},{64,0},{1,65},{65,1},{2,66},{66,2},{3,67},{67,3},{4,68},{68... | collective-permute-start | bytes 196616 | tf_op jit(solution)/shard_map/ppermute | solution.py:23
  31.5 7.2 %collective-permute-start.8 = (bf16[32,2,512]{2,0,1:T(8,128)(2,1)S(1)}, bf16[32,2,512]{2,0,1:T(8,128)(2,1)S(1)}, u32[]{:S(2)}, u32[]{:S(2)}) collective-permute-start(bf16[32,2,512]{2,0,1:T(8,128)(2,1)S(1)} %copy.61), channel_id=1, source_target_pairs={{0,68},{1,69},{2,70},{3,71},{4,64},{5,65},{6,66},{7,67},{64,4},{65... | collective-permute-start | bytes 196616 | tf_op jit(solution)/shard_map/ppermute | solution.py:19
  38.8 2.2 %collective-permute-start.7 = (bf16[32,2,512]{2,0,1:T(8,128)(2,1)S(1)}, bf16[32,2,512]{2,0,1:T(8,128)(2,1)S(1)}, u32[]{:S(2)}, u32[]{:S(2)}) collective-permute-start(bf16[32,2,512]{2,0,1:T(8,128)(2,1)S(1)} %copy.61), channel_id=1, source_target_pairs={{0,4},{1,5},{2,6},{3,7},{4,0},{5,1},{6,2},{7,3},{8,12},{9,13},{10,... | collective-permute-start | bytes 196616 | tf_op jit(solution)/shard_map/ppermute | solution.py:14
  41.0 3.8 %collective-permute-done.7 = bf16[32,2,512]{2,0,1:T(8,128)(2,1)S(1)} collective-permute-done((bf16[32,2,512]{2,0,1:T(8,128)(2,1)S(1)}, bf16[32,2,512]{2,0,1:T(8,128)(2,1)S(1)}, u32[]{:S(2)}, u32[]{:S(2)}) %collective-permute-start.7) | collective-permute-done | bytes 65568 | tf_op jit(solution)/shard_map/ppermute | solution.py:14
  44.8 0.7 fusion.13
  45.5 1.6 slice.70
  47.2 1.4 pad_maximum_fusion
  48.6 4.0 %all-to-all-start = ((bf16[32,192,128]{2,1,0:T(8,128)(2,1)}), bf16[32,192,128]{2,1,0:T(8,128)(2,1)S(1)}, u32[]{:S(2)}, u32[]{:S(2)}) async-start(bf16[32,192,128]{2,1,0:T(8,128)(2,1)} %pad_maximum_fusion), calls=%async_computation | async-start | bytes 3145728 | tf_op jit(solution)/shard_map/all_to_all | solution.py:32
  52.5 1.2 slice.74
  53.8 6.6 %collective-permute-start.3 = (bf16[32,48,128]{2,1,0:T(8,128)(2,1)S(1)}, bf16[32,48,128]{2,1,0:T(8,128)(2,1)S(1)}, u32[]{:S(2)}, u32[]{:S(2)}) collective-permute-start(bf16[32,48,128]{2,1,0:T(8,128)(2,1)S(1)} %bitcast.119), channel_id=1, source_target_pairs={{0,68},{1,69},{2,70},{3,71},{4,64},{5,65},{6,66},{7,67},{64,4},{65... | collective-permute-start | bytes 1179656 | tf_op jit(solution)/shard_map/ppermute | solution.py:19
  60.5 2.7 %collective-permute-start.2 = (bf16[32,48,128]{2,1,0:T(8,128)(2,1)S(1)}, bf16[32,48,128]{2,1,0:T(8,128)(2,1)S(1)}, u32[]{:S(2)}, u32[]{:S(2)}) collective-permute-start(bf16[32,48,128]{2,1,0:T(8,128)(2,1)S(1)} %bitcast.117), channel_id=1, source_target_pairs={{0,4},{1,5},{2,6},{3,7},{4,0},{5,1},{6,2},{7,3},{8,12},{9,13},{10,... | collective-permute-start | bytes 1179656 | tf_op jit(solution)/shard_map/ppermute | solution.py:14
  63.2 3.2 %collective-permute-start.1 = (bf16[32,24,128]{2,1,0:T(8,128)(2,1)S(1)}, bf16[32,24,128]{2,1,0:T(8,128)(2,1)S(1)}, u32[]{:S(2)}, u32[]{:S(2)}) collective-permute-start(bf16[32,24,128]{2,1,0:T(8,128)(2,1)S(1)} %constant_dynamic-slice_fusion), channel_id=1, source_target_pairs={{0,64},{64,0},{1,65},{65,1},{2,66},{66,2},{3,67},{67,3},{4,68},{68... | collective-permute-start | bytes 589832 | tf_op jit(solution)/shard_map/ppermute | solution.py:23
  66.4 23.1 %all-to-all-done = bf16[32,192,128]{2,1,0:T(8,128)(2,1)S(1)} async-done(((bf16[32,192,128]{2,1,0:T(8,128)(2,1)}), bf16[32,192,128]{2,1,0:T(8,128)(2,1)S(1)}, u32[]{:S(2)}, u32[]{:S(2)}) %all-to-all-start) | async-done | bytes 1572896 | tf_op jit(solution)/shard_map/all_to_all | solution.py:32
  89.5 0.5 slice.73
  90.1 0.7 dynamic-slice_select_fusion
  90.8 1.2 pad_maximum_fusion.1
  91.9 10.2 %all-to-all-start.1 = ((bf16[32,144,128]{2,1,0:T(8,128)(2,1)}), bf16[32,144,128]{2,1,0:T(8,128)(2,1)S(1)}, u32[]{:S(2)}, u32[]{:S(2)}) async-start(bf16[32,144,128]{2,1,0:T(8,128)(2,1)} %pad_maximum_fusion.1), calls=%async_computation.1 | async-start | bytes 2359296 | tf_op jit(solution)/shard_map/all_to_all | solution.py:32
  102.9 5.6 %collective-permute-start.4 = (bf16[32,96,128]{2,0,1:T(8,128)(2,1)S(1)}, bf16[32,96,128]{2,0,1:T(8,128)(2,1)S(1)}, u32[]{:S(2)}, u32[]{:S(2)}) collective-permute-start(bf16[32,96,128]{2,0,1:T(8,128)(2,1)S(1)} %copy.73), channel_id=1, source_target_pairs={{0,4},{1,5},{2,6},{3,7},{4,0},{5,1},{6,2},{7,3},{8,12},{9,13},{10,... | collective-permute-start | bytes 2359304 | tf_op jit(solution)/shard_map/ppermute | solution.py:14
  108.5 0.8 constant_dynamic-slice_fusion.3
  109.3 7.0 %collective-permute-start = (bf16[32,48,128]{2,0,1:T(8,128)(2,1)}, bf16[32,48,128]{2,0,1:T(8,128)(2,1)}, u32[]{:S(2)}, u32[]{:S(2)}) collective-permute-start(bf16[32,48,128]{2,0,1:T(8,128)(2,1)} %constant_dynamic-slice_fusion.3), channel_id=1, source_target_pairs={{0,64},{64,0},{1,65},{65,1},{2,66},{66,2},{3,67},{67,3},{4,68},{68... | collective-permute-start | bytes 1179656 | tf_op jit(solution)/shard_map/ppermute | solution.py:23
  116.3 1.9 collective-permute-start.5
  118.2 1.5 reshape.121
  119.7 1.5 copy.63
  121.2 1.5 reshape.122
  122.6 24.1 %collective-permute-done = bf16[32,48,128]{2,0,1:T(8,128)(2,1)} collective-permute-done((bf16[32,48,128]{2,0,1:T(8,128)(2,1)}, bf16[32,48,128]{2,0,1:T(8,128)(2,1)}, u32[]{:S(2)}, u32[]{:S(2)}) %collective-permute-start) | collective-permute-done | bytes 393248 | tf_op jit(solution)/shard_map/ppermute | solution.py:23
  146.8 1.1 select_bitcast_fusion.1
  148.2 1.1 copy.86
  149.3 9.7 %collective-permute-done.4 = bf16[32,96,128]{2,0,1:T(8,128)(2,1)S(1)} collective-permute-done((bf16[32,96,128]{2,0,1:T(8,128)(2,1)S(1)}, bf16[32,96,128]{2,0,1:T(8,128)(2,1)S(1)}, u32[]{:S(2)}, u32[]{:S(2)}) %collective-permute-start.4) | collective-permute-done | bytes 786464 | tf_op jit(solution)/shard_map/ppermute | solution.py:14
  159.1 6.0 %collective-permute-done.5 = bf16[32,96,128]{2,0,1:T(8,128)(2,1)} collective-permute-done((bf16[32,96,128]{2,0,1:T(8,128)(2,1)S(1)}, bf16[32,96,128]{2,0,1:T(8,128)(2,1)}, u32[]{:S(2)}, u32[]{:S(2)}) %collective-permute-start.5) | collective-permute-done | bytes 786464 | tf_op jit(solution)/shard_map/ppermute | solution.py:19
  165.1 1.2 constant_dynamic-update-slice_fusion
  166.3 1.1 copy-done
  168.1 0.7 copy-done.3
  168.8 0.7 multiply_convert_fusion.1
  169.6 0.9 reshape.116
  170.5 3.0 %convolution_convert_fusion.1 = bf16[72,512]{1,0:T(8,128)(2,1)S(1)} fusion(bf16[72,4096]{1,0:T(8,128)(2,1)S(1)} %reshape.116, bf16[4096,512]{1,0:T(8,128)(2,1)} %all-gather.3.cloned.1.call-done), kind=kOutput, calls=%fused_computation.17 | convolution fusion | flops 302026752 | bytes 4857856 | tf_op jit(solution)/shard_map/dot_general | solution.py:109
  173.6 17.3 %all-gather = bf16[576,640]{1,0:T(8,128)(2,1)S(1)} all-gather(bf16[72,640]{1,0:T(8,128)(2,1)S(1)} %pad_maximum_fusion.3), channel_id=2, replica_groups=mesh['x'=4,'zh'=2,'y'=8,'nw'=8] {'nw'}, dimensions={0}, use_global_device_ids=true | all-gather | bytes 829440 | tf_op jit(solution)/shard_map/all_gather | solution.py:112
  191.2 0.7 copy.67
  192.0 0.4 reshape.127
  192.7 3.7 %convolution_convert_fusion = bf16[144,4096]{1,0:T(8,128)(2,1)S(1)} fusion(bf16[4096,512]{1,0:T(8,128)(2,1)} %all-gather.3.cloned.1.call-done, f32[144,512]{1,0:T(8,128)S(1)} %reshape.126, f32[144,512]{1,0:T(8,128)S(1)} %maximum_add_fusion), kind=kOutput, calls=%fused_computation | convolution fusion | flops 605233152 | bytes 5963776 | tf_op jit(solution)/shard_map/dot_general | solution.py:127
  196.4 2.6 %reshape.123 = bf16[144,4,8,2,64]{4,3,2,1,0:T(2,128)(2,1)S(1)} reshape(bf16[144,4096]{1,0:T(8,128)(2,1)S(1)} %convolution_convert_fusion) | data formatting | bytes 2359296 | tf_op jit(solution)/shard_map/reshape | solution.py:130
  199.0 0.5 copy.69
  199.5 0.8 copy-done.1
  200.6 2.2 %fusion = bf16[144,1,64,128]{3,2,1,0:T(8,128)(2,1)} fusion(bf16[144,64,64]{2,1,0:T(8,128)(2,1)S(1)} %bitcast.113, bf16[48,64,128]{2,1,0:T(8,128)(2,1)S(1)} %bitcast.122, bf16[96,64,128]{2,1,0:T(8,128)(2,1)S(1)} %bitcast.115), kind=kOutput, calls=%fused_computation.2 | convolution fusion | flops 154533888 | bytes 5898240 | tf_op jit(solution)/shard_map/sij,sje->sie/dot_general | solution.py:132
  (49 shorter events, 3.0 us)
Async XLA Ops:
  8.7 22.8 %all-to-all-start.2 = ((bf16[32,2,512]{2,1,0:T(2,128)(2,1)}), bf16[32,2,512]{2,1,0:T(2,128)(2,1)S(1)}, u32[]{:S(2)}, u32[]{:S(2)}) async-start(bf16[32,2,512]{2,1,0:T(2,128)(2,1)} %copy.60), calls=%async_computation.2 | async-start | bytes 131072 | tf_op jit(solution)/shard_map/all_to_all | solution.py:32
  19.2 151.3 %all-gather.3.cloned.1.call-start = ((), (), s32[]{:S(2)}) async-start(), calls=%async_computation.3 | async-start | bytes 4325376 | tf_op jit(solution)/shard_map/all_gather | solution.py:82
  20.9 20.1 %collective-permute-start.6 = (bf16[64,512]{1,0:T(8,128)(2,1)S(1)}, bf16[64,512]{1,0:T(8,128)(2,1)S(1)}, u32[]{:S(2)}, u32[]{:S(2)}) collective-permute-start(bf16[64,512]{1,0:T(8,128)(2,1)S(1)} %bitcast.131), channel_id=1, source_target_pairs={{0,64},{64,0},{1,65},{65,1},{2,66},{66,2},{3,67},{67,3},{4,68},{68... | collective-permute-start | bytes 196616 | tf_op jit(solution)/shard_map/ppermute | solution.py:23
  31.5 9.4 %collective-permute-start.8 = (bf16[32,2,512]{2,0,1:T(8,128)(2,1)S(1)}, bf16[32,2,512]{2,0,1:T(8,128)(2,1)S(1)}, u32[]{:S(2)}, u32[]{:S(2)}) collective-permute-start(bf16[32,2,512]{2,0,1:T(8,128)(2,1)S(1)} %copy.61), channel_id=1, source_target_pairs={{0,68},{1,69},{2,70},{3,71},{4,64},{5,65},{6,66},{7,67},{64,4},{65... | collective-permute-start | bytes 196616 | tf_op jit(solution)/shard_map/ppermute | solution.py:19
  38.8 6.0 %collective-permute-start.7 = (bf16[32,2,512]{2,0,1:T(8,128)(2,1)S(1)}, bf16[32,2,512]{2,0,1:T(8,128)(2,1)S(1)}, u32[]{:S(2)}, u32[]{:S(2)}) collective-permute-start(bf16[32,2,512]{2,0,1:T(8,128)(2,1)S(1)} %copy.61), channel_id=1, source_target_pairs={{0,4},{1,5},{2,6},{3,7},{4,0},{5,1},{6,2},{7,3},{8,12},{9,13},{10,... | collective-permute-start | bytes 196616 | tf_op jit(solution)/shard_map/ppermute | solution.py:14
  48.6 41.0 %all-to-all-start = ((bf16[32,192,128]{2,1,0:T(8,128)(2,1)}), bf16[32,192,128]{2,1,0:T(8,128)(2,1)S(1)}, u32[]{:S(2)}, u32[]{:S(2)}) async-start(bf16[32,192,128]{2,1,0:T(8,128)(2,1)} %pad_maximum_fusion), calls=%async_computation | async-start | bytes 3145728 | tf_op jit(solution)/shard_map/all_to_all | solution.py:32
  53.8 36.9 %collective-permute-start.3 = (bf16[32,48,128]{2,1,0:T(8,128)(2,1)S(1)}, bf16[32,48,128]{2,1,0:T(8,128)(2,1)S(1)}, u32[]{:S(2)}, u32[]{:S(2)}) collective-permute-start(bf16[32,48,128]{2,1,0:T(8,128)(2,1)S(1)} %bitcast.119), channel_id=1, source_target_pairs={{0,68},{1,69},{2,70},{3,71},{4,64},{5,65},{6,66},{7,67},{64,4},{65... | collective-permute-start | bytes 1179656 | tf_op jit(solution)/shard_map/ppermute | solution.py:19
  60.5 30.3 %collective-permute-start.2 = (bf16[32,48,128]{2,1,0:T(8,128)(2,1)S(1)}, bf16[32,48,128]{2,1,0:T(8,128)(2,1)S(1)}, u32[]{:S(2)}, u32[]{:S(2)}) collective-permute-start(bf16[32,48,128]{2,1,0:T(8,128)(2,1)S(1)} %bitcast.117), channel_id=1, source_target_pairs={{0,4},{1,5},{2,6},{3,7},{4,0},{5,1},{6,2},{7,3},{8,12},{9,13},{10,... | collective-permute-start | bytes 1179656 | tf_op jit(solution)/shard_map/ppermute | solution.py:14
  63.2 27.5 %collective-permute-start.1 = (bf16[32,24,128]{2,1,0:T(8,128)(2,1)S(1)}, bf16[32,24,128]{2,1,0:T(8,128)(2,1)S(1)}, u32[]{:S(2)}, u32[]{:S(2)}) collective-permute-start(bf16[32,24,128]{2,1,0:T(8,128)(2,1)S(1)} %constant_dynamic-slice_fusion), channel_id=1, source_target_pairs={{0,64},{64,0},{1,65},{65,1},{2,66},{66,2},{3,67},{67,3},{4,68},{68... | collective-permute-start | bytes 589832 | tf_op jit(solution)/shard_map/ppermute | solution.py:23
  91.9 75.6 %all-to-all-start.1 = ((bf16[32,144,128]{2,1,0:T(8,128)(2,1)}), bf16[32,144,128]{2,1,0:T(8,128)(2,1)S(1)}, u32[]{:S(2)}, u32[]{:S(2)}) async-start(bf16[32,144,128]{2,1,0:T(8,128)(2,1)} %pad_maximum_fusion.1), calls=%async_computation.1 | async-start | bytes 2359296 | tf_op jit(solution)/shard_map/all_to_all | solution.py:32
  102.9 56.1 %collective-permute-start.4 = (bf16[32,96,128]{2,0,1:T(8,128)(2,1)S(1)}, bf16[32,96,128]{2,0,1:T(8,128)(2,1)S(1)}, u32[]{:S(2)}, u32[]{:S(2)}) collective-permute-start(bf16[32,96,128]{2,0,1:T(8,128)(2,1)S(1)} %copy.73), channel_id=1, source_target_pairs={{0,4},{1,5},{2,6},{3,7},{4,0},{5,1},{6,2},{7,3},{8,12},{9,13},{10,... | collective-permute-start | bytes 2359304 | tf_op jit(solution)/shard_map/ppermute | solution.py:14
  109.3 37.5 %collective-permute-start = (bf16[32,48,128]{2,0,1:T(8,128)(2,1)}, bf16[32,48,128]{2,0,1:T(8,128)(2,1)}, u32[]{:S(2)}, u32[]{:S(2)}) collective-permute-start(bf16[32,48,128]{2,0,1:T(8,128)(2,1)} %constant_dynamic-slice_fusion.3), channel_id=1, source_target_pairs={{0,64},{64,0},{1,65},{65,1},{2,66},{66,2},{3,67},{67,3},{4,68},{68... | collective-permute-start | bytes 1179656 | tf_op jit(solution)/shard_map/ppermute | solution.py:23
  116.3 48.8 %collective-permute-start.5 = (bf16[32,96,128]{2,0,1:T(8,128)(2,1)S(1)}, bf16[32,96,128]{2,0,1:T(8,128)(2,1)}, u32[]{:S(2)}, u32[]{:S(2)}) collective-permute-start(bf16[32,96,128]{2,0,1:T(8,128)(2,1)S(1)} %copy.74), channel_id=1, source_target_pairs={{0,68},{1,69},{2,70},{3,71},{4,64},{5,65},{6,66},{7,67},{64,4},{65... | collective-permute-start | bytes 2359304 | tf_op jit(solution)/shard_map/ppermute | solution.py:19
  166.3 1.1 copy-start
  167.7 1.2 copy-start.2
  167.9 0.9 copy-start.3
  170.5 3.1 %copy-start.5 = (bf16[72,128]{1,0:T(8,128)(2,1)S(1)}, bf16[72,128]{1,0:T(8,128)(2,1)}, u32[]{:S(2)}) copy-start(bf16[72,128]{1,0:T(8,128)(2,1)} %reshape.122) | copy-start | bytes 55300
  173.6 17.5 %copy-start.6 = (f32[512]{0:T(512)S(1)}, f32[512]{0:T(512)}, u32[]{:S(2)}) copy-start(f32[512]{0:T(512)} %param.6) | copy-start | bytes 6148
  199.0 1.4 copy-start.1
  199.0 1.6 copy-start.4
Sparse Core Ops, SparseCore 0:
  45.6 107.5 all-gather.2

commit v7 on v6

--- a/solution.py
+++ b/solution.py
@@ -5,7 +5,7 @@
 
 X, ZH, Y = 4, 2, 8
 XY = X * Y
-FIRST = 96
+FIRST = 88
 BF = jnp.bfloat16
 F32 = jnp.float32
 

time: 211 us -> 205 us (0.972)
  starting transfers between devices: 71.8 us -> 67.4 us
    ppermute x3, waiting for transfers between devices: 13.5 us -> 36.4 us  [swap_block(): return lax.ppermute(v, 'nw', [(i, i ^ 4) for i in range(8)])]
    ppermute x3, waiting for transfers between devices: 24.1 us -> 9.98 us  [cross_same(): return lax.ppermute(v, 'zh', [(0, 1), (1, 0)])]
    ppermute x3, waiting for transfers between devices: 5.97 us -> 0.01 us  [cross_block(): return lax.ppermute(v, ('zh', 'nw'), pairs)]
    all_to_all x3, waiting for transfers between devices: 23.1 us -> 19.4 us  [along_xy(): return lax.all_to_all(v, ('x', 'y'), 0, 0, tiled=True)]
    ppermute x3, starting transfers between devices: 10.5 us -> 8.31 us  [swap_block(): return lax.ppermute(v, 'nw', [(i, i ^ 4) for i in range(8)])]
where the time goes in v7:
time: 205 us; the launch traced here: 203 us
  starting transfers between devices  67.4 us (33%)
  waiting for transfers between devices  65.7 us (32%)
  local copies, waits for them, and re-layouts  23.4 us (11%)
  blocking collectives  15.7 us (8%)
  between operations  14.6 us (7%)
  matrix products  9.65 us (5%)
  other arithmetic  7.03 us (3%)
    ppermute x3, waiting for transfers between devices, swap_block(): return lax.ppermute(v, 'nw', [(i, i ^ 4) for i in range(8)])  36.4 us
    all_to_all x3, starting transfers between devices, along_xy(): return lax.all_to_all(v, ('x', 'y'), 0, 0, tiled=True)  23.4 us
    all_to_all x3, waiting for transfers between devices, along_xy(): return lax.all_to_all(v, ('x', 'y'), 0, 0, tiled=True)  19.4 us
    ppermute x3, starting transfers between devices, cross_same(): return lax.ppermute(v, 'zh', [(0, 1), (1, 0)])  18.9 us
    ppermute x3, starting transfers between devices, cross_block(): return lax.ppermute(v, ('zh', 'nw'), pairs)  16.8 us
    all_gather x1, blocking collectives, body(): lax.all_gather(jnp.concatenate([part.astype(BF), cot], 1), 'nw', axis=0,...  15.7 us
    ppermute x3, waiting for transfers between devices, cross_same(): return lax.ppermute(v, 'zh', [(0, 1), (1, 0)])  9.98 us
    ppermute x3, starting transfers between devices, swap_block(): return lax.ppermute(v, 'nw', [(i, i ^ 4) for i in range(8)])  8.31 us
  transfers between devices with their start and end apart: 13, of which 5 were waited for; matrix products, arithmetic and copies ran while one was open for 10% of the time, Pallas kernels for 0%

profile of v7, /device:TPU:1, one launch (start us, length us, event | category | flops | bytes accessed | tf_op | source)
XLA Modules:
  0.0 203.4 jit_solution(2893651834376526749)
XLA Ops:
  7.2 0.8 copy.78
  8.0 0.7 copy.54
  8.7 10.5 %all-to-all-start.2 = ((bf16[32,2,512]{2,1,0:T(2,128)(2,1)}), bf16[32,2,512]{2,1,0:T(2,128)(2,1)S(1)}, u32[]{:S(2)}, u32[]{:S(2)}) async-start(bf16[32,2,512]{2,1,0:T(2,128)(2,1)} %copy.54), calls=%async_computation.2 | async-start | bytes 131072 | tf_op jit(solution)/shard_map/all_to_all | solution.py:32
  19.3 0.8 fusion.15
  20.1 0.8 fusion.16
  20.9 10.6 %collective-permute-start.6 = (bf16[64,512]{1,0:T(8,128)(2,1)S(1)}, bf16[64,512]{1,0:T(8,128)(2,1)S(1)}, u32[]{:S(2)}, u32[]{:S(2)}) collective-permute-start(bf16[64,512]{1,0:T(8,128)(2,1)S(1)} %bitcast.127), channel_id=1, source_target_pairs={{0,64},{64,0},{1,65},{65,1},{2,66},{66,2},{3,67},{67,3},{4,68},{68... | collective-permute-start | bytes 196616 | tf_op jit(solution)/shard_map/ppermute | solution.py:23
  31.5 7.2 %collective-permute-start.8 = (bf16[32,2,512]{2,0,1:T(8,128)(2,1)S(1)}, bf16[32,2,512]{2,0,1:T(8,128)(2,1)S(1)}, u32[]{:S(2)}, u32[]{:S(2)}) collective-permute-start(bf16[32,2,512]{2,0,1:T(8,128)(2,1)S(1)} %copy.55), channel_id=1, source_target_pairs={{0,68},{1,69},{2,70},{3,71},{4,64},{5,65},{6,66},{7,67},{64,4},{65... | collective-permute-start | bytes 196616 | tf_op jit(solution)/shard_map/ppermute | solution.py:19
  38.8 2.2 %collective-permute-start.7 = (bf16[32,2,512]{2,0,1:T(8,128)(2,1)S(1)}, bf16[32,2,512]{2,0,1:T(8,128)(2,1)S(1)}, u32[]{:S(2)}, u32[]{:S(2)}) collective-permute-start(bf16[32,2,512]{2,0,1:T(8,128)(2,1)S(1)} %copy.55), channel_id=1, source_target_pairs={{0,4},{1,5},{2,6},{3,7},{4,0},{5,1},{6,2},{7,3},{8,12},{9,13},{10,... | collective-permute-start | bytes 196616 | tf_op jit(solution)/shard_map/ppermute | solution.py:14
  41.0 3.8 %collective-permute-done.7 = bf16[32,2,512]{2,0,1:T(8,128)(2,1)S(1)} collective-permute-done((bf16[32,2,512]{2,0,1:T(8,128)(2,1)S(1)}, bf16[32,2,512]{2,0,1:T(8,128)(2,1)S(1)}, u32[]{:S(2)}, u32[]{:S(2)}) %collective-permute-start.7) | collective-permute-done | bytes 65568 | tf_op jit(solution)/shard_map/ppermute | solution.py:14
  44.8 0.7 fusion.13
  45.5 1.5 slice.70
  47.1 1.2 pad_maximum_fusion
  48.3 4.0 %all-to-all-start = ((bf16[32,176,128]{2,1,0:T(8,128)(2,1)}), bf16[32,176,128]{2,1,0:T(8,128)(2,1)S(1)}, u32[]{:S(2)}, u32[]{:S(2)}) async-start(bf16[32,176,128]{2,1,0:T(8,128)(2,1)} %pad_maximum_fusion), calls=%async_computation | async-start | bytes 2883584 | tf_op jit(solution)/shard_map/all_to_all | solution.py:32
  52.3 1.3 slice.74
  53.7 6.6 %collective-permute-start.3 = (bf16[32,56,128]{2,1,0:T(8,128)(2,1)S(1)}, bf16[32,56,128]{2,1,0:T(8,128)(2,1)S(1)}, u32[]{:S(2)}, u32[]{:S(2)}) collective-permute-start(bf16[32,56,128]{2,1,0:T(8,128)(2,1)S(1)} %bitcast.114), channel_id=1, source_target_pairs={{0,68},{1,69},{2,70},{3,71},{4,64},{5,65},{6,66},{7,67},{64,4},{65... | collective-permute-start | bytes 1376264 | tf_op jit(solution)/shard_map/ppermute | solution.py:19
  60.3 2.7 %collective-permute-start.2 = (bf16[32,56,128]{2,1,0:T(8,128)(2,1)S(1)}, bf16[32,56,128]{2,1,0:T(8,128)(2,1)S(1)}, u32[]{:S(2)}, u32[]{:S(2)}) collective-permute-start(bf16[32,56,128]{2,1,0:T(8,128)(2,1)S(1)} %bitcast.112), channel_id=1, source_target_pairs={{0,4},{1,5},{2,6},{3,7},{4,0},{5,1},{6,2},{7,3},{8,12},{9,13},{10,... | collective-permute-start | bytes 1376264 | tf_op jit(solution)/shard_map/ppermute | solution.py:14
  63.2 3.2 %collective-permute-start.1 = (bf16[32,28,128]{2,1,0:T(8,128)(2,1)S(1)}, bf16[32,28,128]{2,1,0:T(8,128)(2,1)}, u32[]{:S(2)}, u32[]{:S(2)}) collective-permute-start(bf16[32,28,128]{2,1,0:T(8,128)(2,1)S(1)} %constant_dynamic-slice_fusion), channel_id=1, source_target_pairs={{0,64},{64,0},{1,65},{65,1},{2,66},{66,2},{3,67},{67,3},{4,68},{68... | collective-permute-start | bytes 688136 | tf_op jit(solution)/shard_map/ppermute | solution.py:23
  66.4 19.3 %all-to-all-done = bf16[32,176,128]{2,1,0:T(8,128)(2,1)S(1)} async-done(((bf16[32,176,128]{2,1,0:T(8,128)(2,1)}), bf16[32,176,128]{2,1,0:T(8,128)(2,1)S(1)}, u32[]{:S(2)}, u32[]{:S(2)}) %all-to-all-start) | async-done | bytes 1441824 | tf_op jit(solution)/shard_map/all_to_all | solution.py:32
  85.7 0.5 slice.73
  86.2 0.8 dynamic-slice_select_fusion
  87.0 6.2 %collective-permute-done.1 = bf16[32,28,128]{2,1,0:T(8,128)(2,1)} collective-permute-done((bf16[32,28,128]{2,1,0:T(8,128)(2,1)S(1)}, bf16[32,28,128]{2,1,0:T(8,128)(2,1)}, u32[]{:S(2)}, u32[]{:S(2)}) %collective-permute-start.1) | collective-permute-done | bytes 229408 | tf_op jit(solution)/shard_map/ppermute | solution.py:23
  93.2 2.3 %pad_maximum_fusion.1 = bf16[32,168,128]{2,1,0:T(8,128)(2,1)} fusion(bf16[32,56,128]{2,1,0:T(8,128)(2,1)S(1)} %collective-permute-done.3, bf16[32,56,128]{2,1,0:T(8,128)(2,1)S(1)} %collective-permute-done.2, bf16[32,28,128]{2,1,0:T(8,128)(2,1)} %collective-permute-done.1, bf16[32,28,128]{2,1,0:T(8,128)(2,1)S(1)} %dynamic-slice_select_fusion), kind=kLoop, calls=%fused_computation.9 | loop fusion | flops 5505024 | bytes 2752512 | tf_op jit(solution)/shard_map/concatenate | solution.py:88
  95.5 8.9 %all-to-all-start.1 = ((bf16[32,168,128]{2,1,0:T(8,128)(2,1)}), bf16[32,168,128]{2,1,0:T(8,128)(2,1)S(1)}, u32[]{:S(2)}, u32[]{:S(2)}) async-start(bf16[32,168,128]{2,1,0:T(8,128)(2,1)} %pad_maximum_fusion.1), calls=%async_computation.1 | async-start | bytes 2752512 | tf_op jit(solution)/shard_map/all_to_all | solution.py:32
  104.7 5.0 %collective-permute-start = (bf16[32,44,128]{2,0,1:T(8,128)(2,1)S(1)}, bf16[32,44,128]{2,0,1:T(8,128)(2,1)S(1)}, u32[]{:S(2)}, u32[]{:S(2)}) collective-permute-start(bf16[32,44,128]{2,0,1:T(8,128)(2,1)S(1)} %constant_dynamic-slice_fusion.3), channel_id=1, source_target_pairs={{0,64},{64,0},{1,65},{65,1},{2,66},{66,2},{3,67},{67,3},{4,68},{68... | collective-permute-start | bytes 1081352 | tf_op jit(solution)/shard_map/ppermute | solution.py:23
  109.9 3.4 %collective-permute-start.4 = (bf16[32,88,128]{2,0,1:T(8,128)(2,1)S(1)}, bf16[32,88,128]{2,0,1:T(8,128)(2,1)}, u32[]{:S(2)}, u32[]{:S(2)}) collective-permute-start(bf16[32,88,128]{2,0,1:T(8,128)(2,1)S(1)} %copy.67), channel_id=1, source_target_pairs={{0,4},{1,5},{2,6},{3,7},{4,0},{5,1},{6,2},{7,3},{8,12},{9,13},{10,... | collective-permute-start | bytes 2162696 | tf_op jit(solution)/shard_map/ppermute | solution.py:14
  113.3 2.9 %collective-permute-start.5 = (bf16[32,88,128]{2,0,1:T(8,128)(2,1)S(1)}, bf16[32,88,128]{2,0,1:T(8,128)(2,1)}, u32[]{:S(2)}, u32[]{:S(2)}) collective-permute-start(bf16[32,88,128]{2,0,1:T(8,128)(2,1)S(1)} %copy.68), channel_id=1, source_target_pairs={{0,68},{1,69},{2,70},{3,71},{4,64},{5,65},{6,66},{7,67},{64,4},{65... | collective-permute-start | bytes 2162696 | tf_op jit(solution)/shard_map/ppermute | solution.py:19
  116.3 1.5 reshape.121
  117.7 1.5 copy.57
  119.2 1.5 reshape.122
  120.7 3.7 %collective-permute-done = bf16[32,44,128]{2,0,1:T(8,128)(2,1)S(1)} collective-permute-done((bf16[32,44,128]{2,0,1:T(8,128)(2,1)S(1)}, bf16[32,44,128]{2,0,1:T(8,128)(2,1)S(1)}, u32[]{:S(2)}, u32[]{:S(2)}) %collective-permute-start) | collective-permute-done | bytes 360480 | tf_op jit(solution)/shard_map/ppermute | solution.py:23
  124.5 0.7 copy.44
  125.3 32.6 %collective-permute-done.4 = bf16[32,88,128]{2,0,1:T(8,128)(2,1)} collective-permute-done((bf16[32,88,128]{2,0,1:T(8,128)(2,1)S(1)}, bf16[32,88,128]{2,0,1:T(8,128)(2,1)}, u32[]{:S(2)}, u32[]{:S(2)}) %collective-permute-start.4) | collective-permute-done | bytes 720928 | tf_op jit(solution)/shard_map/ppermute | solution.py:14
  157.9 1.2 constant_dynamic-update-slice_fusion.1
  159.1 1.2 constant_dynamic-update-slice_fusion
  160.3 1.1 copy-done
  161.4 0.9 dynamic-slice_bitcast_fusion
  162.5 0.5 copy.46
  163.4 0.9 copy-done.2
  164.3 0.7 multiply_convert_fusion.1
  165.0 0.9 reshape.116
  166.0 3.0 %convolution_convert_fusion.1 = bf16[72,512]{1,0:T(8,128)(2,1)S(1)} fusion(bf16[72,4096]{1,0:T(8,128)(2,1)S(1)} %reshape.116, bf16[4096,512]{1,0:T(8,128)(2,1)} %all-gather.3.cloned.1.call-done), kind=kOutput, calls=%fused_computation.17 | convolution fusion | flops 302026752 | bytes 4857856 | tf_op jit(solution)/shard_map/dot_general | solution.py:109
  169.1 15.7 %all-gather = bf16[576,640]{1,0:T(8,128)(2,1)S(1)} all-gather(bf16[72,640]{1,0:T(8,128)(2,1)S(1)} %pad_maximum_fusion.2), channel_id=2, replica_groups=mesh['x'=4,'zh'=2,'y'=8,'nw'=8] {'nw'}, dimensions={0}, use_global_device_ids=true | all-gather | bytes 829440 | tf_op jit(solution)/shard_map/all_gather | solution.py:112
  185.1 0.7 copy.61
  186.5 3.7 %convolution_convert_fusion = bf16[144,4096]{1,0:T(8,128)(2,1)S(1)} fusion(bf16[4096,512]{1,0:T(8,128)(2,1)} %all-gather.3.cloned.1.call-done, f32[144,512]{1,0:T(8,128)S(1)} %reshape.126, f32[144,512]{1,0:T(8,128)S(1)} %maximum_add_fusion), kind=kOutput, calls=%fused_computation | convolution fusion | flops 605233152 | bytes 5963776 | tf_op jit(solution)/shard_map/dot_general | solution.py:127
  190.2 2.6 %reshape.123 = bf16[144,4,8,2,64]{4,3,2,1,0:T(2,128)(2,1)S(1)} reshape(bf16[144,4096]{1,0:T(8,128)(2,1)S(1)} %convolution_convert_fusion) | data formatting | bytes 2359296 | tf_op jit(solution)/shard_map/reshape | solution.py:130
  192.8 0.5 copy.63
  193.4 0.8 copy-done.1
  194.4 2.2 %fusion = bf16[144,1,64,128]{3,2,1,0:T(8,128)(2,1)} fusion(bf16[144,64,64]{2,1,0:T(8,128)(2,1)S(1)} %bitcast.109, bf16[56,64,128]{2,1,0:T(8,128)(2,1)S(1)} %bitcast.116, bf16[88,64,128]{2,1,0:T(8,128)(2,1)S(1)} %bitcast.111), kind=kOutput, calls=%fused_computation.2 | convolution fusion | flops 154533888 | bytes 5898240 | tf_op jit(solution)/shard_map/sij,sje->sie/dot_general | solution.py:132
  (49 shorter events, 2.7 us)
Async XLA Ops:
  8.7 22.8 %all-to-all-start.2 = ((bf16[32,2,512]{2,1,0:T(2,128)(2,1)}), bf16[32,2,512]{2,1,0:T(2,128)(2,1)S(1)}, u32[]{:S(2)}, u32[]{:S(2)}) async-start(bf16[32,2,512]{2,1,0:T(2,128)(2,1)} %copy.54), calls=%async_computation.2 | async-start | bytes 131072 | tf_op jit(solution)/shard_map/all_to_all | solution.py:32
  19.2 146.8 %all-gather.3.cloned.1.call-start = ((), (), s32[]{:S(2)}) async-start(), calls=%async_computation.3 | async-start | bytes 4325376 | tf_op jit(solution)/shard_map/all_gather | solution.py:82
  20.9 20.1 %collective-permute-start.6 = (bf16[64,512]{1,0:T(8,128)(2,1)S(1)}, bf16[64,512]{1,0:T(8,128)(2,1)S(1)}, u32[]{:S(2)}, u32[]{:S(2)}) collective-permute-start(bf16[64,512]{1,0:T(8,128)(2,1)S(1)} %bitcast.127), channel_id=1, source_target_pairs={{0,64},{64,0},{1,65},{65,1},{2,66},{66,2},{3,67},{67,3},{4,68},{68... | collective-permute-start | bytes 196616 | tf_op jit(solution)/shard_map/ppermute | solution.py:23
  31.5 9.4 %collective-permute-start.8 = (bf16[32,2,512]{2,0,1:T(8,128)(2,1)S(1)}, bf16[32,2,512]{2,0,1:T(8,128)(2,1)S(1)}, u32[]{:S(2)}, u32[]{:S(2)}) collective-permute-start(bf16[32,2,512]{2,0,1:T(8,128)(2,1)S(1)} %copy.55), channel_id=1, source_target_pairs={{0,68},{1,69},{2,70},{3,71},{4,64},{5,65},{6,66},{7,67},{64,4},{65... | collective-permute-start | bytes 196616 | tf_op jit(solution)/shard_map/ppermute | solution.py:19
  38.8 6.0 %collective-permute-start.7 = (bf16[32,2,512]{2,0,1:T(8,128)(2,1)S(1)}, bf16[32,2,512]{2,0,1:T(8,128)(2,1)S(1)}, u32[]{:S(2)}, u32[]{:S(2)}) collective-permute-start(bf16[32,2,512]{2,0,1:T(8,128)(2,1)S(1)} %copy.55), channel_id=1, source_target_pairs={{0,4},{1,5},{2,6},{3,7},{4,0},{5,1},{6,2},{7,3},{8,12},{9,13},{10,... | collective-permute-start | bytes 196616 | tf_op jit(solution)/shard_map/ppermute | solution.py:14
  48.3 37.4 %all-to-all-start = ((bf16[32,176,128]{2,1,0:T(8,128)(2,1)}), bf16[32,176,128]{2,1,0:T(8,128)(2,1)S(1)}, u32[]{:S(2)}, u32[]{:S(2)}) async-start(bf16[32,176,128]{2,1,0:T(8,128)(2,1)} %pad_maximum_fusion), calls=%async_computation | async-start | bytes 2883584 | tf_op jit(solution)/shard_map/all_to_all | solution.py:32
  53.7 39.6 %collective-permute-start.3 = (bf16[32,56,128]{2,1,0:T(8,128)(2,1)S(1)}, bf16[32,56,128]{2,1,0:T(8,128)(2,1)S(1)}, u32[]{:S(2)}, u32[]{:S(2)}) collective-permute-start(bf16[32,56,128]{2,1,0:T(8,128)(2,1)S(1)} %bitcast.114), channel_id=1, source_target_pairs={{0,68},{1,69},{2,70},{3,71},{4,64},{5,65},{6,66},{7,67},{64,4},{65... | collective-permute-start | bytes 1376264 | tf_op jit(solution)/shard_map/ppermute | solution.py:19
  60.3 32.9 %collective-permute-start.2 = (bf16[32,56,128]{2,1,0:T(8,128)(2,1)S(1)}, bf16[32,56,128]{2,1,0:T(8,128)(2,1)S(1)}, u32[]{:S(2)}, u32[]{:S(2)}) collective-permute-start(bf16[32,56,128]{2,1,0:T(8,128)(2,1)S(1)} %bitcast.112), channel_id=1, source_target_pairs={{0,4},{1,5},{2,6},{3,7},{4,0},{5,1},{6,2},{7,3},{8,12},{9,13},{10,... | collective-permute-start | bytes 1376264 | tf_op jit(solution)/shard_map/ppermute | solution.py:14
  63.2 30.1 %collective-permute-start.1 = (bf16[32,28,128]{2,1,0:T(8,128)(2,1)S(1)}, bf16[32,28,128]{2,1,0:T(8,128)(2,1)}, u32[]{:S(2)}, u32[]{:S(2)}) collective-permute-start(bf16[32,28,128]{2,1,0:T(8,128)(2,1)S(1)} %constant_dynamic-slice_fusion), channel_id=1, source_target_pairs={{0,64},{64,0},{1,65},{65,1},{2,66},{66,2},{3,67},{67,3},{4,68},{68... | collective-permute-start | bytes 688136 | tf_op jit(solution)/shard_map/ppermute | solution.py:23
  95.5 66.8 %all-to-all-start.1 = ((bf16[32,168,128]{2,1,0:T(8,128)(2,1)}), bf16[32,168,128]{2,1,0:T(8,128)(2,1)S(1)}, u32[]{:S(2)}, u32[]{:S(2)}) async-start(bf16[32,168,128]{2,1,0:T(8,128)(2,1)} %pad_maximum_fusion.1), calls=%async_computation.1 | async-start | bytes 2752512 | tf_op jit(solution)/shard_map/all_to_all | solution.py:32
  104.7 19.7 %collective-permute-start = (bf16[32,44,128]{2,0,1:T(8,128)(2,1)S(1)}, bf16[32,44,128]{2,0,1:T(8,128)(2,1)S(1)}, u32[]{:S(2)}, u32[]{:S(2)}) collective-permute-start(bf16[32,44,128]{2,0,1:T(8,128)(2,1)S(1)} %constant_dynamic-slice_fusion.3), channel_id=1, source_target_pairs={{0,64},{64,0},{1,65},{65,1},{2,66},{66,2},{3,67},{67,3},{4,68},{68... | collective-permute-start | bytes 1081352 | tf_op jit(solution)/shard_map/ppermute | solution.py:23
  109.9 48.0 %collective-permute-start.4 = (bf16[32,88,128]{2,0,1:T(8,128)(2,1)S(1)}, bf16[32,88,128]{2,0,1:T(8,128)(2,1)}, u32[]{:S(2)}, u32[]{:S(2)}) collective-permute-start(bf16[32,88,128]{2,0,1:T(8,128)(2,1)S(1)} %copy.67), channel_id=1, source_target_pairs={{0,4},{1,5},{2,6},{3,7},{4,0},{5,1},{6,2},{7,3},{8,12},{9,13},{10,... | collective-permute-start | bytes 2162696 | tf_op jit(solution)/shard_map/ppermute | solution.py:14
  113.3 45.8 %collective-permute-start.5 = (bf16[32,88,128]{2,0,1:T(8,128)(2,1)S(1)}, bf16[32,88,128]{2,0,1:T(8,128)(2,1)}, u32[]{:S(2)}, u32[]{:S(2)}) collective-permute-start(bf16[32,88,128]{2,0,1:T(8,128)(2,1)S(1)} %copy.68), channel_id=1, source_target_pairs={{0,68},{1,69},{2,70},{3,71},{4,64},{5,65},{6,66},{7,67},{64,4},{65... | collective-permute-start | bytes 2162696 | tf_op jit(solution)/shard_map/ppermute | solution.py:19
  160.3 1.1 copy-start
  163.1 1.2 copy-start.4
  163.3 1.0 copy-start.2
  165.9 3.1 %copy-start.5 = (bf16[72,128]{1,0:T(8,128)(2,1)S(1)}, bf16[72,128]{1,0:T(8,128)(2,1)}, u32[]{:S(2)}) copy-start(bf16[72,128]{1,0:T(8,128)(2,1)} %reshape.122) | copy-start | bytes 55300
  169.1 15.9 %copy-start.6 = (f32[512]{0:T(512)S(1)}, f32[512]{0:T(512)}, u32[]{:S(2)}) copy-start(f32[512]{0:T(512)} %param.6) | copy-start | bytes 6148
  192.8 1.4 copy-start.1
  192.8 1.6 copy-start.3
Sparse Core Ops, SparseCore 0:
  45.6 111.4 all-gather.2
